TPU v7x, 256 devices: a whole 4x4x8 slice. The times are simulated.
256 devices in a mesh: dom: 8 (over y_lo, x), neu: 32 (over y_hi, z, core).
Axes of the slice: x: 4, y: 4 (y_hi: 2, y_lo: 2; y = y_hi * 2 + y_lo), z: 8, core: 2. Of those that a mesh axis runs over, the one named last changes fastest.
Arguments:
- spec_label: int32 [1728], P('dom'), may hold values from 0 to 9
- spec_offset: int32 [1728], P('dom'), may hold values from 1 to 9
- class_rows: bfloat16 [10, 8192], P(None, 'neu'), may hold values from -0.0625 to 0.0625
- deep_weight: bfloat16 [8192, 8192], P(None, 'neu'), may hold values from -0.0625 to 0.0625
- deep_bias: float32 [8192], P('neu'), may hold values from -3 to 3
- deep_status: int32 [216, 8192], P('dom', 'neu'), may hold values from 0 to 2
- deep_bounds: int32 [2, 216, 8192], P(None, 'dom', 'neu'), may hold values from 1 to 16
- deep_slopes: float32 [8192], P('neu'), may hold values from 0 to 1
- first_weight: bfloat16 [8192, 3072], P(None, 'neu'), may hold values from -0.109375 to 0.109375
- first_bias: float32 [8192], P('neu'), may hold values from -3 to 3
- first_status: int32 [216, 8192], P('dom', 'neu'), may hold values from 0 to 2
- first_bounds: int32 [2, 216, 8192], P(None, 'dom', 'neu'), may hold values from 1 to 16
- first_slopes: float32 [8192], P('neu'), may hold values from 0 to 1
- box_center: float32 [3072], P('neu'), may hold values from -5 to 5
- box_radius: float32 [3072], P('neu'), may hold values from 0.02 to 0.2
Outputs:
- bound_rows: float32 [1728], P('dom')
- first_next: float32 [8192], P('neu')
- deep_next: float32 [8192], P('neu')
Inputs may be any that keep to these rules, and one draw needn't show every extreme that they name: `deep_status`: 0 marks a neuron split inactive in that domain, 1 split active, 2 unsplit. `first_status`: 0 marks a neuron split inactive in that domain, 1 split active, 2 unsplit.
All inputs are finite; a program needn't handle non-finite values.
Results may differ from a plain program's by a relative error of at most 0.0017.
Values may be sent and summed in bfloat16 or wider, within the bound.
No kernel may reach another device: no remote copies, remote signals or barrier semaphores. Data moves between devices by JAX's collectives and lax.ppermute only.
A program may use at most 64 MiB of HBM per device.

v0:
```python
import jax
import jax.numpy as jnp
from jax import lax
from jax.sharding import PartitionSpec as P

HIDDEN_SIZE = 8192


grid_step = 0.0625
step_rate = 0.25
epsilon = 1e-06


def relax_layer(coeffs, status, bounds, slopes):
    domain_count = status.shape[0]
    row_count = coeffs.shape[0]
    column_count = coeffs.shape[1]
    shaped = coeffs.reshape(domain_count, row_count // domain_count, column_count)
    lower_edge = -grid_step * bounds[0].astype(jnp.float32)
    upper_edge = grid_step * bounds[1].astype(jnp.float32)
    slope_ratio = upper_edge / (upper_edge - lower_edge)
    intercept = -slope_ratio * lower_edge
    kind_codes = status[:, None, :]
    positive = shaped >= 0.0
    unstable = kind_codes == 2
    relaxed = jnp.where(positive, slopes[None, None, :], slope_ratio[:, None, :])
    factor = jnp.where(unstable, relaxed, jnp.where(kind_codes == 1, 1.0, 0.0))
    offset = jnp.where(unstable & jnp.logical_not(positive), intercept[:, None, :], 0.0)
    chosen = jnp.where(unstable & positive, 1.0, 0.0)
    shape_back = (row_count, column_count)
    return (factor.reshape(shape_back), offset.reshape(shape_back), chosen.reshape(shape_back))


def advance(slopes, gradient, squares):
    root_mean = jnp.sqrt(squares / HIDDEN_SIZE + epsilon)
    return jnp.clip(slopes + step_rate * gradient / root_mean, 0.0, 1.0)


def contract_last(left, right):
    return lax.dot_general(
        left, right, (((1,), (1,)), ((), ())), preferred_element_type=jnp.float32
    )


def on_device(
    spec_label,
    spec_offset,
    class_rows,
    deep_weight,
    deep_bias,
    deep_status,
    deep_bounds,
    deep_slopes,
    first_weight,
    first_bias,
    first_status,
    first_bounds,
    first_slopes,
    box_center,
    box_radius,
):
    class_count = class_rows.shape[0]
    classes_iota = jnp.arange(class_count, dtype=jnp.int32)
    second_label = (spec_label + spec_offset) % class_count
    select = (spec_label[:, None] == classes_iota[None, :]).astype(jnp.float32) - (
        second_label[:, None] == classes_iota[None, :]
    ).astype(jnp.float32)
    deep_coeffs = jnp.dot(
        select.astype(jnp.bfloat16), class_rows, preferred_element_type=jnp.float32
    )
    deep_factor, deep_offset, deep_chosen = relax_layer(
        deep_coeffs, deep_status, deep_bounds, deep_slopes
    )
    deep_sent = (deep_coeffs * deep_factor).astype(jnp.bfloat16)
    deep_const = jnp.sum(
        deep_sent.astype(jnp.float32) * deep_bias[None, :] + deep_coeffs * deep_offset, axis=1
    )
    weight_block = deep_weight
    first_coeffs = jnp.dot(
        lax.all_gather(deep_sent, "neu", axis=1, tiled=True),
        weight_block,
        preferred_element_type=jnp.float32,
    )
    first_factor, first_offset, first_chosen = relax_layer(
        first_coeffs, first_status, first_bounds, first_slopes
    )
    first_sent = (first_coeffs * first_factor).astype(jnp.bfloat16)
    first_const = jnp.sum(
        first_sent.astype(jnp.float32) * first_bias[None, :] + first_coeffs * first_offset, axis=1
    )
    weight_block = first_weight
    input_coeffs = jnp.dot(
        lax.all_gather(first_sent, "neu", axis=1, tiled=True),
        weight_block,
        preferred_element_type=jnp.float32,
    )
    partial_bound = (
        jnp.sum(
            input_coeffs * box_center[None, :] - jnp.abs(input_coeffs) * box_radius[None, :], axis=1
        )
        + first_const
        + deep_const
    )
    bound_rows = lax.psum(partial_bound, "neu")
    input_grads = (box_center[None, :] - jnp.sign(input_coeffs) * box_radius[None, :]).astype(
        jnp.bfloat16
    )
    weight_block = first_weight
    first_back = (
        lax.psum_scatter(
            contract_last(weight_block, input_grads).astype(jnp.bfloat16),
            "neu",
            scatter_dimension=0,
            tiled=True,
        )
        .astype(jnp.float32)
        .T
    )
    first_grads = first_back + first_bias[None, :]
    back_grads = (first_grads * first_factor + first_offset).astype(jnp.bfloat16)
    weight_block = deep_weight
    deep_back = (
        lax.psum_scatter(
            contract_last(weight_block, back_grads).astype(jnp.bfloat16),
            "neu",
            scatter_dimension=0,
            tiled=True,
        )
        .astype(jnp.float32)
        .T
    )
    deep_grads = deep_back + deep_bias[None, :]
    first_part = jnp.sum(first_grads * first_coeffs * first_chosen, axis=0)
    deep_part = jnp.sum(deep_grads * deep_coeffs * deep_chosen, axis=0)
    first_sum, deep_sum = lax.psum((first_part, deep_part), "dom")
    first_power, deep_power = lax.psum(
        (jnp.sum(first_sum * first_sum), jnp.sum(deep_sum * deep_sum)), "neu"
    )
    first_next = advance(first_slopes, first_sum, first_power)
    deep_next = advance(deep_slopes, deep_sum, deep_power)
    return (bound_rows, first_next, deep_next)


def solution(mesh):
    in_specs = (
        P("dom"),
        P("dom"),
        P(None, "neu"),
        P(None, "neu"),
        P("neu"),
        P("dom", "neu"),
        P(None, "dom", "neu"),
        P("neu"),
        P(None, "neu"),
        P("neu"),
        P("dom", "neu"),
        P(None, "dom", "neu"),
        P("neu"),
        P("neu"),
        P("neu"),
    )
    out_specs = (P("dom"), P("neu"), P("neu"))
    return jax.shard_map(
        on_device, mesh=mesh, in_specs=in_specs, out_specs=out_specs, check_vma=False
    )
```

profile of v0, /device:TPU:1, one launch (start us, length us, event | category | flops | bytes accessed | tf_op | source)
XLA Modules:
  0.0 538.2 jit_solution(16917038298632530872)
XLA Ops:
  7.2 0.0 all-gather.3.cloned.1.call-start
  7.2 0.9 broadcast_compare_fusion.4
  8.1 0.9 fusion.43
  9.0 0.7 and_select_fusion
  9.8 0.8 negate_multiply_fusion
  10.5 1.6 fusion.3
  12.1 0.0 all-gather.3.cloned.1.call-update
  12.1 0.0 all-gather.5.cloned.1.call-start
  12.2 0.8 broadcast_compare_fusion.3
  13.0 0.9 fusion.42
  13.9 0.8 negate_multiply_fusion.1
  14.7 85.8 %all-gather.3.cloned.1.call-done = bf16[216,8192]{1,0:T(8,128)(2,1)} async-done(((bf16[216,256]{1,0:T(8,128)(2,1)}), bf16[216,8192]{1,0:T(8,128)(2,1)}) %all-gather.3.cloned.1.call-update) | async-done | bytes 3538960 | tf_op jit(solution)/shard_map/all_gather | solution.py:80
  100.5 5.1 fusion.17
  105.5 0.0 all-gather.5.cloned.1.call-update
  105.6 0.0 reduce-scatter.3.cloned.1.call-start
  105.6 80.6 %all-gather.5.cloned.1.call-done = bf16[216,8192]{1,0:T(8,128)(2,1)} async-done(((bf16[216,256]{1,0:T(8,128)(2,1)}), bf16[216,8192]{1,0:T(8,128)(2,1)}) %all-gather.5.cloned.1.call-update) | async-done | bytes 3538960 | tf_op jit(solution)/shard_map/all_gather | solution.py:93
  186.2 3.3 subtract_reduce_fusion
  189.6 2.9 fusion
  192.5 0.0 reduce-scatter.5.cloned.1.call-start
  192.6 116.9 %reduce-scatter.3.cloned.1.call-done = bf16[256,216]{0,1:T(8,128)(2,1)} async-done(((bf16[8192,216]{0,1:T(8,128)(2,1)}), bf16[256,216]{0,1:T(8,128)(2,1)}) %reduce-scatter.3.cloned.1.call-update) | async-done | bytes 110608 | tf_op jit(solution)/shard_map/reduce_scatter | solution.py:110
  309.4 5.5 %fusion.1 = bf16[8192,216]{0,1:T(8,128)(2,1)} fusion(bf16[8192,256]{1,0:T(8,128)(2,1)} %param.18, bf16[256,216]{0,1:T(8,128)(2,1)} %reduce-scatter.3.cloned.1.call-done, f32[256]{0:T(256)S(1)} %copy-done.2, f32[27,256]{1,0:T(8,128)S(1)} %get-tuple-element.14, f32[27,256]{1,0:T(8,128)S(1)} %get-tuple-element.27, f32[27,256]{1,0:T(8,128)S(1)} %get-tuple-element.15, ...), kind=kOutput, calls=%fused_computation.3 | convolution fusion | flops 908347392 | bytes 8156928 | tf_op jit(solution)/shard_map/dot_general | solution.py:40
  315.0 0.0 reduce-scatter.5.cloned.1.call-update
  315.0 0.9 copy-done.1
  315.9 0.3 fusion.7
  316.2 121.3 %reduce-scatter.5.cloned.1.call-done = bf16[256,216]{0,1:T(8,128)(2,1)} async-done(((bf16[8192,216]{0,1:T(8,128)(2,1)}), bf16[256,216]{0,1:T(8,128)(2,1)}) %reduce-scatter.5.cloned.1.call-update) | async-done | bytes 110608 | tf_op jit(solution)/shard_map/reduce_scatter | solution.py:123
  437.5 1.2 fusion.5
  438.7 14.9 %all-reduce.1 = (f32[256]{0:T(256)S(1)}, f32[256]{0:T(256)S(1)}) all-reduce(f32[256]{0:T(256)S(1)} %get-tuple-element.5, f32[256]{0:T(256)S(1)} %get-tuple-element.3), channel_id=1, replica_groups=mesh['dom'=8,'neu'=32] {'dom'}, use_global_device_ids=true, to_apply=%region_6.7 | all-reduce | flops 512 | bytes 4096 | tf_op jit(solution)/shard_map/psum | solution.py:135
  453.6 0.6 multiply_reduce_fusion
  454.2 0.6 multiply_reduce_fusion.1
  454.8 74.3 %all-reduce = (f32[216]{0:T(256)}, f32[]{:T(128)}, f32[]{:T(128)}) all-reduce(f32[216]{0:T(256)S(1)} %add_add_fusion, f32[]{:T(128)} %multiply_reduce_fusion.1, f32[]{:T(128)} %multiply_reduce_fusion), channel_id=1, replica_groups=mesh['dom'=8,'neu'=32] {'neu'}, use_global_device_ids=true, to_apply=%region_3.4 | all-reduce | flops 218 | bytes 1744 | tf_op jit(solution)/shard_map/psum | solution.py:104
  530.5 0.6 fusion.39
  531.1 0.6 fusion.40
  (17 shorter events, 0.1 us)
Async XLA Ops:
  7.2 179.1 %copy-start = (bf16[8192,96]{0,1:T(8,128)(2,1)S(1)}, bf16[8192,96]{0,1:T(8,128)(2,1)}, u32[]{:S(2)}) copy-start(bf16[8192,96]{0,1:T(8,128)(2,1)} %param.23) | copy-start | bytes 4718596
  7.2 93.3 %all-gather.3.cloned.1.call-start = ((), (), s32[]{:S(2)}) async-start(), calls=%async_computation.2 | async-start | bytes 3649536 | tf_op jit(solution)/shard_map/all_gather | solution.py:80
  12.1 174.1 %all-gather.5.cloned.1.call-start = ((), (), s32[]{:S(2)}) async-start(), calls=%async_computation.3 | async-start | bytes 3649536 | tf_op jit(solution)/shard_map/all_gather | solution.py:93
  100.5 85.8 %copy-start.5 = (f32[96]{0:T(128)S(1)}, f32[96]{0:T(128)}, u32[]{:S(2)}) copy-start(f32[96]{0:T(128)} %param.29) | copy-start | bytes 1156
  100.5 85.8 %copy-start.6 = (f32[96]{0:T(128)S(1)}, f32[96]{0:T(128)}, u32[]{:S(2)}) copy-start(f32[96]{0:T(128)} %param.28) | copy-start | bytes 1156
  105.6 203.9 %reduce-scatter.3.cloned.1.call-start = ((), (), s32[]{:S(2)}) async-start(), calls=%async_computation.4 | async-start | bytes 3649536 | tf_op jit(solution)/shard_map/reduce_scatter | solution.py:110
  189.5 119.9 %copy-start.2 = (f32[256]{0:T(256)S(1)}, f32[256]{0:T(256)}, u32[]{:S(2)}) copy-start(f32[256]{0:T(256)} %param.24) | copy-start | bytes 3076
  189.6 119.9 %copy-start.3 = (f32[256]{0:T(256)S(1)}, f32[256]{0:T(256)}, u32[]{:S(2)}) copy-start(f32[256]{0:T(256)} %param.27) | copy-start | bytes 3076
  192.5 245.0 %reduce-scatter.5.cloned.1.call-start = ((), (), s32[]{:S(2)}) async-start(), calls=%async_computation.5 | async-start | bytes 3649536 | tf_op jit(solution)/shard_map/reduce_scatter | solution.py:123
  315.0 0.9 copy-start.1
  315.0 122.5 %copy-start.4 = (f32[256]{0:T(256)S(1)}, f32[256]{0:T(256)}, u32[]{:S(2)}) copy-start(f32[256]{0:T(256)} %param.22) | copy-start | bytes 3076
  315.0 122.5 %copy-start.7 = (f32[256]{0:T(256)S(1)}, f32[256]{0:T(256)}, u32[]{:S(2)}) copy-start(f32[256]{0:T(256)} %param.19) | copy-start | bytes 3076
Sparse Core Ops, SparseCore 0:
  12.3 88.1 all-gather.2
  105.7 80.5 all-gather.4
  192.7 116.7 reduce-scatter.2
  315.1 122.3 reduce-scatter.4
where the time goes:
time: 539 us; the launch traced here: 538 us
  waiting for transfers between devices  405 us (75%)
  blocking collectives  89.3 us (17%)
  matrix products  18.4 us (3%)
  between operations  15.2 us (3%)
  other arithmetic  7.7 us (1%)
    reduce_scatter x1, waiting for transfers between devices, on_device(): lax.psum_scatter(contract_last(weight_block, back_grads).astype(jnp.bfloa...  121 us
    reduce_scatter x1, waiting for transfers between devices, on_device(): lax.psum_scatter(contract_last(weight_block, input_grads).astype(jnp.bflo...  117 us
    all_gather x1, waiting for transfers between devices, on_device(): lax.all_gather(deep_sent, 'neu', axis=1, tiled=True)  85.8 us
    all_gather x1, waiting for transfers between devices, on_device(): lax.all_gather(first_sent, 'neu', axis=1, tiled=True)  80.6 us
    psum x1, blocking collectives, on_device(): bound_rows = lax.psum(partial_bound, 'neu')  74.3 us
    psum x1, blocking collectives, on_device(): first_sum, deep_sum = lax.psum((first_part, deep_part), 'dom')  14.9 us
  transfers between devices with their start and end apart: 4, of which 4 were waited for; matrix products, arithmetic and copies ran while one was open for 1% of the time, Pallas kernels for 0%

commit v1 on v0

v1 whole, which is shorter than its diff:
```python
import functools

import jax
import jax.numpy as jnp
from jax import lax
from jax.experimental import pallas as pl
from jax.experimental.pallas import tpu as pltpu
from jax.sharding import Mesh
from jax.sharding import PartitionSpec as P

HIDDEN_SIZE = 8192
CLASSES = 10
GROUP = 8
LANES = 256

grid_step = 0.0625
step_rate = 0.25
epsilon = 1e-06

ROWS_UP, ROWS_LOW, ROWS_CLASS, ROWS_ALL = 0, 32, 64, 80

DOM = ("ylo", "x")
NEU = ("yhi", "z", "core")
F32, BF16 = jnp.float32, jnp.bfloat16


def spread(per_domain):
    count, width = per_domain.shape
    return jnp.broadcast_to(per_domain[:, None, :], (count, GROUP, width)).reshape(
        count * GROUP, width
    )


def contract(left, right, left_dim, right_dim):
    return lax.dot_general(
        left, right, (((left_dim,), (right_dim,)), ((), ())), preferred_element_type=F32
    )


def selector(label, offset):
    second = label + offset
    second = jnp.where(second >= CLASSES, second - CLASSES, second)
    classes = lax.broadcasted_iota(jnp.int32, (16, label.shape[1]), 0)
    picked = jnp.where(classes == label, 1.0, 0.0) - jnp.where(classes == second, 1.0, 0.0)
    return picked.astype(BF16)


def decode(block, domains):
    up = block[ROWS_UP : ROWS_UP + 32].astype(F32)[:domains]
    low = block[ROWS_LOW : ROWS_LOW + 32].astype(F32)[:domains]
    tail = block[ROWS_CLASS:ROWS_ALL].astype(F32)
    slope = tail[10:11] + tail[11:12] + tail[12:13]
    ratio = up / (up + low)
    unsplit = (up > 0.0) & (low > 0.0)
    return up, low, ratio, slope, unsplit


def relax_rows(coeffs, status, low, up, slopes):
    ratio = up / (up + low)
    cept = ratio * (low * grid_step)
    unsplit = status == 2
    fixed = jnp.where(status == 1, 1.0, 0.0)
    at_pos = spread(jnp.where(unsplit, jnp.broadcast_to(slopes, ratio.shape), fixed))
    at_neg = spread(jnp.where(unsplit, ratio, fixed))
    off_neg = spread(jnp.where(unsplit, cept, 0.0))
    on_pos = spread(jnp.where(unsplit, 1.0, 0.0))
    positive = coeffs >= 0.0
    factor = jnp.where(positive, at_pos, at_neg)
    offset = jnp.where(positive, 0.0, off_neg)
    chosen = jnp.where(positive, on_pos, 0.0)
    return factor, offset, chosen


def forward_kernel(
    label_ref, offset_ref, a_ref, b_ref, c_ref, d_ref, weight_ref, deep_bias_ref,
    status_ref, bounds_ref, slopes_ref, bias_ref,
    sent_ref, coeffs_ref, const_ref, total, terms,
):
    step = pl.program_id(0)
    yhi, z, core = (lax.axis_index(n) for n in NEU)
    domains = status_ref.shape[0]
    select = selector(label_ref[...], offset_ref[...])

    @pl.when(step == 0)
    def _():
        total[...] = jnp.zeros_like(total)

    acc = total[...]
    for place, ref in enumerate((a_ref, b_ref, c_ref, d_ref)):
        other_y, other_core = place % 2, place // 2
        block = ref[0]
        up, low, ratio, slope, unsplit = decode(block, domains)
        coeffs = contract(select, block[ROWS_CLASS:ROWS_ALL], 0, 0)
        at_pos = jnp.where(unsplit, jnp.broadcast_to(slope, ratio.shape), ratio)
        factor = jnp.where(coeffs >= 0.0, spread(at_pos), spread(ratio))
        sent = (coeffs * factor).astype(BF16)
        if place == 0:

            @pl.when(step == z)
            def _():
                cept = jnp.where(unsplit, ratio * (low * grid_step), 0.0)
                terms[...] = sent.astype(F32) * deep_bias_ref[...] + jnp.where(
                    coeffs >= 0.0, 0.0, coeffs * spread(cept)
                )

        weight = weight_ref[yhi if not other_y else 1 - yhi, 0, core if not other_core else 1 - core]
        acc = acc + jnp.dot(sent, weight, preferred_element_type=F32)
    total[...] = acc

    @pl.when(step == pl.num_programs(0) - 1)
    def _():
        coeffs = total[...]
        factor, offset, _ = relax_rows(
            coeffs, status_ref[...], bounds_ref[0].astype(F32), bounds_ref[1].astype(F32), slopes_ref[...]
        )
        sent = (coeffs * factor).astype(BF16)
        sent_ref[...] = sent
        coeffs_ref[...] = coeffs
        summed = terms[...] + sent.astype(F32) * bias_ref[...] + coeffs * offset
        const_ref[...] = lax.dot_general(
            jnp.ones((8, summed.shape[1]), F32), summed, (((1,), (1,)), ((), ())),
            precision=lax.Precision.HIGHEST, preferred_element_type=F32,
        )


def input_kernel(a_ref, b_ref, c_ref, d_ref, w0_ref, w1_ref, w2_ref, w3_ref, out_ref, held):
    yhi, core, x = lax.axis_index("yhi"), lax.axis_index("core"), lax.axis_index("x")
    own = yhi * 2 + core
    for place, ref in enumerate((a_ref, b_ref, c_ref, d_ref)):
        held[own ^ ((place % 2) * 2 + place // 2)] = ref[...]
    zs, feats, _ = w0_ref.shape
    acc = None
    for k, ref in enumerate((w0_ref, w1_ref, w2_ref, w3_ref)):
        part = contract(ref[...].reshape(zs * feats, LANES), held[(x + 4 - k) % 4], 1, 1)
        acc = part if acc is None else acc + part
    out_ref[...] = acc.reshape(zs, feats, acc.shape[1])


def box_kernel(parts_ref, center_ref, radius_ref, const_ref, grads_ref, bound_ref):
    coeffs = parts_ref[0]
    for k in range(1, parts_ref.shape[0]):
        coeffs = coeffs + parts_ref[k]
    center, radius = center_ref[...], radius_ref[...]
    signed = jnp.where(coeffs > 0.0, radius, jnp.where(coeffs < 0.0, -radius, 0.0))
    grads = (center - signed).astype(BF16)
    for k in range(grads_ref.shape[0]):
        grads_ref[k] = grads
    terms = coeffs * center - jnp.abs(coeffs) * radius
    bound_ref[...] = jnp.sum(terms, axis=0, keepdims=True) + const_ref[0:1]


def grads_kernel(g_ref, w0_ref, w1_ref, w2_ref, w3_ref, near_ref, far_ref):
    yhi, core, x = lax.axis_index("yhi"), lax.axis_index("core"), lax.axis_index("x")
    own = yhi * 2 + core
    zs, feats, rows = g_ref.shape
    grads = g_ref[...].reshape(zs * feats, rows)
    for k, ref in enumerate((w0_ref, w1_ref, w2_ref, w3_ref)):
        part = contract(grads, ref[...].reshape(zs * feats, LANES), 0, 0)
        place = own ^ ((x + 4 - k) % 4)

        @pl.when(place % 2 == 0)
        def _():
            near_ref[place // 2] = part

        @pl.when(place % 2 == 1)
        def _():
            far_ref[place // 2] = part


def backward_kernel(
    label_ref, offset_ref, a_ref, b_ref, c_ref, d_ref, weight_ref, deep_bias_ref,
    status_ref, bounds_ref, slopes_ref, bias_ref, coeffs_ref, mine_ref, their_ref, bound_ref,
    out_ref, back,
):
    step = pl.program_id(0)
    yhi, z, core = (lax.axis_index(n) for n in NEU)
    domains = status_ref.shape[0]
    select = selector(label_ref[...], offset_ref[...])

    @pl.when(step == 0)
    def _():
        coeffs = coeffs_ref[...]
        grads = mine_ref[...] + their_ref[...].astype(F32) + bias_ref[...]
        factor, offset, chosen = relax_rows(
            coeffs, status_ref[...], bounds_ref[0].astype(F32), bounds_ref[1].astype(F32), slopes_ref[...]
        )
        back[...] = (grads * factor + offset).astype(BF16)
        out_ref[32:40] = jnp.zeros((8, LANES), F32)
        out_ref[32:33] = jnp.sum(grads * coeffs * chosen, axis=0, keepdims=True)
        out_ref[33:34, 0 : bound_ref.shape[1]] = bound_ref[...]

    for place, ref in enumerate((a_ref, b_ref, c_ref, d_ref)):
        other_y, other_core = place % 2, place // 2
        block = ref[0]
        _, _, _, _, unsplit = decode(block, domains)
        coeffs = contract(select, block[ROWS_CLASS:ROWS_ALL], 0, 0)
        mask = spread(jnp.where(unsplit, 1.0, 0.0))
        kept = jnp.maximum(coeffs, 0.0) * mask
        y = yhi if not other_y else 1 - yhi
        c = core if not other_core else 1 - core
        grads = contract(back[...], weight_ref[y, 0, c], 1, 1)
        if place == 0:
            grads = grads + jnp.where(step == z, 1.0, 0.0) * deep_bias_ref[...]
        out_ref[pl.ds((y * 8 + step) * 2 + c, 1)] = jnp.sum(grads * kept, axis=0, keepdims=True)


def whole(shape):
    return pl.BlockSpec(shape, lambda s: (0,) * len(shape))


def shifted(value, axis, size, by):
    return lax.ppermute(value, axis, [(i, (i + by) % size) for i in range(size)])


def on_device(
    spec_label, spec_offset, class_rows, deep_weight, deep_bias, deep_status, deep_bounds,
    deep_slopes, first_weight, first_bias, first_status, first_bounds, first_slopes,
    box_center, box_radius,
):
    rows = spec_label.shape[0]
    domains = deep_status.shape[0]
    feats = box_center.shape[0]
    params = pltpu.CompilerParams(vmem_limit_bytes=24 * 1024 * 1024)

    active, unsplit = deep_status == 1, deep_status == 2
    up = jnp.where(unsplit, deep_bounds[1], jnp.where(active, 1, 0))
    low = jnp.where(unsplit, deep_bounds[0], jnp.where(active, 0, 1))
    high = lax.reduce_precision(deep_slopes, 8, 7)
    rest = deep_slopes - high
    middle = lax.reduce_precision(rest, 8, 7)
    last = rest - middle
    pad = jnp.ones((32 - domains, LANES), F32)
    info = jnp.concatenate(
        [
            up.astype(F32), pad, low.astype(F32), pad, class_rows.astype(F32),
            high[None], middle[None], last[None], jnp.zeros((3, LANES), F32),
        ],
        axis=0,
    ).astype(BF16)
    x = lax.axis_index("x")
    quarter = lax.dynamic_index_in_dim(
        first_weight.reshape(2, 8, 2, LANES, feats).transpose(0, 2, 1, 3, 4).reshape(4, 8, LANES, feats),
        x, 0, keepdims=False,
    )
    message = jnp.concatenate(
        [jnp.broadcast_to(info[None], (8,) + info.shape), quarter.transpose(0, 2, 1)], axis=1
    )
    message = lax.all_to_all(message, "z", 0, 0, tiled=True)
    info_a = message[:, :ROWS_ALL]
    w_own = message[:, ROWS_ALL:]
    info_b = shifted(info_a, "yhi", 2, 1)
    info_c = shifted(info_a, "core", 2, 1)
    info_d = shifted(info_b, "core", 2, 1)
    w_all = [w_own] + [shifted(w_own, "x", 4, k) for k in (1, 2, 3)]
    infos = (info_a, info_b, info_c, info_d)

    label, offset = spec_label[None], spec_offset[None]
    weight = deep_weight.reshape(2, 8, 2, LANES, LANES)
    info_spec = pl.BlockSpec((1, ROWS_ALL, LANES), lambda s: (s, 0, 0))
    weight_spec = pl.BlockSpec((2, 1, 2, LANES, LANES), lambda s: (0, s, 0, 0, 0))
    layer_specs = [whole((domains, LANES)), whole((2, domains, LANES)), whole((1, LANES)), whole((1, LANES))]
    layer = (first_status, first_bounds, first_slopes[None], first_bias[None])

    sent, coeffs, const = pl.pallas_call(
        forward_kernel,
        grid=(8,),
        in_specs=[whole((1, rows))] * 2 + [info_spec] * 4 + [weight_spec, whole((1, LANES))] + layer_specs,
        out_specs=[whole((rows, LANES)), whole((rows, LANES)), whole((8, rows))],
        out_shape=[
            jax.ShapeDtypeStruct((rows, LANES), BF16),
            jax.ShapeDtypeStruct((rows, LANES), F32),
            jax.ShapeDtypeStruct((8, rows), F32),
        ],
        scratch_shapes=[pltpu.VMEM((rows, LANES), F32), pltpu.VMEM((rows, LANES), F32)],
        compiler_params=params,
        name="forward",
    )(label, offset, *infos, weight, deep_bias[None], *layer)

    sent_b = shifted(sent, "yhi", 2, 1)
    sent_c = shifted(sent, "core", 2, 1)
    sent_d = shifted(sent_b, "core", 2, 1)
    parts = pl.pallas_call(
        input_kernel,
        out_shape=jax.ShapeDtypeStruct((8, feats, rows), F32),
        scratch_shapes=[pltpu.VMEM((4, rows, LANES), BF16)],
        compiler_params=params,
        name="inputs",
    )(sent, sent_b, sent_c, sent_d, *w_all)
    parts = lax.all_to_all(parts, "z", 0, 0, tiled=True)
    grads, bound = pl.pallas_call(
        box_kernel,
        out_shape=[jax.ShapeDtypeStruct((8, feats, rows), BF16), jax.ShapeDtypeStruct((1, rows), F32)],
        compiler_params=params,
        name="box",
    )(parts, box_center[:, None], box_radius[:, None], const)
    grads = lax.all_to_all(grads, "z", 0, 0, tiled=True)
    near, far = pl.pallas_call(
        grads_kernel,
        out_shape=[jax.ShapeDtypeStruct((2, rows, LANES), F32)] * 2,
        compiler_params=params,
        name="grads",
    )(grads, *w_all)
    near = near + shifted(far, "core", 2, 1)
    their = shifted(near[1].astype(BF16), "yhi", 2, 1)

    summary = pl.pallas_call(
        backward_kernel,
        grid=(8,),
        in_specs=[whole((1, rows))] * 2
        + [info_spec] * 4
        + [weight_spec, whole((1, LANES))]
        + layer_specs
        + [whole((rows, LANES))] * 3
        + [whole((1, rows))],
        out_specs=whole((40, LANES)),
        out_shape=jax.ShapeDtypeStruct((40, LANES), F32),
        scratch_shapes=[pltpu.VMEM((rows, LANES), BF16)],
        compiler_params=params,
        name="backward",
    )(label, offset, *infos, weight, deep_bias[None], *layer, coeffs, near[0], their, bound)

    gathered = lax.all_to_all(jnp.broadcast_to(summary[None], (8, 40, LANES)), "z", 0, 0, tiled=True)
    sums = jnp.concatenate([jnp.sum(gathered[:, :32], axis=0), gathered[:, 32]], axis=0)
    bound = jnp.sum(gathered[:, 33], axis=0)
    moved = [shifted(sums, "x", 4, k) for k in (1, 2, 3)]
    sums = (sums + moved[1]) + (moved[0] + moved[2])
    sums = sums + shifted(sums, "ylo", 2, 1)
    first_all = sums[32:]
    first_power = jnp.sum(first_all * first_all)
    deep = jnp.concatenate([sums[:32], bound[None], jnp.full((1, LANES), first_power)], axis=0)
    deep = deep + shifted(deep, "core", 2, 1)
    deep = deep + shifted(deep, "yhi", 2, 1)
    z = lax.axis_index("z")
    own = (lax.axis_index("yhi") * 8 + z) * 2 + lax.axis_index("core")
    first_sum = lax.dynamic_index_in_dim(first_all, z, 0, keepdims=False)
    deep_sum = lax.dynamic_index_in_dim(deep, own, 0, keepdims=False)
    deep_power = jnp.sum(deep[:32] * deep[:32])

    def advance(slopes, gradient, squares):
        root_mean = jnp.sqrt(squares / HIDDEN_SIZE + epsilon)
        return jnp.clip(slopes + step_rate * gradient / root_mean, 0.0, 1.0)

    return (
        deep[32, :rows],
        advance(first_slopes, first_sum, deep[33, 0]),
        advance(deep_slopes, deep_sum, deep_power),
    )


def solution(mesh):
    fine = Mesh(mesh.devices.reshape(2, 4, 2, 8, 2), DOM + NEU)
    in_specs = (
        P(DOM), P(DOM), P(None, NEU), P(None, NEU), P(NEU), P(DOM, NEU), P(None, DOM, NEU), P(NEU),
        P(None, NEU), P(NEU), P(DOM, NEU), P(None, DOM, NEU), P(NEU), P(NEU), P(NEU),
    )
    out_specs = (P(DOM), P(NEU), P(NEU))
    return jax.shard_map(on_device, mesh=fine, in_specs=in_specs, out_specs=out_specs, check_vma=False)
```

time: 539 us -> 169 us (0.31)
  waiting for transfers between devices: 405 us -> 36.7 us
  starting transfers between devices: 0.16 us -> 44.6 us
  blocking collectives: 89.3 us -> 58.9 us
  matrix products: 18.4 us -> 0 us
  Pallas kernels: 0 us -> 14.4 us
  between operations: 15.2 us -> 2.47 us
  local copies, waits for them, and re-layouts: 2.78 us -> 8.41 us
    reduce_scatter x2 -> x0, waiting for transfers between devices: 238 us -> none  [the longest x1 121 us: on_device(): lax.psum_scatter(contract_last(weight_block, back_grads).astype(jnp.bfloa...]
    all_gather x2 -> x0, waiting for transfers between devices: 166 us -> none  [the longest x1 85.8 us: on_device(): lax.all_gather(deep_sent, 'neu', axis=1, tiled=True)]
    psum x2 -> x0, blocking collectives: 89.3 us -> none  [the longest x1 74.3 us: on_device(): bound_rows = lax.psum(partial_bound, 'neu')]
    all_to_all x0 -> x3, blocking collectives: none -> 58.9 us  [the longest x1 29.2 us: on_device(): message = lax.all_to_all(message, 'z', 0, 0, tiled=True)]
    ppermute x0 -> x17, starting transfers between devices: none -> 41.1 us  [shifted(): lax.ppermute(value, axis, [(i, (i + by) % size) for i in range(size)])]
    all_to_all x0 -> x1, waiting for transfers between devices: none -> 20.8 us  [on_device(): parts = lax.all_to_all(parts, 'z', 0, 0, tiled=True)]
    dot_general x5 -> x0, matrix products: 18.4 us -> none  [the longest x2 8.48 us: contract_last(): lax.dot_general(left, right, (((1,), (1,)), ((), ())), preferred_element_...]
    ppermute x0 -> x17, waiting for transfers between devices: none -> 15.9 us  [shifted(): lax.ppermute(value, axis, [(i, (i + by) % size) for i in range(size)])]
  transfers between devices with their start and end apart: 4 -> 18, of which waited for: 4 -> 10; matrix products, arithmetic and copies ran while one was open for 1% -> 1% of each run, Pallas kernels for 0% -> 4%
where the time goes in v1:
time: 169 us; the launch traced here: 168 us
  blocking collectives  58.9 us (35%)
  starting transfers between devices  44.6 us (26%)
  waiting for transfers between devices  36.7 us (22%)
  Pallas kernels  14.4 us (9%)
  local copies, waits for them, and re-layouts  8.41 us (5%)
  other arithmetic  2.87 us (2%)
  between operations  2.47 us (1%)
    ppermute x17, starting transfers between devices, shifted(): lax.ppermute(value, axis, [(i, (i + by) % size) for i in range(size)])  41.1 us
    all_to_all x1, blocking collectives, on_device(): message = lax.all_to_all(message, 'z', 0, 0, tiled=True)  29.2 us
    all_to_all x1, waiting for transfers between devices, on_device(): parts = lax.all_to_all(parts, 'z', 0, 0, tiled=True)  20.8 us
    ppermute x17, waiting for transfers between devices, shifted(): lax.ppermute(value, axis, [(i, (i + by) % size) for i in range(size)])  15.9 us
    all_to_all x1, blocking collectives, on_device(): grads = lax.all_to_all(grads, 'z', 0, 0, tiled=True)  15.7 us
    all_to_all x1, blocking collectives, on_device(): lax.all_to_all(jnp.broadcast_to(summary[None], (8, 40, LANES)), 'z', 0, 0...  14.1 us
    pallas_call x1, Pallas kernels, on_device(): pl.pallas_call(forward_kernel, grid=(8,), in_specs=[whole((1, rows))] * 2...  6.64 us
    pallas_call x1, Pallas kernels, on_device(): pl.pallas_call(backward_kernel, grid=(8,), in_specs=[whole((1, rows))] *...  4.7 us
  transfers between devices with their start and end apart: 18, of which 10 were waited for; matrix products, arithmetic and copies ran while one was open for 1% of the time, Pallas kernels for 4%

profile of v1, /device:TPU:1, one launch (start us, length us, event | category | flops | bytes accessed | tf_op | source)
XLA Modules:
  0.0 168.4 jit_solution(17784390019513866793)
XLA Ops:
  2.3 2.9 %reshape.91 = bf16[2,8,2,256,96]{3,2,1,0,4:T(2,128)(2,1)S(1)} reshape(bf16[8192,96]{0,1:T(8,128)(2,1)} %param.23) | data formatting | bytes 3145728 | tf_op jit(solution)/shard_map/reshape | solution.py:242
  6.4 29.2 %all_to_all.20 = bf16[8,176,256]{2,1,0:T(8,128)(2,1)S(1)} all-to-all(bf16[8,176,256]{2,1,0:T(8,128)(2,1)S(1)} %pad_maximum_fusion), channel_id=1, replica_groups=mesh['ylo'=2,'x'=4,'yhi'=2,'z'=8,'core'=2] {'z'}, dimensions={0} | all-to-all | bytes 1441792 | tf_op jit(solution)/shard_map/all_to_all | solution.py:248
  35.7 3.0 %collective-permute-start = (bf16[8,80,256]{2,1,0:T(8,128)(2,1)S(1)}, bf16[8,80,256]{2,1,0:T(8,128)(2,1)S(1)}, u32[]{:S(2)}, u32[]{:S(2)}) collective-permute-start(bf16[8,80,256]{2,1,0:T(8,128)(2,1)S(1)} %slice.58.a_ref), channel_id=1, source_target_pairs={{0,16},{16,0},{1,17},{17,1},{2,18},{18,2},{3,19},{19,3},{4,20},{20... | collective-permute-start | bytes 983048 | tf_op jit(solution)/shard_map/ppermute | solution.py:212
  38.7 2.8 %collective-permute-start.1 = (bf16[8,80,256]{2,1,0:T(8,128)(2,1)S(1)}, bf16[8,80,256]{2,1,0:T(8,128)(2,1)S(1)}, u32[]{:S(2)}, u32[]{:S(2)}) collective-permute-start(bf16[8,80,256]{2,1,0:T(8,128)(2,1)S(1)} %slice.58.a_ref), channel_id=1, source_target_pairs={{0,1},{1,0},{2,3},{3,2},{4,5},{5,4},{6,7},{7,6},{8,9},{9,8},{10,11... | collective-permute-start | bytes 983048 | tf_op jit(solution)/shard_map/ppermute | solution.py:212
  41.5 2.4 %collective-permute-done.b_ref = bf16[8,80,256]{2,1,0:T(8,128)(2,1)S(1)} collective-permute-done((bf16[8,80,256]{2,1,0:T(8,128)(2,1)S(1)}, bf16[8,80,256]{2,1,0:T(8,128)(2,1)S(1)}, u32[]{:S(2)}, u32[]{:S(2)}) %collective-permute-start) | collective-permute-done | bytes 327712 | tf_op jit(solution)/shard_map/ppermute | solution.py:212
  43.9 3.5 %collective-permute-start.2 = (bf16[8,80,256]{2,1,0:T(8,128)(2,1)S(1)}, bf16[8,80,256]{2,1,0:T(8,128)(2,1)S(1)}, u32[]{:S(2)}, u32[]{:S(2)}) collective-permute-start(bf16[8,80,256]{2,1,0:T(8,128)(2,1)S(1)} %collective-permute-done.b_ref), channel_id=1, source_target_pairs={{0,1},{1,0},{2,3},{3,2},{4,5},{5,4},{6,7},{7,6},{8,9},{9,8},{10,11... | collective-permute-start | bytes 983048 | tf_op jit(solution)/shard_map/ppermute | solution.py:212
  47.4 1.3 collective-permute-start.6
  48.7 2.5 %collective-permute-start.7 = (bf16[8,96,256]{2,1,0:T(8,128)(2,1)S(1)}, bf16[8,96,256]{2,1,0:T(8,128)(2,1)S(1)}, u32[]{:S(2)}, u32[]{:S(2)}) collective-permute-start(bf16[8,96,256]{2,1,0:T(8,128)(2,1)S(1)} %slice.59.w0_ref), channel_id=1, source_target_pairs={{0,64},{32,96},{64,0},{96,32},{1,65},{33,97},{65,1},{97,33},{2,66}... | collective-permute-start | bytes 1179656 | tf_op jit(solution)/shard_map/ppermute | solution.py:212
  52.4 6.6 %forward.1 = (bf16[216,256]{1,0:T(8,128)(2,1)S(1)}, f32[216,256]{1,0:T(8,128)S(1)}, f32[8,216]{1,0:T(8,128)S(1)}) custom-call(s32[1,216]{1,0:T(1,128)S(1)} %bitcast.49, s32[1,216]{1,0:T(1,128)S(1)} %bitcast.51, bf16[8,80,256]{2,1,0:T(8,128)(2,1)S(1)} %slice.58.a_ref, bf16[8,80,256]{2,1,0:T(8,128)(2,1)S(1)} %collective-permute-done.b_ref, ...), custom_call_target="tpu_custom_call" | custom-call | tf_op jit(solution)/shard_map/forward/pallas_call | solution.py:264
  59.8 2.9 %collective-permute-start.3 = (bf16[216,256]{1,0:T(8,128)(2,1)S(1)}, bf16[216,256]{1,0:T(8,128)(2,1)S(1)}, u32[]{:S(2)}, u32[]{:S(2)}) collective-permute-start(bf16[216,256]{1,0:T(8,128)(2,1)S(1)} %get-tuple-element.11.a_ref), channel_id=1, source_target_pairs={{0,16},{16,0},{1,17},{17,1},{2,18},{18,2},{3,19},{19,3},{4,20},{20... | collective-permute-start | bytes 331784 | tf_op jit(solution)/shard_map/ppermute | solution.py:212
  63.8 1.4 collective-permute-done.3.b_ref
  65.2 1.7 %collective-permute-start.5 = (bf16[216,256]{1,0:T(8,128)(2,1)S(1)}, bf16[216,256]{1,0:T(8,128)(2,1)S(1)}, u32[]{:S(2)}, u32[]{:S(2)}) collective-permute-start(bf16[216,256]{1,0:T(8,128)(2,1)S(1)} %collective-permute-done.3.b_ref), channel_id=1, source_target_pairs={{0,1},{1,0},{2,3},{3,2},{4,5},{5,4},{6,7},{7,6},{8,9},{9,8},{10,11... | collective-permute-start | bytes 331784 | tf_op jit(solution)/shard_map/ppermute | solution.py:212
  66.9 2.0 %collective-permute-done.7.w2_ref = bf16[8,96,256]{2,1,0:T(8,128)(2,1)S(1)} collective-permute-done((bf16[8,96,256]{2,1,0:T(8,128)(2,1)S(1)}, bf16[8,96,256]{2,1,0:T(8,128)(2,1)S(1)}, u32[]{:S(2)}, u32[]{:S(2)}) %collective-permute-start.7) | collective-permute-done | bytes 393248 | tf_op jit(solution)/shard_map/ppermute | solution.py:212
  68.9 1.6 inputs.1
  70.4 3.5 %all-to-all-start.1 = ((f32[8,96,216]{2,1,0:T(8,128)}), f32[8,96,216]{2,1,0:T(8,128)S(1)}, u32[]{:S(2)}, u32[]{:S(2)}) async-start(f32[8,96,216]{2,1,0:T(8,128)} %inputs.1), calls=%async_computation.1 | async-start | bytes 1572864 | tf_op jit(solution)/shard_map/all_to_all | solution.py:289
  74.8 20.8 %all-to-all-done.1.parts_ref = f32[8,96,216]{2,1,0:T(8,128)S(1)} async-done(((f32[8,96,216]{2,1,0:T(8,128)}), f32[8,96,216]{2,1,0:T(8,128)S(1)}, u32[]{:S(2)}, u32[]{:S(2)}) %all-to-all-start.1) | async-done | bytes 663584 | tf_op jit(solution)/shard_map/all_to_all | solution.py:289
  95.8 15.7 %all_to_all.21.g_ref = bf16[8,96,216]{2,1,0:T(8,128)(2,1)S(1)} all-to-all(bf16[8,96,216]{2,1,0:T(8,128)(2,1)S(1)} %get-tuple-element.13), channel_id=1, replica_groups=mesh['ylo'=2,'x'=4,'yhi'=2,'z'=8,'core'=2] {'z'}, dimensions={0} | all-to-all | bytes 663552 | tf_op jit(solution)/shard_map/all_to_all | solution.py:296
  111.4 1.4 grads.1
  112.8 3.3 %collective-permute-start.9 = (f32[2,216,256]{2,1,0:T(8,128)S(1)}, f32[2,216,256]{2,1,0:T(8,128)S(1)}, u32[]{:S(2)}, u32[]{:S(2)}) collective-permute-start(f32[2,216,256]{2,1,0:T(8,128)S(1)} %get-tuple-element.15), channel_id=1, source_target_pairs={{0,1},{1,0},{2,3},{3,2},{4,5},{5,4},{6,7},{7,6},{8,9},{9,8},{10,11... | collective-permute-start | bytes 1327112 | tf_op jit(solution)/shard_map/ppermute | solution.py:212
  116.1 1.4 collective-permute-done.9
  117.6 3.0 %collective-permute-start.10 = (bf16[216,256]{1,0:T(8,128)(2,1)S(1)}, bf16[216,256]{1,0:T(8,128)(2,1)S(1)}, u32[]{:S(2)}, u32[]{:S(2)}) collective-permute-start(bf16[216,256]{1,0:T(8,128)(2,1)S(1)} %fusion), channel_id=1, source_target_pairs={{0,16},{16,0},{1,17},{17,1},{2,18},{18,2},{3,19},{19,3},{4,20},{20... | collective-permute-start | bytes 331784 | tf_op jit(solution)/shard_map/ppermute | solution.py:212
  120.6 2.8 %collective-permute-done.10.their_ref = bf16[216,256]{1,0:T(8,128)(2,1)S(1)} collective-permute-done((bf16[216,256]{1,0:T(8,128)(2,1)S(1)}, bf16[216,256]{1,0:T(8,128)(2,1)S(1)}, u32[]{:S(2)}, u32[]{:S(2)}) %collective-permute-start.10) | collective-permute-done | bytes 110624 | tf_op jit(solution)/shard_map/ppermute | solution.py:212
  123.5 4.7 %backward.1 = f32[40,256]{1,0:T(8,128)S(1)} custom-call(s32[1,216]{1,0:T(1,128)S(1)} %bitcast.50, s32[1,216]{1,0:T(1,128)S(1)} %bitcast.52, bf16[8,80,256]{2,1,0:T(8,128)(2,1)S(1)} %slice.58.a_ref, bf16[8,80,256]{2,1,0:T(8,128)(2,1)S(1)} %collective-permute-done.b_ref, bf16[8,80,256]{2,1,0:T(8,128)(2,1)S(1)} %collective-permute-done.1.c_ref, ...), custom_call_target="tpu_custom_call" | custom-call | tf_op jit(solution)/shard_map/backward/pallas_call | solution.py:306
  128.3 14.1 %all_to_all.22 = f32[8,40,256]{2,1,0:T(8,128)S(1)} all-to-all(f32[8,40,256]{2,1,0:T(8,128)S(1)} %broadcast_in_dim.68), channel_id=1, replica_groups=mesh['ylo'=2,'x'=4,'yhi'=2,'z'=8,'core'=2] {'z'}, dimensions={0} | all-to-all | bytes 655360 | tf_op jit(solution)/shard_map/all_to_all | solution.py:322
  142.4 3.4 %collective-permute-start.11 = (f32[40,256]{1,0:T(8,128)S(1)}, f32[40,256]{1,0:T(8,128)S(1)}, u32[]{:S(2)}, u32[]{:S(2)}) collective-permute-start(f32[40,256]{1,0:T(8,128)S(1)} %pad_maximum_fusion.1), channel_id=1, source_target_pairs={{0,64},{32,96},{64,0},{96,32},{1,65},{33,97},{65,1},{97,33},{2,66}... | collective-permute-start | bytes 122888 | tf_op jit(solution)/shard_map/ppermute | solution.py:212
  146.7 1.8 %collective-permute-start.13 = (f32[40,256]{1,0:T(8,128)S(1)}, f32[40,256]{1,0:T(8,128)S(1)}, u32[]{:S(2)}, u32[]{:S(2)}) collective-permute-start(f32[40,256]{1,0:T(8,128)S(1)} %pad_maximum_fusion.1), channel_id=1, source_target_pairs={{0,96},{32,0},{64,32},{96,64},{1,97},{33,1},{65,33},{97,65},{2,98}... | collective-permute-start | bytes 122888 | tf_op jit(solution)/shard_map/ppermute | solution.py:212
  148.5 1.8 %collective-permute-done.12 = f32[40,256]{1,0:T(8,128)S(1)} collective-permute-done((f32[40,256]{1,0:T(8,128)S(1)}, f32[40,256]{1,0:T(8,128)S(1)}, u32[]{:S(2)}, u32[]{:S(2)}) %collective-permute-start.12) | collective-permute-done | bytes 40992 | tf_op jit(solution)/shard_map/ppermute | solution.py:212
  150.4 1.3 collective-permute-start.14
  151.7 1.8 %collective-permute-done.14 = f32[40,256]{1,0:T(8,128)S(1)} collective-permute-done((f32[40,256]{1,0:T(8,128)S(1)}, f32[40,256]{1,0:T(8,128)S(1)}, u32[]{:S(2)}, u32[]{:S(2)}) %collective-permute-start.14) | collective-permute-done | bytes 40992 | tf_op jit(solution)/shard_map/ppermute | solution.py:212
  154.9 4.5 %collective-permute-start.15 = (f32[34,256]{1,0:T(8,128)S(1)}, f32[34,256]{1,0:T(8,128)S(1)}, u32[]{:S(2)}, u32[]{:S(2)}) collective-permute-start(f32[34,256]{1,0:T(8,128)S(1)} %maximum_maximum_fusion), channel_id=1, source_target_pairs={{0,1},{1,0},{2,3},{3,2},{4,5},{5,4},{6,7},{7,6},{8,9},{9,8},{10,11... | collective-permute-start | bytes 104456 | tf_op jit(solution)/shard_map/ppermute | solution.py:212
  160.3 3.0 %collective-permute-start.16 = (f32[34,256]{1,0:T(8,128)S(1)}, f32[34,256]{1,0:T(8,128)S(1)}, u32[]{:S(2)}, u32[]{:S(2)}) collective-permute-start(f32[34,256]{1,0:T(8,128)S(1)} %fusion.9), channel_id=1, source_target_pairs={{0,16},{16,0},{1,17},{17,1},{2,18},{18,2},{3,19},{19,3},{4,20},{20... | collective-permute-start | bytes 104456 | tf_op jit(solution)/shard_map/ppermute | solution.py:212
  163.3 1.4 collective-permute-done.16
  (94 shorter events, 12.5 us)
Async XLA Ops:
  6.3 46.1 %copy-start = (bf16[8192,256]{1,0:T(8,128)(2,1)S(1)}, bf16[8192,256]{1,0:T(8,128)(2,1)}, u32[]{:S(2)}) copy-start(bf16[8192,256]{1,0:T(8,128)(2,1)} %param.18) | copy-start | bytes 12582916
  6.4 46.0 %copy-start.15 = (s32[2,27,256]{2,0,1:T(2,128)S(1)}, s32[2,27,256]{2,0,1:T(2,128)}, u32[]{:S(2)}) copy-start(s32[2,27,256]{2,0,1:T(2,128)} %param.26) | copy-start | bytes 165892
  6.4 46.0 %copy-start.6 = (s32[27,256]{1,0:T(8,128)S(1)}, s32[27,256]{1,0:T(8,128)}, u32[]{:S(2)}) copy-start(s32[27,256]{1,0:T(8,128)} %status_ref.3) | copy-start | bytes 82948
  6.4 46.0 %copy-start.7 = (f32[256]{0:T(256)S(1)}, f32[256]{0:T(256)}, u32[]{:S(2)}) copy-start(f32[256]{0:T(256)} %param.27) | copy-start | bytes 3076
  6.4 46.0 %copy-start.8 = (s32[216]{0:T(256)S(1)}, s32[216]{0:T(256)}, u32[]{:S(2)}) copy-start(s32[216]{0:T(256)} %param.15) | copy-start | bytes 2596
  6.4 46.0 %copy-start.9 = (s32[216]{0:T(256)S(1)}, s32[216]{0:T(256)}, u32[]{:S(2)}) copy-start(s32[216]{0:T(256)} %param.16) | copy-start | bytes 2596
  6.4 46.0 %copy-start.11 = (f32[256]{0:T(256)S(1)}, f32[256]{0:T(256)}, u32[]{:S(2)}) copy-start(f32[256]{0:T(256)} %param.19) | copy-start | bytes 3076
  6.4 46.0 %copy-start.13 = (f32[256]{0:T(256)S(1)}, f32[256]{0:T(256)}, u32[]{:S(2)}) copy-start(f32[256]{0:T(256)} %param.24) | copy-start | bytes 3076
  35.7 8.3 %collective-permute-start = (bf16[8,80,256]{2,1,0:T(8,128)(2,1)S(1)}, bf16[8,80,256]{2,1,0:T(8,128)(2,1)S(1)}, u32[]{:S(2)}, u32[]{:S(2)}) collective-permute-start(bf16[8,80,256]{2,1,0:T(8,128)(2,1)S(1)} %slice.58.a_ref), channel_id=1, source_target_pairs={{0,16},{16,0},{1,17},{17,1},{2,18},{18,2},{3,19},{19,3},{4,20},{20... | collective-permute-start | bytes 983048 | tf_op jit(solution)/shard_map/ppermute | solution.py:212
  38.7 13.7 %collective-permute-start.1 = (bf16[8,80,256]{2,1,0:T(8,128)(2,1)S(1)}, bf16[8,80,256]{2,1,0:T(8,128)(2,1)S(1)}, u32[]{:S(2)}, u32[]{:S(2)}) collective-permute-start(bf16[8,80,256]{2,1,0:T(8,128)(2,1)S(1)} %slice.58.a_ref), channel_id=1, source_target_pairs={{0,1},{1,0},{2,3},{3,2},{4,5},{5,4},{6,7},{7,6},{8,9},{9,8},{10,11... | collective-permute-start | bytes 983048 | tf_op jit(solution)/shard_map/ppermute | solution.py:212
  43.9 8.4 %collective-permute-start.2 = (bf16[8,80,256]{2,1,0:T(8,128)(2,1)S(1)}, bf16[8,80,256]{2,1,0:T(8,128)(2,1)S(1)}, u32[]{:S(2)}, u32[]{:S(2)}) collective-permute-start(bf16[8,80,256]{2,1,0:T(8,128)(2,1)S(1)} %collective-permute-done.b_ref), channel_id=1, source_target_pairs={{0,1},{1,0},{2,3},{3,2},{4,5},{5,4},{6,7},{7,6},{8,9},{9,8},{10,11... | collective-permute-start | bytes 983048 | tf_op jit(solution)/shard_map/ppermute | solution.py:212
  47.4 19.5 %collective-permute-start.6 = (bf16[8,96,256]{2,1,0:T(8,128)(2,1)S(1)}, bf16[8,96,256]{2,1,0:T(8,128)(2,1)S(1)}, u32[]{:S(2)}, u32[]{:S(2)}) collective-permute-start(bf16[8,96,256]{2,1,0:T(8,128)(2,1)S(1)} %slice.59.w0_ref), channel_id=1, source_target_pairs={{0,32},{32,64},{64,96},{96,0},{1,33},{33,65},{65,97},{97,1},{2,34}... | collective-permute-start | bytes 1179656 | tf_op jit(solution)/shard_map/ppermute | solution.py:212
  48.7 20.2 %collective-permute-start.7 = (bf16[8,96,256]{2,1,0:T(8,128)(2,1)S(1)}, bf16[8,96,256]{2,1,0:T(8,128)(2,1)S(1)}, u32[]{:S(2)}, u32[]{:S(2)}) collective-permute-start(bf16[8,96,256]{2,1,0:T(8,128)(2,1)S(1)} %slice.59.w0_ref), channel_id=1, source_target_pairs={{0,64},{32,96},{64,0},{96,32},{1,65},{33,97},{65,1},{97,33},{2,66}... | collective-permute-start | bytes 1179656 | tf_op jit(solution)/shard_map/ppermute | solution.py:212
  51.2 17.7 %collective-permute-start.8 = (bf16[8,96,256]{2,1,0:T(8,128)(2,1)S(1)}, bf16[8,96,256]{2,1,0:T(8,128)(2,1)S(1)}, u32[]{:S(2)}, u32[]{:S(2)}) collective-permute-start(bf16[8,96,256]{2,1,0:T(8,128)(2,1)S(1)} %slice.59.w0_ref), channel_id=1, source_target_pairs={{0,96},{32,0},{64,32},{96,64},{1,97},{33,1},{65,33},{97,65},{2,98}... | collective-permute-start | bytes 1179656 | tf_op jit(solution)/shard_map/ppermute | solution.py:212
  59.8 14.2 %copy-start.19 = (f32[96]{0:T(128)S(1)}, f32[96]{0:T(128)}, u32[]{:S(2)}) copy-start(f32[96]{0:T(128)} %param.28) | copy-start | bytes 1156
  59.8 5.4 %collective-permute-start.3 = (bf16[216,256]{1,0:T(8,128)(2,1)S(1)}, bf16[216,256]{1,0:T(8,128)(2,1)S(1)}, u32[]{:S(2)}, u32[]{:S(2)}) collective-permute-start(bf16[216,256]{1,0:T(8,128)(2,1)S(1)} %get-tuple-element.11.a_ref), channel_id=1, source_target_pairs={{0,16},{16,0},{1,17},{17,1},{2,18},{18,2},{3,19},{19,3},{4,20},{20... | collective-permute-start | bytes 331784 | tf_op jit(solution)/shard_map/ppermute | solution.py:212
  62.7 6.2 %collective-permute-start.4 = (bf16[216,256]{1,0:T(8,128)(2,1)S(1)}, bf16[216,256]{1,0:T(8,128)(2,1)S(1)}, u32[]{:S(2)}, u32[]{:S(2)}) collective-permute-start(bf16[216,256]{1,0:T(8,128)(2,1)S(1)} %get-tuple-element.11.a_ref), channel_id=1, source_target_pairs={{0,1},{1,0},{2,3},{3,2},{4,5},{5,4},{6,7},{7,6},{8,9},{9,8},{10,11... | collective-permute-start | bytes 331784 | tf_op jit(solution)/shard_map/ppermute | solution.py:212
  65.2 3.7 %collective-permute-start.5 = (bf16[216,256]{1,0:T(8,128)(2,1)S(1)}, bf16[216,256]{1,0:T(8,128)(2,1)S(1)}, u32[]{:S(2)}, u32[]{:S(2)}) collective-permute-start(bf16[216,256]{1,0:T(8,128)(2,1)S(1)} %collective-permute-done.3.b_ref), channel_id=1, source_target_pairs={{0,1},{1,0},{2,3},{3,2},{4,5},{5,4},{6,7},{7,6},{8,9},{9,8},{10,11... | collective-permute-start | bytes 331784 | tf_op jit(solution)/shard_map/ppermute | solution.py:212
  70.4 25.2 %all-to-all-start.1 = ((f32[8,96,216]{2,1,0:T(8,128)}), f32[8,96,216]{2,1,0:T(8,128)S(1)}, u32[]{:S(2)}, u32[]{:S(2)}) async-start(f32[8,96,216]{2,1,0:T(8,128)} %inputs.1), calls=%async_computation.1 | async-start | bytes 1572864 | tf_op jit(solution)/shard_map/all_to_all | solution.py:289
  95.8 27.7 %copy-start.1 = (bf16[8192,256]{1,0:T(8,128)(2,1)S(1)}, bf16[8192,256]{1,0:T(8,128)(2,1)}, u32[]{:S(2)}) copy-start(bf16[8192,256]{1,0:T(8,128)(2,1)} %param.18) | copy-start | bytes 12582916
  111.4 12.1 %copy-start.10 = (s32[216]{0:T(256)S(1)}, s32[216]{0:T(256)}, u32[]{:S(2)}) copy-start(s32[216]{0:T(256)} %param.16) | copy-start | bytes 2596
  111.4 12.1 %copy-start.12 = (f32[256]{0:T(256)S(1)}, f32[256]{0:T(256)}, u32[]{:S(2)}) copy-start(f32[256]{0:T(256)} %param.19) | copy-start | bytes 3076
  111.4 12.1 %copy-start.14 = (f32[256]{0:T(256)S(1)}, f32[256]{0:T(256)}, u32[]{:S(2)}) copy-start(f32[256]{0:T(256)} %param.24) | copy-start | bytes 3076
  112.8 4.7 %collective-permute-start.9 = (f32[2,216,256]{2,1,0:T(8,128)S(1)}, f32[2,216,256]{2,1,0:T(8,128)S(1)}, u32[]{:S(2)}, u32[]{:S(2)}) collective-permute-start(f32[2,216,256]{2,1,0:T(8,128)S(1)} %get-tuple-element.15), channel_id=1, source_target_pairs={{0,1},{1,0},{2,3},{3,2},{4,5},{5,4},{6,7},{7,6},{8,9},{9,8},{10,11... | collective-permute-start | bytes 1327112 | tf_op jit(solution)/shard_map/ppermute | solution.py:212
  117.6 5.9 %collective-permute-start.10 = (bf16[216,256]{1,0:T(8,128)(2,1)S(1)}, bf16[216,256]{1,0:T(8,128)(2,1)S(1)}, u32[]{:S(2)}, u32[]{:S(2)}) collective-permute-start(bf16[216,256]{1,0:T(8,128)(2,1)S(1)} %fusion), channel_id=1, source_target_pairs={{0,16},{16,0},{1,17},{17,1},{2,18},{18,2},{3,19},{19,3},{4,20},{20... | collective-permute-start | bytes 331784 | tf_op jit(solution)/shard_map/ppermute | solution.py:212
  128.2 39.6 %copy-start.18 = (f32[256]{0:T(256)S(1)}, f32[256]{0:T(256)}, u32[]{:S(2)}) copy-start(f32[256]{0:T(256)} %param.22) | copy-start | bytes 3076
  142.4 6.1 %collective-permute-start.11 = (f32[40,256]{1,0:T(8,128)S(1)}, f32[40,256]{1,0:T(8,128)S(1)}, u32[]{:S(2)}, u32[]{:S(2)}) collective-permute-start(f32[40,256]{1,0:T(8,128)S(1)} %pad_maximum_fusion.1), channel_id=1, source_target_pairs={{0,64},{32,96},{64,0},{96,32},{1,65},{33,97},{65,1},{97,33},{2,66}... | collective-permute-start | bytes 122888 | tf_op jit(solution)/shard_map/ppermute | solution.py:212
  145.8 4.5 %collective-permute-start.12 = (f32[40,256]{1,0:T(8,128)S(1)}, f32[40,256]{1,0:T(8,128)S(1)}, u32[]{:S(2)}, u32[]{:S(2)}) collective-permute-start(f32[40,256]{1,0:T(8,128)S(1)} %pad_maximum_fusion.1), channel_id=1, source_target_pairs={{0,32},{32,64},{64,96},{96,0},{1,33},{33,65},{65,97},{97,1},{2,34}... | collective-permute-start | bytes 122888 | tf_op jit(solution)/shard_map/ppermute | solution.py:212
  146.7 3.7 %collective-permute-start.13 = (f32[40,256]{1,0:T(8,128)S(1)}, f32[40,256]{1,0:T(8,128)S(1)}, u32[]{:S(2)}, u32[]{:S(2)}) collective-permute-start(f32[40,256]{1,0:T(8,128)S(1)} %pad_maximum_fusion.1), channel_id=1, source_target_pairs={{0,96},{32,0},{64,32},{96,64},{1,97},{33,1},{65,33},{97,65},{2,98}... | collective-permute-start | bytes 122888 | tf_op jit(solution)/shard_map/ppermute | solution.py:212
  150.4 3.1 %collective-permute-start.14 = (f32[40,256]{1,0:T(8,128)S(1)}, f32[40,256]{1,0:T(8,128)S(1)}, u32[]{:S(2)}, u32[]{:S(2)}) collective-permute-start(f32[40,256]{1,0:T(8,128)S(1)} %add_add_fusion), channel_id=1, source_target_pairs={{0,128},{128,0},{1,129},{129,1},{2,130},{130,2},{3,131},{131,3},{4... | collective-permute-start | bytes 122888 | tf_op jit(solution)/shard_map/ppermute | solution.py:212
  154.9 5.4 %collective-permute-start.15 = (f32[34,256]{1,0:T(8,128)S(1)}, f32[34,256]{1,0:T(8,128)S(1)}, u32[]{:S(2)}, u32[]{:S(2)}) collective-permute-start(f32[34,256]{1,0:T(8,128)S(1)} %maximum_maximum_fusion), channel_id=1, source_target_pairs={{0,1},{1,0},{2,3},{3,2},{4,5},{5,4},{6,7},{7,6},{8,9},{9,8},{10,11... | collective-permute-start | bytes 104456 | tf_op jit(solution)/shard_map/ppermute | solution.py:212
  160.3 4.4 %collective-permute-start.16 = (f32[34,256]{1,0:T(8,128)S(1)}, f32[34,256]{1,0:T(8,128)S(1)}, u32[]{:S(2)}, u32[]{:S(2)}) collective-permute-start(f32[34,256]{1,0:T(8,128)S(1)} %fusion.9), channel_id=1, source_target_pairs={{0,16},{16,0},{1,17},{17,1},{2,18},{18,2},{3,19},{19,3},{4,20},{20... | collective-permute-start | bytes 104456 | tf_op jit(solution)/shard_map/ppermute | solution.py:212
  (6 other events, 33.5 us)

commit v2 on v1

v2 whole, which is shorter than its diff:
```python
import functools

import jax
import jax.numpy as jnp
from jax import lax
from jax.experimental import pallas as pl
from jax.experimental.pallas import tpu as pltpu
from jax.sharding import Mesh
from jax.sharding import PartitionSpec as P

HIDDEN_SIZE = 8192
CLASSES = 10
GROUP = 8
LANES = 256

grid_step = 0.0625
step_rate = 0.25
epsilon = 1e-06

ROWS_UP, ROWS_LOW, ROWS_CLASS, ROWS_ALL = 0, 32, 64, 80

DOM = ("ylo", "x")
NEU = ("yhi", "z", "core")
F32, BF16 = jnp.float32, jnp.bfloat16


def spread(per_domain):
    count, width = per_domain.shape
    return jnp.broadcast_to(per_domain[:, None, :], (count, GROUP, width)).reshape(
        count * GROUP, width
    )


def contract(left, right, left_dim, right_dim):
    return lax.dot_general(
        left, right, (((left_dim,), (right_dim,)), ((), ())), preferred_element_type=F32
    )


def selector(label, offset):
    second = label + offset
    second = jnp.where(second >= CLASSES, second - CLASSES, second)
    classes = lax.broadcasted_iota(jnp.int32, (16, label.shape[1]), 0)
    picked = jnp.where(classes == label, 1.0, 0.0) - jnp.where(classes == second, 1.0, 0.0)
    return picked.astype(BF16)


def decode(block, domains):
    up = block[ROWS_UP : ROWS_UP + 32].astype(F32)[:domains]
    low = block[ROWS_LOW : ROWS_LOW + 32].astype(F32)[:domains]
    tail = block[ROWS_CLASS:ROWS_ALL].astype(F32)
    slope = tail[10:11] + tail[11:12] + tail[12:13]
    ratio = up / (up + low)
    unsplit = (up > 0.0) & (low > 0.0)
    return up, low, ratio, slope, unsplit


def relax_rows(coeffs, status, low, up, slopes):
    ratio = up / (up + low)
    cept = ratio * (low * grid_step)
    unsplit = status == 2
    fixed = jnp.where(status == 1, 1.0, 0.0)
    at_pos = spread(jnp.where(unsplit, jnp.broadcast_to(slopes, ratio.shape), fixed))
    at_neg = spread(jnp.where(unsplit, ratio, fixed))
    off_neg = spread(jnp.where(unsplit, cept, 0.0))
    on_pos = spread(jnp.where(unsplit, 1.0, 0.0))
    positive = coeffs >= 0.0
    factor = jnp.where(positive, at_pos, at_neg)
    offset = jnp.where(positive, 0.0, off_neg)
    chosen = jnp.where(positive, on_pos, 0.0)
    return factor, offset, chosen


def prep_kernel(status_ref, bounds_ref, class_ref, slopes_ref, weight_ref, out_ref, held, sems):
    x = lax.axis_index("x")
    domains = status_ref.shape[0]
    count = held.shape[0]
    copies = [
        pltpu.make_async_copy(weight_ref.at[x // 2, k, x % 2], held.at[k], sems.at[k]) for k in range(count)
    ]
    for copy in copies:
        copy.start()
    status = status_ref[...]
    active, unsplit = status == 1, status == 2
    pad = jnp.ones((32 - domains, LANES), F32)
    up = jnp.where(unsplit, bounds_ref[1], jnp.where(active, 1, 0)).astype(F32)
    low = jnp.where(unsplit, bounds_ref[0], jnp.where(active, 0, 1)).astype(F32)
    slopes = slopes_ref[...]
    high = lax.reduce_precision(slopes, 8, 7)
    middle = lax.reduce_precision(slopes - high, 8, 7)
    last = (slopes - high) - middle
    tail = jnp.concatenate([class_ref[...].astype(F32), high, middle, last, jnp.zeros((3, LANES), F32)], axis=0)
    info = jnp.concatenate([up, pad, low, pad, tail], axis=0).astype(BF16)
    for k in range(count):
        out_ref[k, 0:ROWS_ALL] = info
    for k, copy in enumerate(copies):
        copy.wait()
        out_ref[k, ROWS_ALL : ROWS_ALL + held.shape[2]] = held[k].astype(F32).T.astype(BF16)


def forward_half(
    last, label_ref, offset_ref, own_ref, other_ref, weight_ref, total, keep_terms,
):
    step = pl.program_id(0)
    core, z = lax.axis_index("core"), lax.axis_index("z")
    domains = label_ref.shape[1] // GROUP
    select = selector(label_ref[...], offset_ref[...])
    acc = total[...]
    for k in range(own_ref.shape[0]):
        for ref, side in ((own_ref, core), (other_ref, 1 - core)):
            block = ref[k]
            up, low, ratio, slope, unsplit = decode(block, domains)
            coeffs = contract(select, block[ROWS_CLASS:ROWS_ALL], 0, 0)
            at_pos = jnp.where(unsplit, jnp.broadcast_to(slope, ratio.shape), ratio)
            factor = jnp.where(coeffs >= 0.0, spread(at_pos), spread(ratio))
            sent = (coeffs * factor).astype(BF16)
            if keep_terms is not None and ref is own_ref:

                @pl.when(step * own_ref.shape[0] + k == z)
                def _():
                    keep_terms(coeffs, sent, ratio, low, unsplit)

            acc = acc + jnp.dot(sent, weight_ref[0, k, side], preferred_element_type=F32)
    total[...] = acc


def near_kernel(label_ref, offset_ref, own_ref, other_ref, weight_ref, deep_bias_ref, total_ref, terms_ref):
    @pl.when(pl.program_id(0) == 0)
    def _():
        total_ref[...] = jnp.zeros_like(total_ref)

    def keep_terms(coeffs, sent, ratio, low, unsplit):
        cept = jnp.where(unsplit, ratio * (low * grid_step), 0.0)
        terms_ref[...] = sent.astype(F32) * deep_bias_ref[...] + jnp.where(
            coeffs >= 0.0, 0.0, coeffs * spread(cept)
        )

    forward_half(False, label_ref, offset_ref, own_ref, other_ref, weight_ref, total_ref, keep_terms)


def far_kernel(
    label_ref, offset_ref, own_ref, other_ref, weight_ref, so_far_ref, terms_ref,
    status_ref, bounds_ref, slopes_ref, bias_ref, sent_ref, coeffs_ref, const_ref, total,
):
    @pl.when(pl.program_id(0) == 0)
    def _():
        total[...] = so_far_ref[...]

    forward_half(True, label_ref, offset_ref, own_ref, other_ref, weight_ref, total, None)

    @pl.when(pl.program_id(0) == pl.num_programs(0) - 1)
    def _():
        coeffs = total[...]
        factor, offset, _ = relax_rows(
            coeffs, status_ref[...], bounds_ref[0].astype(F32), bounds_ref[1].astype(F32), slopes_ref[...]
        )
        sent = (coeffs * factor).astype(BF16)
        sent_ref[...] = sent
        coeffs_ref[...] = coeffs
        const_ref[...] = row_sums(terms_ref[...] + sent.astype(F32) * bias_ref[...] + coeffs * offset)


def row_sums(values):
    return lax.dot_general(
        jnp.ones((8, values.shape[1]), F32), values, (((1,), (1,)), ((), ())),
        precision=lax.Precision.HIGHEST, preferred_element_type=F32,
    )


def hold(held, refs, own):
    for place, ref in enumerate(refs):
        held[own ^ ((place % 2) * 2 + place // 2)] = ref[...]


def input_kernel(a_ref, b_ref, c_ref, d_ref, weight_ref, out_ref, held):
    own = lax.axis_index("yhi") * 2 + lax.axis_index("core")
    hold(held, (a_ref, b_ref, c_ref, d_ref), own)
    _, zs, feats, _ = weight_ref.shape
    acc = None
    for q in range(4):
        part = contract(weight_ref[q].reshape(zs * feats, LANES), held[q], 1, 1)
        acc = part if acc is None else acc + part
    out_ref[...] = acc.reshape(zs, feats, acc.shape[1]).astype(BF16)


def column(row):
    count = row.shape[1]
    down = lax.broadcasted_iota(jnp.int32, (count, count), 0)
    across = lax.broadcasted_iota(jnp.int32, (count, count), 1)
    return jnp.sum(jnp.where(down == across, row, 0.0), axis=1, keepdims=True)


def box_kernel(parts_ref, center_ref, radius_ref, const_ref, grads_ref, bound_ref):
    coeffs = parts_ref[0].astype(F32)
    for k in range(1, parts_ref.shape[0]):
        coeffs = coeffs + parts_ref[k].astype(F32)
    center, radius = column(center_ref[...]), column(radius_ref[...])
    wide = center - jnp.where(coeffs > 0.0, radius, jnp.where(coeffs < 0.0, -radius, 0.0))
    grads = wide.astype(BF16)
    for k in range(grads_ref.shape[0]):
        grads_ref[k] = grads
    rest = coeffs * (wide - grads.astype(F32))
    bound_ref[...] = jnp.sum(rest, axis=0, keepdims=True) + const_ref[0:1]


def grads_kernel(
    g_ref, weight_ref, a_ref, b_ref, c_ref, d_ref, so_far_ref, near_ref, far_ref, bound_ref, held
):
    own = lax.axis_index("yhi") * 2 + lax.axis_index("core")
    hold(held, (a_ref, b_ref, c_ref, d_ref), own)
    zs, feats, rows = g_ref.shape
    grads = g_ref[...].reshape(zs * feats, rows)
    terms = None
    for q in range(4):
        part = contract(grads, weight_ref[q].reshape(zs * feats, LANES), 0, 0)
        term = part * held[q].astype(F32)
        terms = term if terms is None else terms + term
        place = own ^ q

        @pl.when(place % 2 == 0)
        def _():
            near_ref[place // 2] = part

        @pl.when(place % 2 == 1)
        def _():
            far_ref[place // 2] = part

    bound_ref[...] = row_sums(terms) + so_far_ref[...]


def backward_kernel(
    label_ref, offset_ref, a_ref, b_ref, c_ref, d_ref, weight_ref, deep_bias_ref,
    status_ref, bounds_ref, slopes_ref, bias_ref, coeffs_ref, near_ref, got_ref, their_ref, bound_ref,
    mine_ref, other_ref, back,
):
    step = pl.program_id(0)
    yhi, z, core = (lax.axis_index(n) for n in NEU)
    domains = status_ref.shape[0]
    select = selector(label_ref[...], offset_ref[...])

    @pl.when(step == 0)
    def _():
        coeffs = coeffs_ref[...]
        grads = near_ref[0] + got_ref[0] + their_ref[...].astype(F32) + bias_ref[...]
        factor, offset, chosen = relax_rows(
            coeffs, status_ref[...], bounds_ref[0].astype(F32), bounds_ref[1].astype(F32), slopes_ref[...]
        )
        back[...] = (grads * factor + offset).astype(BF16)
        mine_ref[16:24] = jnp.zeros((8, LANES), F32)
        mine_ref[16:17] = jnp.sum(grads * coeffs * chosen, axis=0, keepdims=True)
        mine_ref[17:18, 0 : bound_ref.shape[1]] = bound_ref[0:1]

    zs = a_ref.shape[0]
    for k in range(zs):
        for place, ref in enumerate((a_ref, b_ref, c_ref, d_ref)):
            y = yhi if place % 2 == 0 else 1 - yhi
            c = core if place // 2 == 0 else 1 - core
            block = ref[k]
            _, _, _, _, unsplit = decode(block, domains)
            coeffs = contract(select, block[ROWS_CLASS:ROWS_ALL], 0, 0)
            kept = jnp.maximum(coeffs, 0.0) * spread(jnp.where(unsplit, 1.0, 0.0))
            grads = contract(back[...], weight_ref[y, k, c], 1, 1)
            if place == 0:
                grads = grads + jnp.where(step * zs + k == z, 1.0, 0.0) * deep_bias_ref[...]
            out = mine_ref if place // 2 == 0 else other_ref
            out[pl.ds(y * 8 + step * zs + k, 1)] = jnp.sum(grads * kept, axis=0, keepdims=True)


def send_z_kernel(mine_ref, got_ref, out_ref):
    deep = mine_ref[0:16] + got_ref[...]
    rest = mine_ref[16:24]
    for k in range(out_ref.shape[0]):
        out_ref[k, 0:16] = deep
        out_ref[k, 16:24] = rest


def send_dom_kernel(got_ref, out_ref, bound_ref):
    total = got_ref[0]
    for k in range(1, got_ref.shape[0]):
        total = total + got_ref[k]
    bound_ref[...] = total[17:18]
    first = jnp.concatenate([got_ref[k, 16:17] for k in range(got_ref.shape[0])], axis=0)
    for k in range(out_ref.shape[0]):
        out_ref[k, 0:16] = total[0:16]
        out_ref[k, 16:24] = first


def send_y_kernel(got_ref, bound_ref, out_ref, first_ref):
    total = got_ref[0]
    for k in range(1, got_ref.shape[0]):
        total = total + got_ref[k]
    first = total[16:24]
    first_ref[...] = first
    out_ref[0:16] = total[0:16]
    out_ref[16:24] = jnp.zeros((8, LANES), F32)
    out_ref[16:17] = bound_ref[...]
    out_ref[17:18] = jnp.broadcast_to(jnp.sum(first * first, keepdims=True), (1, LANES))


def send_core_kernel(mine_ref, got_ref, out_ref, deep_ref):
    deep = mine_ref[0:16] + got_ref[0:16]
    deep_ref[...] = deep
    out_ref[...] = mine_ref[16:24] + got_ref[16:24]
    out_ref[2:3] = jnp.broadcast_to(jnp.sum(deep * deep, keepdims=True), (1, LANES))


def finish_kernel(mine_ref, got_ref, deep_ref, first_ref, deep_slopes_ref, first_slopes_ref, bound_ref, first_out, deep_out):
    yhi, z = lax.axis_index("yhi"), lax.axis_index("z")
    total = mine_ref[...] + got_ref[...]
    bound_ref[...] = total[0:1, 0 : bound_ref.shape[1]]

    def advance(slopes, gradient, squares):
        root_mean = jnp.sqrt(squares / HIDDEN_SIZE + epsilon)
        return jnp.clip(slopes + step_rate * gradient / root_mean, 0.0, 1.0)

    first_out[...] = advance(first_slopes_ref[...], first_ref[pl.ds(z, 1)], total[1:2])
    deep_out[...] = advance(deep_slopes_ref[...], deep_ref[pl.ds(yhi * 8 + z, 1)], total[2:3])


def whole(shape):
    return pl.BlockSpec(shape, lambda s: (0,) * len(shape))


def shape(dims, kind=F32):
    return jax.ShapeDtypeStruct(dims, kind)


def shifted(value, axis, size, by):
    return lax.ppermute(value, axis, [(i, (i + by) % size) for i in range(size)])


def on_device(
    spec_label, spec_offset, class_rows, deep_weight, deep_bias, deep_status, deep_bounds,
    deep_slopes, first_weight, first_bias, first_status, first_bounds, first_slopes,
    box_center, box_radius,
):
    rows = spec_label.shape[0]
    domains = deep_status.shape[0]
    feats = box_center.shape[0]
    params = pltpu.CompilerParams(vmem_limit_bytes=24 * 1024 * 1024)
    call = functools.partial(pl.pallas_call, compiler_params=params)
    vmem = pl.BlockSpec(memory_space=pltpu.VMEM)

    message = call(
        prep_kernel,
        in_specs=[vmem] * 4 + [pl.BlockSpec(memory_space=pl.ANY)],
        out_specs=vmem,
        out_shape=shape((8, ROWS_ALL + feats, LANES), BF16),
        scratch_shapes=[pltpu.VMEM((8, LANES, feats), BF16), pltpu.SemaphoreType.DMA((8,))],
        name="prep",
    )(deep_status, deep_bounds, class_rows, deep_slopes[None], first_weight.reshape(2, 8, 2, LANES, feats))
    message = lax.all_to_all(message, "z", 0, 0, tiled=True)
    info_a = message[:, :ROWS_ALL]
    info_b = shifted(info_a, "yhi", 2, 1)
    info_c = shifted(info_a, "core", 2, 1)
    info_d = shifted(info_b, "core", 2, 1)
    w_all = lax.all_gather(message[:, ROWS_ALL:], "x", axis=0)

    label, offset = spec_label[None], spec_offset[None]
    weight = deep_weight.reshape(2, 8, 2, LANES, LANES)
    depth = 2
    info_spec = pl.BlockSpec((depth, ROWS_ALL, LANES), lambda s: (s, 0, 0))
    label_specs = [whole((1, rows))] * 2
    layer_specs = [whole((domains, LANES)), whole((2, domains, LANES)), whole((1, LANES)), whole((1, LANES))]
    layer = (first_status, first_bounds, first_slopes[None], first_bias[None])
    half_spec = lambda other: pl.BlockSpec(
        (1, depth, 2, LANES, LANES), lambda s: (lax.axis_index("yhi") ^ other, s, 0, 0, 0)
    )
    square = whole((rows, LANES))

    total, terms = call(
        near_kernel,
        grid=(8 // depth,),
        in_specs=label_specs + [info_spec] * 2 + [half_spec(0), whole((1, LANES))],
        out_specs=[square, square],
        out_shape=[shape((rows, LANES)), shape((rows, LANES))],
        name="forward_near",
    )(label, offset, info_a, info_c, weight, deep_bias[None])
    sent, coeffs, const = call(
        far_kernel,
        grid=(8 // depth,),
        in_specs=label_specs + [info_spec] * 2 + [half_spec(1), square, square] + layer_specs,
        out_specs=[square, square, whole((8, rows))],
        out_shape=[shape((rows, LANES), BF16), shape((rows, LANES)), shape((8, rows))],
        scratch_shapes=[pltpu.VMEM((rows, LANES), F32)],
        name="forward_far",
    )(label, offset, info_b, info_d, weight, total, terms, *layer)

    sent_b = shifted(sent, "yhi", 2, 1)
    sent_c = shifted(sent, "core", 2, 1)
    sent_d = shifted(sent_b, "core", 2, 1)
    sents = (sent, sent_b, sent_c, sent_d)
    held = [pltpu.VMEM((4, rows, LANES), BF16)]
    parts = call(
        input_kernel, out_shape=shape((8, feats, rows), BF16), scratch_shapes=held, name="inputs"
    )(*sents, w_all)
    parts = lax.all_to_all(parts, "z", 0, 0, tiled=True)
    grads, bound = call(
        box_kernel, out_shape=[shape((8, feats, rows), BF16), shape((1, rows))], name="box"
    )(parts, box_center[None], box_radius[None], const)
    grads = lax.all_to_all(grads, "z", 0, 0, tiled=True)
    near, far, bound = call(
        grads_kernel,
        out_shape=[shape((2, rows, LANES))] * 2 + [shape((8, rows))],
        scratch_shapes=held,
        name="grads",
    )(grads, w_all, *sents, bound)
    got = shifted(far, "core", 2, 1)
    their = shifted((near[1] + got[1]).astype(BF16), "yhi", 2, 1)

    first_of_two = pl.BlockSpec((1, rows, LANES), lambda s: (0, 0, 0))
    mine, other = call(
        backward_kernel,
        grid=(8 // depth,),
        in_specs=label_specs
        + [info_spec] * 4
        + [pl.BlockSpec((2, depth, 2, LANES, LANES), lambda s: (0, s, 0, 0, 0)), whole((1, LANES))]
        + layer_specs
        + [square, first_of_two, first_of_two, square, whole((8, rows))],
        out_specs=[whole((24, LANES)), whole((16, LANES))],
        out_shape=[shape((24, LANES)), shape((16, LANES))],
        scratch_shapes=[pltpu.VMEM((rows, LANES), BF16)],
        name="backward",
    )(label, offset, info_a, info_b, info_c, info_d, weight, deep_bias[None], *layer, coeffs, near, got, their, bound)

    to_all = shape((8, 24, LANES))
    to_z = call(send_z_kernel, out_shape=to_all, name="send_z")(mine, shifted(other, "core", 2, 1))
    got = lax.all_to_all(to_z, "z", 0, 0, tiled=True)
    to_dom, bound = call(send_dom_kernel, out_shape=[to_all, shape((1, LANES))], name="send_dom")(got)
    got = lax.all_to_all(to_dom, DOM, 0, 0, tiled=True)
    to_y, first = call(
        send_y_kernel, out_shape=[shape((24, LANES)), shape((8, LANES))], name="send_y"
    )(got, bound)
    to_core, deep = call(
        send_core_kernel, out_shape=[shape((8, LANES)), shape((16, LANES))], name="send_core"
    )(to_y, shifted(to_y, "yhi", 2, 1))
    bound, first_next, deep_next = call(
        finish_kernel, out_shape=[shape((1, rows)), shape((1, LANES)), shape((1, LANES))], name="finish"
    )(to_core, shifted(to_core, "core", 2, 1), deep, first, deep_slopes[None], first_slopes[None])
    return bound[0], first_next[0], deep_next[0]


def solution(mesh):
    fine = Mesh(mesh.devices.reshape(2, 4, 2, 8, 2), DOM + NEU)
    in_specs = (
        P(DOM), P(DOM), P(None, NEU), P(None, NEU), P(NEU), P(DOM, NEU), P(None, DOM, NEU), P(NEU),
        P(None, NEU), P(NEU), P(DOM, NEU), P(None, DOM, NEU), P(NEU), P(NEU), P(NEU),
    )
    out_specs = (P(DOM), P(NEU), P(NEU))
    return jax.shard_map(on_device, mesh=fine, in_specs=in_specs, out_specs=out_specs, check_vma=False)
```

time: 169 us -> 164 us (0.970)
  blocking collectives: 58.9 us -> 83.5 us
  waiting for transfers between devices: 36.7 us -> 13.9 us
  starting transfers between devices: 44.6 us -> 28.2 us
  between operations: 2.47 us -> 14.3 us
  other arithmetic: 2.87 us -> 0.03 us
    all_to_all x1 -> x3, blocking collectives: 14.1 us -> 40.4 us  [the longest x1 19.1 us: on_device(): parts = lax.all_to_all(parts, 'z', 0, 0, tiled=True)]
    all_to_all x1 -> x0, waiting for transfers between devices: 20.8 us -> none  [on_device(): parts = lax.all_to_all(parts, 'z', 0, 0, tiled=True)]
    ppermute x17 -> x11, starting transfers between devices: 41.1 us -> 28.2 us  [shifted(): lax.ppermute(value, axis, [(i, (i + by) % size) for i in range(size)])]
    unnamed x42 -> x37, local copies, waits for them, and re-layouts: 0.83 us -> 7.59 us
    all_to_all x1 -> x0, starting transfers between devices: 3.55 us -> none  [on_device(): parts = lax.all_to_all(parts, 'z', 0, 0, tiled=True)]
    reshape x1 -> x0, local copies, waits for them, and re-layouts: 2.86 us -> none  [on_device(): first_weight.reshape(2, 8, 2, LANES, feats).transpose(0, 2, 1, 3, 4)]
    ppermute x17 -> x11, waiting for transfers between devices: 15.9 us -> 13.9 us  [shifted(): lax.ppermute(value, axis, [(i, (i + by) % size) for i in range(size)])]
    pallas_call x5 -> x12, Pallas kernels: 14.4 us -> 15.1 us  [the longest x1 3.69 us: on_device(): call(backward_kernel, grid=(8 // depth,), in_specs=label_specs + [info_sp...]
  transfers between devices with their start and end apart: 18 -> 12, of which waited for: 10 -> 8; matrix products, arithmetic and copies ran while one was open for 1% -> 0% of each run, Pallas kernels for 4% -> 4%
where the time goes in v2:
time: 164 us
  blocking collectives  83.5 us (51%)
  starting transfers between devices  28.2 us (17%)
  Pallas kernels  15.1 us (9%)
  between operations  14.3 us (9%)
  waiting for transfers between devices  13.9 us (8%)
  local copies, waits for them, and re-layouts  8.38 us (5%)
    all_to_all x1, blocking collectives, on_device(): message = lax.all_to_all(message, 'z', 0, 0, tiled=True)  29.1 us
    ppermute x11, starting transfers between devices, shifted(): lax.ppermute(value, axis, [(i, (i + by) % size) for i in range(size)])  28.2 us
    all_to_all x1, blocking collectives, on_device(): parts = lax.all_to_all(parts, 'z', 0, 0, tiled=True)  19.1 us
    all_to_all x1, blocking collectives, on_device(): grads = lax.all_to_all(grads, 'z', 0, 0, tiled=True)  14.1 us
    ppermute x11, waiting for transfers between devices, shifted(): lax.ppermute(value, axis, [(i, (i + by) % size) for i in range(size)])  13.9 us
    all_to_all x1, blocking collectives, on_device(): got = lax.all_to_all(to_z, 'z', 0, 0, tiled=True)  12.6 us
    all_to_all x1, blocking collectives, on_device(): got = lax.all_to_all(to_dom, DOM, 0, 0, tiled=True)  8.75 us
    unnamed x37, local copies, waits for them, and re-layouts  7.59 us
  transfers between devices with their start and end apart: 12, of which 8 were waited for; matrix products, arithmetic and copies ran while one was open for 0% of the time, Pallas kernels for 4%

profile of v2, /device:TPU:1, one launch (start us, length us, event | category | flops | bytes accessed | tf_op | source)
XLA Modules:
  0.0 163.5 jit_solution(18060444851543581006)
XLA Ops:
  7.2 0.8 copy.23.bounds_ref
  8.1 3.1 %copy.22 = bf16[8192,96]{1,0:T(8,128)(2,1)S(1)} copy(bf16[8192,96]{0,1:T(8,128)(2,1)} %param.23) | data formatting | bytes 3145728 | tf_op args[8]
  11.2 1.6 prep.1
  12.8 29.1 %all_to_all.25 = bf16[8,176,256]{2,1,0:T(8,128)(2,1)S(1)} all-to-all(bf16[8,176,256]{2,1,0:T(8,128)(2,1)S(1)} %prep.1), channel_id=1, replica_groups=mesh['ylo'=2,'x'=4,'yhi'=2,'z'=8,'core'=2] {'z'}, dimensions={0} | all-to-all | bytes 1441792 | tf_op jit(solution)/shard_map/all_to_all | solution.py:352
  42.7 3.0 %collective-permute-start = (bf16[8,80,256]{2,1,0:T(8,128)(2,1)S(1)}, bf16[8,80,256]{2,1,0:T(8,128)(2,1)S(1)}, u32[]{:S(2)}, u32[]{:S(2)}) collective-permute-start(bf16[8,80,256]{2,1,0:T(8,128)(2,1)S(1)} %slice.16.own_ref.a_ref), channel_id=1, source_target_pairs={{0,16},{16,0},{1,17},{17,1},{2,18},{18,2},{3,19},{19,3},{4,20},{20... | collective-permute-start | bytes 983048 | tf_op jit(solution)/shard_map/ppermute | solution.py:329
  45.7 2.8 %collective-permute-start.1 = (bf16[8,80,256]{2,1,0:T(8,128)(2,1)S(1)}, bf16[8,80,256]{2,1,0:T(8,128)(2,1)S(1)}, u32[]{:S(2)}, u32[]{:S(2)}) collective-permute-start(bf16[8,80,256]{2,1,0:T(8,128)(2,1)S(1)} %slice.16.own_ref.a_ref), channel_id=1, source_target_pairs={{0,1},{1,0},{2,3},{3,2},{4,5},{5,4},{6,7},{7,6},{8,9},{9,8},{10,11... | collective-permute-start | bytes 983048 | tf_op jit(solution)/shard_map/ppermute | solution.py:329
  48.5 2.4 %collective-permute-done.own_ref.b_ref = bf16[8,80,256]{2,1,0:T(8,128)(2,1)S(1)} collective-permute-done((bf16[8,80,256]{2,1,0:T(8,128)(2,1)S(1)}, bf16[8,80,256]{2,1,0:T(8,128)(2,1)S(1)}, u32[]{:S(2)}, u32[]{:S(2)}) %collective-permute-start) | collective-permute-done | bytes 327712 | tf_op jit(solution)/shard_map/ppermute | solution.py:329
  51.0 3.5 %collective-permute-start.2 = (bf16[8,80,256]{2,1,0:T(8,128)(2,1)S(1)}, bf16[8,80,256]{2,1,0:T(8,128)(2,1)S(1)}, u32[]{:S(2)}, u32[]{:S(2)}) collective-permute-start(bf16[8,80,256]{2,1,0:T(8,128)(2,1)S(1)} %collective-permute-done.own_ref.b_ref), channel_id=1, source_target_pairs={{0,1},{1,0},{2,3},{3,2},{4,5},{5,4},{6,7},{7,6},{8,9},{9,8},{10,11... | collective-permute-start | bytes 983048 | tf_op jit(solution)/shard_map/ppermute | solution.py:329
  54.5 2.2 %copy-done = bf16[8192,256]{1,0:T(8,128)(2,1)S(1)} copy-done((bf16[8192,256]{1,0:T(8,128)(2,1)S(1)}, bf16[8192,256]{1,0:T(8,128)(2,1)}, u32[]{:S(2)}) %copy-start) | copy-done | bytes 4194328
  56.7 3.5 %forward_near.1 = (f32[216,256]{1,0:T(8,128)S(1)}, f32[216,256]{1,0:T(8,128)S(1)}) custom-call(s32[1,216]{1,0:T(1,128)S(1)} %bitcast.22, s32[1,216]{1,0:T(1,128)S(1)} %bitcast.25, bf16[8,80,256]{2,1,0:T(8,128)(2,1)S(1)} %slice.16.own_ref.a_ref, bf16[8,80,256]{2,1,0:T(8,128)(2,1)S(1)} %collective-permute-done.1.other_ref.c_ref, ...), custom_call_target="tpu_custom_call" | custom-call | tf_op jit(solution)/shard_map/forward_near/pallas_call | solution.py:371
  60.3 3.0 %forward_far.1 = (bf16[216,256]{1,0:T(8,128)(2,1)S(1)}, f32[216,256]{1,0:T(8,128)S(1)}, f32[8,216]{1,0:T(8,128)S(1)}) custom-call(s32[1,216]{1,0:T(1,128)S(1)} %bitcast.23, s32[1,216]{1,0:T(1,128)S(1)} %bitcast.26, bf16[8,80,256]{2,1,0:T(8,128)(2,1)S(1)} %collective-permute-done.own_ref.b_ref, ...), custom_call_target="tpu_custom_call" | custom-call | tf_op jit(solution)/shard_map/forward_far/pallas_call | solution.py:379
  63.2 2.9 %collective-permute-start.3 = (bf16[216,256]{1,0:T(8,128)(2,1)S(1)}, bf16[216,256]{1,0:T(8,128)(2,1)S(1)}, u32[]{:S(2)}, u32[]{:S(2)}) collective-permute-start(bf16[216,256]{1,0:T(8,128)(2,1)S(1)} %get-tuple-element.27.a_ref), channel_id=1, source_target_pairs={{0,16},{16,0},{1,17},{17,1},{2,18},{18,2},{3,19},{19,3},{4,20},{20... | collective-permute-start | bytes 331784 | tf_op jit(solution)/shard_map/ppermute | solution.py:329
  66.5 2.8 %collective-permute-done.3.b_ref = bf16[216,256]{1,0:T(8,128)(2,1)S(1)} collective-permute-done((bf16[216,256]{1,0:T(8,128)(2,1)S(1)}, bf16[216,256]{1,0:T(8,128)(2,1)S(1)}, u32[]{:S(2)}, u32[]{:S(2)}) %collective-permute-start.3) | collective-permute-done | bytes 110624 | tf_op jit(solution)/shard_map/ppermute | solution.py:329
  69.3 1.0 collective-permute-start.5
  70.3 1.0 collective-permute-done.5.d_ref
  71.2 1.4 copy-done.3
  73.3 19.1 %all_to_all.26.parts_ref = bf16[8,96,216]{2,1,0:T(8,128)(2,1)S(1)} all-to-all(bf16[8,96,216]{2,1,0:T(8,128)(2,1)S(1)} %inputs.1), channel_id=1, replica_groups=mesh['ylo'=2,'x'=4,'yhi'=2,'z'=8,'core'=2] {'z'}, dimensions={0} | all-to-all | bytes 663552 | tf_op jit(solution)/shard_map/all_to_all | solution.py:397
  92.5 14.1 %all_to_all.27.g_ref = bf16[8,96,216]{2,1,0:T(8,128)(2,1)S(1)} all-to-all(bf16[8,96,216]{2,1,0:T(8,128)(2,1)S(1)} %get-tuple-element.29), channel_id=1, replica_groups=mesh['ylo'=2,'x'=4,'yhi'=2,'z'=8,'core'=2] {'z'}, dimensions={0} | all-to-all | bytes 663552 | tf_op jit(solution)/shard_map/all_to_all | solution.py:401
  106.6 1.7 %grads.1 = (f32[2,216,256]{2,1,0:T(8,128)S(1)}, f32[2,216,256]{2,1,0:T(8,128)S(1)}, f32[8,216]{1,0:T(8,128)S(1)}) custom-call(bf16[8,96,216]{2,1,0:T(8,128)(2,1)S(1)} %all_to_all.27.g_ref, bf16[4,8,96,256]{3,2,1,0:T(8,128)(2,1)S(1)} %bitcast.21, bf16[216,256]{1,0:T(8,128)(2,1)S(1)} %get-tuple-element.27.a_ref, ...), custom_call_target="tpu_custom_call" | custom-call | tf_op jit(solution)/shard_map/grads/pallas_call | solution.py:402
  108.3 4.0 %collective-permute-start.6 = (f32[2,216,256]{2,1,0:T(8,128)S(1)}, f32[2,216,256]{2,1,0:T(8,128)S(1)}, u32[]{:S(2)}, u32[]{:S(2)}) collective-permute-start(f32[2,216,256]{2,1,0:T(8,128)S(1)} %get-tuple-element.32), channel_id=1, source_target_pairs={{0,1},{1,0},{2,3},{3,2},{4,5},{5,4},{6,7},{7,6},{8,9},{9,8},{10,11... | collective-permute-start | bytes 1327112 | tf_op jit(solution)/shard_map/ppermute | solution.py:329
  112.3 1.4 collective-permute-done.6.got_ref
  113.8 3.0 %collective-permute-start.7 = (bf16[216,256]{1,0:T(8,128)(2,1)S(1)}, bf16[216,256]{1,0:T(8,128)(2,1)S(1)}, u32[]{:S(2)}, u32[]{:S(2)}) collective-permute-start(bf16[216,256]{1,0:T(8,128)(2,1)S(1)} %fusion.1), channel_id=1, source_target_pairs={{0,16},{16,0},{1,17},{17,1},{2,18},{18,2},{3,19},{19,3},{4,20},{20... | collective-permute-start | bytes 331784 | tf_op jit(solution)/shard_map/ppermute | solution.py:329
  116.8 2.9 %collective-permute-done.7.their_ref = bf16[216,256]{1,0:T(8,128)(2,1)S(1)} collective-permute-done((bf16[216,256]{1,0:T(8,128)(2,1)S(1)}, bf16[216,256]{1,0:T(8,128)(2,1)S(1)}, u32[]{:S(2)}, u32[]{:S(2)}) %collective-permute-start.7) | collective-permute-done | bytes 110624 | tf_op jit(solution)/shard_map/ppermute | solution.py:329
  119.6 3.7 %backward.1 = (f32[24,256]{1,0:T(8,128)S(1)}, f32[16,256]{1,0:T(8,128)S(1)}) custom-call(s32[1,216]{1,0:T(1,128)S(1)} %bitcast.24, s32[1,216]{1,0:T(1,128)S(1)} %bitcast.27, bf16[8,80,256]{2,1,0:T(8,128)(2,1)S(1)} %slice.16.own_ref.a_ref, bf16[8,80,256]{2,1,0:T(8,128)(2,1)S(1)} %collective-permute-done.own_ref.b_ref, ...), custom_call_target="tpu_custom_call" | custom-call | tf_op jit(solution)/shard_map/backward/pallas_call | solution.py:412
  123.3 1.3 collective-permute-start.8
  124.6 0.8 collective-permute-done.8.got_ref
  125.5 12.6 %all_to_all.28.got_ref = f32[8,24,256]{2,1,0:T(8,128)S(1)} all-to-all(f32[8,24,256]{2,1,0:T(8,128)S(1)} %send_z.1), channel_id=1, replica_groups=mesh['ylo'=2,'x'=4,'yhi'=2,'z'=8,'core'=2] {'z'}, dimensions={0} | all-to-all | bytes 393216 | tf_op jit(solution)/shard_map/all_to_all | solution.py:428
  138.1 8.7 %all_to_all.29.got_ref = f32[8,24,256]{2,1,0:T(8,128)S(1)} all-to-all(f32[8,24,256]{2,1,0:T(8,128)S(1)} %get-tuple-element.36), channel_id=1, replica_groups=mesh['ylo'=2,'x'=4,'yhi'=2,'z'=8,'core'=2] {'ylo','x'}, dimensions={0} | all-to-all | bytes 393216 | tf_op jit(solution)/shard_map/all_to_all | solution.py:430
  146.9 2.5 %collective-permute-start.9 = (f32[24,256]{1,0:T(8,128)S(1)}, f32[24,256]{1,0:T(8,128)S(1)}, u32[]{:S(2)}, u32[]{:S(2)}) collective-permute-start(f32[24,256]{1,0:T(8,128)S(1)} %get-tuple-element.38.mine_ref), channel_id=1, source_target_pairs={{0,16},{16,0},{1,17},{17,1},{2,18},{18,2},{3,19},{19,3},{4,20},{20... | collective-permute-start | bytes 73736 | tf_op jit(solution)/shard_map/ppermute | solution.py:329
  149.5 1.7 %collective-permute-done.9.got_ref = f32[24,256]{1,0:T(8,128)S(1)} collective-permute-done((f32[24,256]{1,0:T(8,128)S(1)}, f32[24,256]{1,0:T(8,128)S(1)}, u32[]{:S(2)}, u32[]{:S(2)}) %collective-permute-start.9) | collective-permute-done | bytes 24608 | tf_op jit(solution)/shard_map/ppermute | solution.py:329
  151.3 3.9 %collective-permute-start.10 = (f32[8,256]{1,0:T(8,128)S(1)}, f32[8,256]{1,0:T(8,128)S(1)}, u32[]{:S(2)}, u32[]{:S(2)}) collective-permute-start(f32[8,256]{1,0:T(8,128)S(1)} %get-tuple-element.39.mine_ref), channel_id=1, source_target_pairs={{0,1},{1,0},{2,3},{3,2},{4,5},{5,4},{6,7},{7,6},{8,9},{9,8},{10,11... | collective-permute-start | bytes 24584 | tf_op jit(solution)/shard_map/ppermute | solution.py:329
  155.2 0.8 collective-permute-done.10.got_ref
  (50 shorter events, 2.9 us)
Async XLA Ops:
  7.2 4.0 %copy-start.13 = (f32[256]{0:T(256)S(1)}, f32[256]{0:T(256)}, u32[]{:S(2)}) copy-start(f32[256]{0:T(256)} %param.22) | copy-start | bytes 3076
  7.2 4.0 %copy-start.6 = (s32[27,256]{1,0:T(8,128)S(1)}, s32[27,256]{1,0:T(8,128)}, u32[]{:S(2)}) copy-start(s32[27,256]{1,0:T(8,128)} %status_ref.3) | copy-start | bytes 82948
  7.2 4.0 %copy-start.10 = (bf16[10,256]{1,0:T(8,128)(2,1)S(1)}, bf16[10,256]{1,0:T(8,128)(2,1)}, u32[]{:S(2)}) copy-start(bf16[10,256]{1,0:T(8,128)(2,1)} %class_ref.1) | copy-start | bytes 15364
  7.2 64.0 %all-gather.3.cloned.1.call-start = ((), (), s32[]{:S(2)}) async-start(), calls=%async_computation.5 | async-start | bytes 1966080 | tf_op jit(solution)/shard_map/all_gather | solution.py:357
  12.8 41.7 %copy-start.16 = (s32[2,27,256]{2,0,1:T(2,128)S(1)}, s32[2,27,256]{2,0,1:T(2,128)}, u32[]{:S(2)}) copy-start(s32[2,27,256]{2,0,1:T(2,128)} %param.26) | copy-start | bytes 165892
  12.8 41.7 %copy-start.7 = (s32[216]{0:T(256)S(1)}, s32[216]{0:T(256)}, u32[]{:S(2)}) copy-start(s32[216]{0:T(256)} %param.15) | copy-start | bytes 2596
  12.8 41.7 %copy-start.8 = (s32[216]{0:T(256)S(1)}, s32[216]{0:T(256)}, u32[]{:S(2)}) copy-start(s32[216]{0:T(256)} %param.16) | copy-start | bytes 2596
  12.8 41.7 %copy-start.11 = (f32[256]{0:T(256)S(1)}, f32[256]{0:T(256)}, u32[]{:S(2)}) copy-start(f32[256]{0:T(256)} %param.19) | copy-start | bytes 3076
  42.7 8.3 %collective-permute-start = (bf16[8,80,256]{2,1,0:T(8,128)(2,1)S(1)}, bf16[8,80,256]{2,1,0:T(8,128)(2,1)S(1)}, u32[]{:S(2)}, u32[]{:S(2)}) collective-permute-start(bf16[8,80,256]{2,1,0:T(8,128)(2,1)S(1)} %slice.16.own_ref.a_ref), channel_id=1, source_target_pairs={{0,16},{16,0},{1,17},{17,1},{2,18},{18,2},{3,19},{19,3},{4,20},{20... | collective-permute-start | bytes 983048 | tf_op jit(solution)/shard_map/ppermute | solution.py:329
  45.7 8.7 %collective-permute-start.1 = (bf16[8,80,256]{2,1,0:T(8,128)(2,1)S(1)}, bf16[8,80,256]{2,1,0:T(8,128)(2,1)S(1)}, u32[]{:S(2)}, u32[]{:S(2)}) collective-permute-start(bf16[8,80,256]{2,1,0:T(8,128)(2,1)S(1)} %slice.16.own_ref.a_ref), channel_id=1, source_target_pairs={{0,1},{1,0},{2,3},{3,2},{4,5},{5,4},{6,7},{7,6},{8,9},{9,8},{10,11... | collective-permute-start | bytes 983048 | tf_op jit(solution)/shard_map/ppermute | solution.py:329
  51.0 9.2 %collective-permute-start.2 = (bf16[8,80,256]{2,1,0:T(8,128)(2,1)S(1)}, bf16[8,80,256]{2,1,0:T(8,128)(2,1)S(1)}, u32[]{:S(2)}, u32[]{:S(2)}) collective-permute-start(bf16[8,80,256]{2,1,0:T(8,128)(2,1)S(1)} %collective-permute-done.own_ref.b_ref), channel_id=1, source_target_pairs={{0,1},{1,0},{2,3},{3,2},{4,5},{5,4},{6,7},{7,6},{8,9},{9,8},{10,11... | collective-permute-start | bytes 983048 | tf_op jit(solution)/shard_map/ppermute | solution.py:329
  54.5 2.2 %copy-start = (bf16[8192,256]{1,0:T(8,128)(2,1)S(1)}, bf16[8192,256]{1,0:T(8,128)(2,1)}, u32[]{:S(2)}) copy-start(bf16[8192,256]{1,0:T(8,128)(2,1)} %param.18) | copy-start | bytes 12582916
  56.7 3.5 %copy-start.1 = (bf16[8192,256]{1,0:T(8,128)(2,1)S(1)}, bf16[8192,256]{1,0:T(8,128)(2,1)}, u32[]{:S(2)}) copy-start(bf16[8192,256]{1,0:T(8,128)(2,1)} %param.18) | copy-start | bytes 12582916
  56.7 3.5 %copy-start.5 = (s32[27,256]{1,0:T(8,128)S(1)}, s32[27,256]{1,0:T(8,128)}, u32[]{:S(2)}) copy-start(s32[27,256]{1,0:T(8,128)} %status_ref.5) | copy-start | bytes 82948
  56.7 3.6 %copy-start.9 = (f32[256]{0:T(256)S(1)}, f32[256]{0:T(256)}, u32[]{:S(2)}) copy-start(f32[256]{0:T(256)} %param.27) | copy-start | bytes 3076
  56.7 3.6 %copy-start.12 = (f32[256]{0:T(256)S(1)}, f32[256]{0:T(256)}, u32[]{:S(2)}) copy-start(f32[256]{0:T(256)} %param.24) | copy-start | bytes 3076
  63.2 29.1 %copy-start.14 = (f32[96]{0:T(128)S(1)}, f32[96]{0:T(128)}, u32[]{:S(2)}) copy-start(f32[96]{0:T(128)} %param.28) | copy-start | bytes 1156
  63.2 29.1 %copy-start.15 = (f32[96]{0:T(128)S(1)}, f32[96]{0:T(128)}, u32[]{:S(2)}) copy-start(f32[96]{0:T(128)} %param.29) | copy-start | bytes 1156
  63.2 6.1 %collective-permute-start.3 = (bf16[216,256]{1,0:T(8,128)(2,1)S(1)}, bf16[216,256]{1,0:T(8,128)(2,1)S(1)}, u32[]{:S(2)}, u32[]{:S(2)}) collective-permute-start(bf16[216,256]{1,0:T(8,128)(2,1)S(1)} %get-tuple-element.27.a_ref), channel_id=1, source_target_pairs={{0,16},{16,0},{1,17},{17,1},{2,18},{18,2},{3,19},{19,3},{4,20},{20... | collective-permute-start | bytes 331784 | tf_op jit(solution)/shard_map/ppermute | solution.py:329
  66.2 4.1 %collective-permute-start.4 = (bf16[216,256]{1,0:T(8,128)(2,1)S(1)}, bf16[216,256]{1,0:T(8,128)(2,1)S(1)}, u32[]{:S(2)}, u32[]{:S(2)}) collective-permute-start(bf16[216,256]{1,0:T(8,128)(2,1)S(1)} %get-tuple-element.27.a_ref), channel_id=1, source_target_pairs={{0,1},{1,0},{2,3},{3,2},{4,5},{5,4},{6,7},{7,6},{8,9},{9,8},{10,11... | collective-permute-start | bytes 331784 | tf_op jit(solution)/shard_map/ppermute | solution.py:329
  69.3 1.9 %collective-permute-start.5 = (bf16[216,256]{1,0:T(8,128)(2,1)S(1)}, bf16[216,256]{1,0:T(8,128)(2,1)S(1)}, u32[]{:S(2)}, u32[]{:S(2)}) collective-permute-start(bf16[216,256]{1,0:T(8,128)(2,1)S(1)} %collective-permute-done.3.b_ref), channel_id=1, source_target_pairs={{0,1},{1,0},{2,3},{3,2},{4,5},{5,4},{6,7},{7,6},{8,9},{9,8},{10,11... | collective-permute-start | bytes 331784 | tf_op jit(solution)/shard_map/ppermute | solution.py:329
  71.2 1.4 copy-start.3
  72.6 34.0 %copy-start.4 = (bf16[32,96,256]{2,1,0:T(8,128)(2,1)S(1)}, bf16[32,96,256]{2,1,0:T(8,128)(2,1)}, u32[]{:S(2)}) copy-start(bf16[32,96,256]{2,1,0:T(8,128)(2,1)} %all-gather.3.cloned.1.call-done) | copy-start | bytes 4718596
  73.3 46.3 %copy-start.2 = (bf16[8192,256]{1,0:T(8,128)(2,1)S(1)}, bf16[8192,256]{1,0:T(8,128)(2,1)}, u32[]{:S(2)}) copy-start(bf16[8192,256]{1,0:T(8,128)(2,1)} %param.18) | copy-start | bytes 12582916
  108.3 5.4 %collective-permute-start.6 = (f32[2,216,256]{2,1,0:T(8,128)S(1)}, f32[2,216,256]{2,1,0:T(8,128)S(1)}, u32[]{:S(2)}, u32[]{:S(2)}) collective-permute-start(f32[2,216,256]{2,1,0:T(8,128)S(1)} %get-tuple-element.32), channel_id=1, source_target_pairs={{0,1},{1,0},{2,3},{3,2},{4,5},{5,4},{6,7},{7,6},{8,9},{9,8},{10,11... | collective-permute-start | bytes 1327112 | tf_op jit(solution)/shard_map/ppermute | solution.py:329
  113.8 5.9 %collective-permute-start.7 = (bf16[216,256]{1,0:T(8,128)(2,1)S(1)}, bf16[216,256]{1,0:T(8,128)(2,1)S(1)}, u32[]{:S(2)}, u32[]{:S(2)}) collective-permute-start(bf16[216,256]{1,0:T(8,128)(2,1)S(1)} %fusion.1), channel_id=1, source_target_pairs={{0,16},{16,0},{1,17},{17,1},{2,18},{18,2},{3,19},{19,3},{4,20},{20... | collective-permute-start | bytes 331784 | tf_op jit(solution)/shard_map/ppermute | solution.py:329
  123.3 2.1 %collective-permute-start.8 = (f32[16,256]{1,0:T(8,128)S(1)}, f32[16,256]{1,0:T(8,128)S(1)}, u32[]{:S(2)}, u32[]{:S(2)}) collective-permute-start(f32[16,256]{1,0:T(8,128)S(1)} %get-tuple-element.35), channel_id=1, source_target_pairs={{0,1},{1,0},{2,3},{3,2},{4,5},{5,4},{6,7},{7,6},{8,9},{9,8},{10,11... | collective-permute-start | bytes 49160 | tf_op jit(solution)/shard_map/ppermute | solution.py:329
  146.9 4.3 %collective-permute-start.9 = (f32[24,256]{1,0:T(8,128)S(1)}, f32[24,256]{1,0:T(8,128)S(1)}, u32[]{:S(2)}, u32[]{:S(2)}) collective-permute-start(f32[24,256]{1,0:T(8,128)S(1)} %get-tuple-element.38.mine_ref), channel_id=1, source_target_pairs={{0,16},{16,0},{1,17},{17,1},{2,18},{18,2},{3,19},{19,3},{4,20},{20... | collective-permute-start | bytes 73736 | tf_op jit(solution)/shard_map/ppermute | solution.py:329
  151.3 4.7 %collective-permute-start.10 = (f32[8,256]{1,0:T(8,128)S(1)}, f32[8,256]{1,0:T(8,128)S(1)}, u32[]{:S(2)}, u32[]{:S(2)}) collective-permute-start(f32[8,256]{1,0:T(8,128)S(1)} %get-tuple-element.39.mine_ref), channel_id=1, source_target_pairs={{0,1},{1,0},{2,3},{3,2},{4,5},{5,4},{6,7},{7,6},{8,9},{9,8},{10,11... | collective-permute-start | bytes 24584 | tf_op jit(solution)/shard_map/ppermute | solution.py:329
Sparse Core Ops, SparseCore 0:
  42.8 27.2 all-gather.2

commit v3 on v2

--- a/solution.py
+++ b/solution.py
@@ -12,6 +12,7 @@
 CLASSES = 10
 GROUP = 8
 LANES = 256
+LIMIT = 16 * 1024 * 1024
 
 grid_step = 0.0625
 step_rate = 0.25
@@ -71,31 +72,40 @@
     return factor, offset, chosen
 
 
-def prep_kernel(status_ref, bounds_ref, class_ref, slopes_ref, weight_ref, out_ref, held, sems):
+def prep_kernel(status_ref, bounds_ref, class_ref, slopes_ref, weight_ref, out_ref, status, bounds, sems):
     x = lax.axis_index("x")
     domains = status_ref.shape[0]
-    count = held.shape[0]
+    count, feats = out_ref.shape[0], weight_ref.shape[0]
+    firsts = [
+        pltpu.make_async_copy(status_ref, status, sems.at[count]),
+        pltpu.make_async_copy(bounds_ref, bounds, sems.at[count + 1]),
+    ]
     copies = [
-        pltpu.make_async_copy(weight_ref.at[x // 2, k, x % 2], held.at[k], sems.at[k]) for k in range(count)
+        pltpu.make_async_copy(
+            weight_ref.at[:, pl.ds(pl.multiple_of(((x // 2 * count + k) * 2 + x % 2) * LANES, LANES), LANES)],
+            out_ref.at[k, pl.ds(ROWS_ALL, feats)],
+            sems.at[k],
+        )
+        for k in range(count)
     ]
-    for copy in copies:
+    for copy in firsts + copies:
         copy.start()
-    status = status_ref[...]
-    active, unsplit = status == 1, status == 2
-    pad = jnp.ones((32 - domains, LANES), F32)
-    up = jnp.where(unsplit, bounds_ref[1], jnp.where(active, 1, 0)).astype(F32)
-    low = jnp.where(unsplit, bounds_ref[0], jnp.where(active, 0, 1)).astype(F32)
     slopes = slopes_ref[...]
     high = lax.reduce_precision(slopes, 8, 7)
     middle = lax.reduce_precision(slopes - high, 8, 7)
     last = (slopes - high) - middle
     tail = jnp.concatenate([class_ref[...].astype(F32), high, middle, last, jnp.zeros((3, LANES), F32)], axis=0)
+    for copy in firsts:
+        copy.wait()
+    active, unsplit = status[...] == 1, status[...] == 2
+    pad = jnp.ones((32 - domains, LANES), F32)
+    up = jnp.where(unsplit, bounds[:, 1], jnp.where(active, 1, 0)).astype(F32)
+    low = jnp.where(unsplit, bounds[:, 0], jnp.where(active, 0, 1)).astype(F32)
     info = jnp.concatenate([up, pad, low, pad, tail], axis=0).astype(BF16)
     for k in range(count):
         out_ref[k, 0:ROWS_ALL] = info
-    for k, copy in enumerate(copies):
+    for copy in copies:
         copy.wait()
-        out_ref[k, ROWS_ALL : ROWS_ALL + held.shape[2]] = held[k].astype(F32).T.astype(BF16)
 
 
 def forward_half(
@@ -152,7 +162,7 @@
     def _():
         coeffs = total[...]
         factor, offset, _ = relax_rows(
-            coeffs, status_ref[...], bounds_ref[0].astype(F32), bounds_ref[1].astype(F32), slopes_ref[...]
+            coeffs, status_ref[...], bounds_ref[:, 0].astype(F32), bounds_ref[:, 1].astype(F32), slopes_ref[...]
         )
         sent = (coeffs * factor).astype(BF16)
         sent_ref[...] = sent
@@ -172,13 +182,16 @@
         held[own ^ ((place % 2) * 2 + place // 2)] = ref[...]
 
 
-def input_kernel(a_ref, b_ref, c_ref, d_ref, weight_ref, out_ref, held):
-    own = lax.axis_index("yhi") * 2 + lax.axis_index("core")
+SHIFTS = (0, 1, 3, 2)
+
+
+def input_kernel(a_ref, b_ref, c_ref, d_ref, w0_ref, w1_ref, w2_ref, w3_ref, out_ref, held):
+    own, x = lax.axis_index("yhi") * 2 + lax.axis_index("core"), lax.axis_index("x")
     hold(held, (a_ref, b_ref, c_ref, d_ref), own)
-    _, zs, feats, _ = weight_ref.shape
+    zs, feats, _ = w0_ref.shape
     acc = None
-    for q in range(4):
-        part = contract(weight_ref[q].reshape(zs * feats, LANES), held[q], 1, 1)
+    for by, ref in zip(SHIFTS, (w0_ref, w1_ref, w2_ref, w3_ref)):
+        part = contract(ref[...].reshape(zs * feats, LANES), held[(x + 4 - by) % 4], 1, 1)
         acc = part if acc is None else acc + part
     out_ref[...] = acc.reshape(zs, feats, acc.shape[1]).astype(BF16)
 
@@ -204,15 +217,17 @@
 
 
 def grads_kernel(
-    g_ref, weight_ref, a_ref, b_ref, c_ref, d_ref, so_far_ref, near_ref, far_ref, bound_ref, held
+    g_ref, w0_ref, w1_ref, w2_ref, w3_ref, a_ref, b_ref, c_ref, d_ref, so_far_ref,
+    near_ref, far_ref, bound_ref, held,
 ):
-    own = lax.axis_index("yhi") * 2 + lax.axis_index("core")
+    own, x = lax.axis_index("yhi") * 2 + lax.axis_index("core"), lax.axis_index("x")
     hold(held, (a_ref, b_ref, c_ref, d_ref), own)
     zs, feats, rows = g_ref.shape
     grads = g_ref[...].reshape(zs * feats, rows)
     terms = None
-    for q in range(4):
-        part = contract(grads, weight_ref[q].reshape(zs * feats, LANES), 0, 0)
+    for by, ref in zip(SHIFTS, (w0_ref, w1_ref, w2_ref, w3_ref)):
+        q = (x + 4 - by) % 4
+        part = contract(grads, ref[...].reshape(zs * feats, LANES), 0, 0)
         term = part * held[q].astype(F32)
         terms = term if terms is None else terms + term
         place = own ^ q
@@ -243,7 +258,7 @@
         coeffs = coeffs_ref[...]
         grads = near_ref[0] + got_ref[0] + their_ref[...].astype(F32) + bias_ref[...]
         factor, offset, chosen = relax_rows(
-            coeffs, status_ref[...], bounds_ref[0].astype(F32), bounds_ref[1].astype(F32), slopes_ref[...]
+            coeffs, status_ref[...], bounds_ref[:, 0].astype(F32), bounds_ref[:, 1].astype(F32), slopes_ref[...]
         )
         back[...] = (grads * factor + offset).astype(BF16)
         mine_ref[16:24] = jnp.zeros((8, LANES), F32)
@@ -274,33 +289,33 @@
         out_ref[k, 16:24] = rest
 
 
-def send_dom_kernel(got_ref, out_ref, bound_ref):
+def send_dom_kernel(got_ref, out_ref):
     total = got_ref[0]
     for k in range(1, got_ref.shape[0]):
         total = total + got_ref[k]
-    bound_ref[...] = total[17:18]
     first = jnp.concatenate([got_ref[k, 16:17] for k in range(got_ref.shape[0])], axis=0)
     for k in range(out_ref.shape[0]):
         out_ref[k, 0:16] = total[0:16]
         out_ref[k, 16:24] = first
-
-
-def send_y_kernel(got_ref, bound_ref, out_ref, first_ref):
-    total = got_ref[0]
-    for k in range(1, got_ref.shape[0]):
-        total = total + got_ref[k]
-    first = total[16:24]
-    first_ref[...] = first
-    out_ref[0:16] = total[0:16]
-    out_ref[16:24] = jnp.zeros((8, LANES), F32)
-    out_ref[16:17] = bound_ref[...]
-    out_ref[17:18] = jnp.broadcast_to(jnp.sum(first * first, keepdims=True), (1, LANES))
-
-
-def send_core_kernel(mine_ref, got_ref, out_ref, deep_ref):
-    deep = mine_ref[0:16] + got_ref[0:16]
+        out_ref[k, 24:32] = total[16:24]
+
+
+def send_core_kernel(got_ref, out_ref, deep_ref, first_ref):
+    yhi, dom = lax.axis_index("yhi"), lax.axis_index("ylo") * 4 + lax.axis_index("x")
+    halves = []
+    for y in range(2):
+        total = got_ref[y, 0:24]
+        for k in range(1, got_ref.shape[0] // 2):
+            total = total + got_ref[2 * k + y, 0:24]
+        halves.append(total)
+    deep = halves[0][0:16] + halves[1][0:16]
     deep_ref[...] = deep
-    out_ref[...] = mine_ref[16:24] + got_ref[16:24]
+    firsts = [half[16:24] for half in halves]
+    first_ref[...] = jnp.where(yhi == 0, firsts[0], firsts[1])
+    power = jnp.sum(firsts[0] * firsts[0] + firsts[1] * firsts[1], keepdims=True)
+    out_ref[...] = jnp.zeros_like(out_ref)
+    out_ref[0:1] = (got_ref[2 * dom] + got_ref[2 * dom + 1])[25:26]
+    out_ref[1:2] = jnp.broadcast_to(power, (1, LANES))
     out_ref[2:3] = jnp.broadcast_to(jnp.sum(deep * deep, keepdims=True), (1, LANES))
 
 
@@ -337,32 +352,38 @@
     rows = spec_label.shape[0]
     domains = deep_status.shape[0]
     feats = box_center.shape[0]
-    params = pltpu.CompilerParams(vmem_limit_bytes=24 * 1024 * 1024)
-    call = functools.partial(pl.pallas_call, compiler_params=params)
-    vmem = pl.BlockSpec(memory_space=pltpu.VMEM)
-
-    message = call(
+    call = functools.partial(
+        pl.pallas_call, compiler_params=pltpu.CompilerParams(vmem_limit_bytes=LIMIT)
+    )
+    vmem, hbm = pl.BlockSpec(), pl.BlockSpec(memory_space=pltpu.HBM)
+
+    message = pl.pallas_call(
         prep_kernel,
-        in_specs=[vmem] * 4 + [pl.BlockSpec(memory_space=pl.ANY)],
+        compiler_params=pltpu.CompilerParams(vmem_limit_bytes=62 * 1024 * 1024),
+        in_specs=[hbm, hbm, vmem, vmem, hbm],
         out_specs=vmem,
         out_shape=shape((8, ROWS_ALL + feats, LANES), BF16),
-        scratch_shapes=[pltpu.VMEM((8, LANES, feats), BF16), pltpu.SemaphoreType.DMA((8,))],
+        scratch_shapes=[
+            pltpu.VMEM((domains, LANES), jnp.int32),
+            pltpu.VMEM((domains, 2, LANES), jnp.int32),
+            pltpu.SemaphoreType.DMA((10,)),
+        ],
         name="prep",
-    )(deep_status, deep_bounds, class_rows, deep_slopes[None], first_weight.reshape(2, 8, 2, LANES, feats))
+    )(deep_status, deep_bounds.transpose(1, 0, 2), class_rows, deep_slopes[None], first_weight.T)
     message = lax.all_to_all(message, "z", 0, 0, tiled=True)
     info_a = message[:, :ROWS_ALL]
     info_b = shifted(info_a, "yhi", 2, 1)
     info_c = shifted(info_a, "core", 2, 1)
-    info_d = shifted(info_b, "core", 2, 1)
-    w_all = lax.all_gather(message[:, ROWS_ALL:], "x", axis=0)
+    w_own = message[:, ROWS_ALL:]
+    w_all = [w_own] + [shifted(w_own, "x", 4, k) for k in SHIFTS[1:]]
 
     label, offset = spec_label[None], spec_offset[None]
     weight = deep_weight.reshape(2, 8, 2, LANES, LANES)
     depth = 2
     info_spec = pl.BlockSpec((depth, ROWS_ALL, LANES), lambda s: (s, 0, 0))
     label_specs = [whole((1, rows))] * 2
-    layer_specs = [whole((domains, LANES)), whole((2, domains, LANES)), whole((1, LANES)), whole((1, LANES))]
-    layer = (first_status, first_bounds, first_slopes[None], first_bias[None])
+    layer_specs = [whole((domains, LANES)), whole((domains, 2, LANES)), whole((1, LANES)), whole((1, LANES))]
+    layer = (first_status, first_bounds.transpose(1, 0, 2), first_slopes[None], first_bias[None])
     half_spec = lambda other: pl.BlockSpec(
         (1, depth, 2, LANES, LANES), lambda s: (lax.axis_index("yhi") ^ other, s, 0, 0, 0)
     )
@@ -376,6 +397,8 @@
         out_shape=[shape((rows, LANES)), shape((rows, LANES))],
         name="forward_near",
     )(label, offset, info_a, info_c, weight, deep_bias[None])
+    total, info_b, w_all[1], w_all[2] = lax.optimization_barrier((total, info_b, w_all[1], w_all[2]))
+    info_d = shifted(info_b, "core", 2, 1)
     sent, coeffs, const = call(
         far_kernel,
         grid=(8 // depth,),
@@ -393,7 +416,7 @@
     held = [pltpu.VMEM((4, rows, LANES), BF16)]
     parts = call(
         input_kernel, out_shape=shape((8, feats, rows), BF16), scratch_shapes=held, name="inputs"
-    )(*sents, w_all)
+    )(*sents, *w_all)
     parts = lax.all_to_all(parts, "z", 0, 0, tiled=True)
     grads, bound = call(
         box_kernel, out_shape=[shape((8, feats, rows), BF16), shape((1, rows))], name="box"
@@ -404,7 +427,7 @@
         out_shape=[shape((2, rows, LANES))] * 2 + [shape((8, rows))],
         scratch_shapes=held,
         name="grads",
-    )(grads, w_all, *sents, bound)
+    )(grads, *w_all, *sents, bound)
     got = shifted(far, "core", 2, 1)
     their = shifted((near[1] + got[1]).astype(BF16), "yhi", 2, 1)
 
@@ -423,17 +446,15 @@
         name="backward",
     )(label, offset, info_a, info_b, info_c, info_d, weight, deep_bias[None], *layer, coeffs, near, got, their, bound)
 
-    to_all = shape((8, 24, LANES))
-    to_z = call(send_z_kernel, out_shape=to_all, name="send_z")(mine, shifted(other, "core", 2, 1))
+    to_z = call(send_z_kernel, out_shape=shape((8, 24, LANES)), name="send_z")(mine, shifted(other, "core", 2, 1))
     got = lax.all_to_all(to_z, "z", 0, 0, tiled=True)
-    to_dom, bound = call(send_dom_kernel, out_shape=[to_all, shape((1, LANES))], name="send_dom")(got)
-    got = lax.all_to_all(to_dom, DOM, 0, 0, tiled=True)
-    to_y, first = call(
-        send_y_kernel, out_shape=[shape((24, LANES)), shape((8, LANES))], name="send_y"
-    )(got, bound)
-    to_core, deep = call(
-        send_core_kernel, out_shape=[shape((8, LANES)), shape((16, LANES))], name="send_core"
-    )(to_y, shifted(to_y, "yhi", 2, 1))
+    to_dom = call(send_dom_kernel, out_shape=shape((16, 32, LANES)), name="send_dom")(got)
+    got = lax.all_to_all(to_dom, DOM + ("yhi",), 0, 0, tiled=True)
+    to_core, deep, first = call(
+        send_core_kernel,
+        out_shape=[shape((8, LANES)), shape((16, LANES)), shape((8, LANES))],
+        name="send_core",
+    )(got)
     bound, first_next, deep_next = call(
         finish_kernel, out_shape=[shape((1, rows)), shape((1, LANES)), shape((1, LANES))], name="finish"
     )(to_core, shifted(to_core, "core", 2, 1), deep, first, deep_slopes[None], first_slopes[None])

time: 164 us -> 147 us (0.90)
  between operations: 14.3 us -> 0.83 us
  blocking collectives: 83.5 us -> 91 us
  local copies, waits for them, and re-layouts: 8.38 us -> 2.29 us
  starting transfers between devices: 28.2 us -> 24.6 us
  waiting for transfers between devices: 13.9 us -> 11.3 us
    all_to_all x1, blocking collectives: 8.75 us -> 14.9 us  [on_device(): got = lax.all_to_all(to_dom, DOM + ('yhi',), 0, 0, tiled=True)]
    unnamed x37 -> x24, local copies, waits for them, and re-layouts: 7.59 us -> 2.24 us
    ppermute x11 -> x13, starting transfers between devices: 28.2 us -> 24.6 us  [shifted(): lax.ppermute(value, axis, [(i, (i + by) % size) for i in range(size)])]
    all_to_all x1, blocking collectives: 14.1 us -> 16.7 us  [on_device(): grads = lax.all_to_all(grads, 'z', 0, 0, tiled=True)]
    ppermute x11 -> x13, waiting for transfers between devices: 13.9 us -> 11.3 us  [shifted(): lax.ppermute(value, axis, [(i, (i + by) % size) for i in range(size)])]
  transfers between devices with their start and end apart: 12 -> 13, of which waited for: 8 -> 8; matrix products, arithmetic and copies ran while one was open for 0% -> 0% of each run, Pallas kernels for 4% -> 4%
where the time goes in v3:
time: 147 us; the launch traced here: 146 us
  blocking collectives  91 us (62%)
  starting transfers between devices  24.6 us (17%)
  Pallas kernels  16.2 us (11%)
  waiting for transfers between devices  11.3 us (8%)
  local copies, waits for them, and re-layouts  2.29 us (2%)
    all_to_all x1, blocking collectives, on_device(): message = lax.all_to_all(message, 'z', 0, 0, tiled=True)  29.3 us
    ppermute x13, starting transfers between devices, shifted(): lax.ppermute(value, axis, [(i, (i + by) % size) for i in range(size)])  24.6 us
    all_to_all x1, blocking collectives, on_device(): parts = lax.all_to_all(parts, 'z', 0, 0, tiled=True)  17.6 us
    all_to_all x1, blocking collectives, on_device(): grads = lax.all_to_all(grads, 'z', 0, 0, tiled=True)  16.7 us
    all_to_all x1, blocking collectives, on_device(): got = lax.all_to_all(to_dom, DOM + ('yhi',), 0, 0, tiled=True)  14.9 us
    all_to_all x1, blocking collectives, on_device(): got = lax.all_to_all(to_z, 'z', 0, 0, tiled=True)  12.6 us
    ppermute x13, waiting for transfers between devices, shifted(): lax.ppermute(value, axis, [(i, (i + by) % size) for i in range(size)])  11.3 us
    pallas_call x1, Pallas kernels, on_device(): call(backward_kernel, grid=(8 // depth,), in_specs=label_specs + [info_sp...  3.76 us
  transfers between devices with their start and end apart: 13, of which 8 were waited for; matrix products, arithmetic and copies ran while one was open for 0% of the time, Pallas kernels for 4%

profile of v3, /device:TPU:1, one launch (start us, length us, event | category | flops | bytes accessed | tf_op | source)
XLA Modules:
  0.0 146.3 jit_solution(5059093718351258681)
XLA Ops:
  0.7 2.7 %prep.1 = bf16[8,176,256]{2,1,0:T(8,128)(2,1)} custom-call(s32[27,256]{1,0:T(8,128)} %status_ref.3, s32[27,2,256]{2,1,0:T(2,128)} %bitcast.40, bf16[10,256]{1,0:T(8,128)(2,1)} %class_ref.1, f32[1,256]{1,0:T(1,128)} %bitcast.31, bf16[96,8192]{1,0:T(8,128)(2,1)} %bitcast.39), custom_call_target="tpu_custom_call" | custom-call | tf_op jit(solution)/shard_map/prep/pallas_call | solution.py:360
  3.4 29.3 %all_to_all.25 = bf16[8,176,256]{2,1,0:T(8,128)(2,1)S(1)} all-to-all(bf16[8,176,256]{2,1,0:T(8,128)(2,1)} %prep.1), channel_id=1, replica_groups=mesh['ylo'=2,'x'=4,'yhi'=2,'z'=8,'core'=2] {'z'}, dimensions={0} | all-to-all | bytes 1441792 | tf_op jit(solution)/shard_map/all_to_all | solution.py:373
  32.7 2.6 %collective-permute-start.3 = (bf16[8,96,256]{2,1,0:T(8,128)(2,1)S(1)}, bf16[8,96,256]{2,1,0:T(8,128)(2,1)S(1)}, u32[]{:S(2)}, u32[]{:S(2)}) collective-permute-start(bf16[8,96,256]{2,1,0:T(8,128)(2,1)S(1)} %slice.17.w0_ref), channel_id=1, source_target_pairs={{0,96},{32,0},{64,32},{96,64},{1,97},{33,1},{65,33},{97,65},{2,98}... | collective-permute-start | bytes 1179656 | tf_op jit(solution)/shard_map/ppermute | solution.py:344
  35.3 2.9 %collective-permute-start = (bf16[8,80,256]{2,1,0:T(8,128)(2,1)S(1)}, bf16[8,80,256]{2,1,0:T(8,128)(2,1)S(1)}, u32[]{:S(2)}, u32[]{:S(2)}) collective-permute-start(bf16[8,80,256]{2,1,0:T(8,128)(2,1)S(1)} %slice.16.own_ref.a_ref), channel_id=1, source_target_pairs={{0,1},{1,0},{2,3},{3,2},{4,5},{5,4},{6,7},{7,6},{8,9},{9,8},{10,11... | collective-permute-start | bytes 983048 | tf_op jit(solution)/shard_map/ppermute | solution.py:344
  38.2 2.9 %collective-permute-start.1 = (bf16[8,80,256]{2,1,0:T(8,128)(2,1)S(1)}, bf16[8,80,256]{2,1,0:T(8,128)(2,1)S(1)}, u32[]{:S(2)}, u32[]{:S(2)}) collective-permute-start(bf16[8,80,256]{2,1,0:T(8,128)(2,1)S(1)} %slice.16.own_ref.a_ref), channel_id=1, source_target_pairs={{0,16},{16,0},{1,17},{17,1},{2,18},{18,2},{3,19},{19,3},{4,20},{20... | collective-permute-start | bytes 983048 | tf_op jit(solution)/shard_map/ppermute | solution.py:344
  41.2 2.2 %copy-done = bf16[8192,256]{1,0:T(8,128)(2,1)S(1)} copy-done((bf16[8192,256]{1,0:T(8,128)(2,1)S(1)}, bf16[8192,256]{1,0:T(8,128)(2,1)}, u32[]{:S(2)}) %copy-start) | copy-done | bytes 4194328
  43.3 3.5 %forward_near.1 = (f32[216,256]{1,0:T(8,128)S(1)}, f32[216,256]{1,0:T(8,128)S(1)}) custom-call(s32[1,216]{1,0:T(1,128)S(1)} %bitcast.22, s32[1,216]{1,0:T(1,128)S(1)} %bitcast.25, bf16[8,80,256]{2,1,0:T(8,128)(2,1)S(1)} %slice.16.own_ref.a_ref, bf16[8,80,256]{2,1,0:T(8,128)(2,1)S(1)} %collective-permute-done.other_ref.c_ref, ...), custom_call_target="tpu_custom_call" | custom-call | tf_op jit(solution)/shard_map/forward_near/pallas_call | solution.py:392
  46.8 2.1 %collective-permute-done.1.own_ref.b_ref = bf16[8,80,256]{2,1,0:T(8,128)(2,1)S(1)} collective-permute-done((bf16[8,80,256]{2,1,0:T(8,128)(2,1)S(1)}, bf16[8,80,256]{2,1,0:T(8,128)(2,1)S(1)}, u32[]{:S(2)}, u32[]{:S(2)}) %collective-permute-start.1) | collective-permute-done | bytes 327712 | tf_op jit(solution)/shard_map/ppermute | solution.py:344
  49.0 0.9 collective-permute-start.4
  49.9 2.0 %collective-permute-start.8 = (bf16[8,96,256]{2,1,0:T(8,128)(2,1)S(1)}, bf16[8,96,256]{2,1,0:T(8,128)(2,1)S(1)}, u32[]{:S(2)}, u32[]{:S(2)}) collective-permute-start(bf16[8,96,256]{2,1,0:T(8,128)(2,1)S(1)} %slice.17.w0_ref), channel_id=1, source_target_pairs={{0,64},{32,96},{64,0},{96,32},{1,65},{33,97},{65,1},{97,33},{2,66}... | collective-permute-start | bytes 1179656 | tf_op jit(solution)/shard_map/ppermute | solution.py:344
  51.9 3.0 %forward_far.1 = (bf16[216,256]{1,0:T(8,128)(2,1)S(1)}, f32[216,256]{1,0:T(8,128)S(1)}, f32[8,216]{1,0:T(8,128)S(1)}) custom-call(s32[1,216]{1,0:T(1,128)S(1)} %bitcast.23, s32[1,216]{1,0:T(1,128)S(1)} %bitcast.26, bf16[8,80,256]{2,1,0:T(8,128)(2,1)S(1)} %collective-permute-done.1.own_ref.b_ref, ...), custom_call_target="tpu_custom_call" | custom-call | tf_op jit(solution)/shard_map/forward_far/pallas_call | solution.py:402
  55.0 2.9 %collective-permute-start.5 = (bf16[216,256]{1,0:T(8,128)(2,1)S(1)}, bf16[216,256]{1,0:T(8,128)(2,1)S(1)}, u32[]{:S(2)}, u32[]{:S(2)}) collective-permute-start(bf16[216,256]{1,0:T(8,128)(2,1)S(1)} %get-tuple-element.30.a_ref), channel_id=1, source_target_pairs={{0,16},{16,0},{1,17},{17,1},{2,18},{18,2},{3,19},{19,3},{4,20},{20... | collective-permute-start | bytes 331784 | tf_op jit(solution)/shard_map/ppermute | solution.py:344
  57.9 0.6 collective-permute-start.6
  58.5 2.2 %collective-permute-done.5.b_ref = bf16[216,256]{1,0:T(8,128)(2,1)S(1)} collective-permute-done((bf16[216,256]{1,0:T(8,128)(2,1)S(1)}, bf16[216,256]{1,0:T(8,128)(2,1)S(1)}, u32[]{:S(2)}, u32[]{:S(2)}) %collective-permute-start.5) | collective-permute-done | bytes 110624 | tf_op jit(solution)/shard_map/ppermute | solution.py:344
  60.8 1.2 collective-permute-start.7
  62.0 0.9 collective-permute-done.7.d_ref
  62.9 0.6 inputs.1
  63.6 17.6 %all_to_all.26.parts_ref = bf16[8,96,216]{2,1,0:T(8,128)(2,1)S(1)} all-to-all(bf16[8,96,216]{2,1,0:T(8,128)(2,1)S(1)} %inputs.1), channel_id=1, replica_groups=mesh['ylo'=2,'x'=4,'yhi'=2,'z'=8,'core'=2] {'z'}, dimensions={0} | all-to-all | bytes 663552 | tf_op jit(solution)/shard_map/all_to_all | solution.py:420
  81.3 16.7 %all_to_all.27.g_ref = bf16[8,96,216]{2,1,0:T(8,128)(2,1)S(1)} all-to-all(bf16[8,96,216]{2,1,0:T(8,128)(2,1)S(1)} %get-tuple-element.34), channel_id=1, replica_groups=mesh['ylo'=2,'x'=4,'yhi'=2,'z'=8,'core'=2] {'z'}, dimensions={0} | all-to-all | bytes 663552 | tf_op jit(solution)/shard_map/all_to_all | solution.py:424
  98.0 1.7 %grads.1 = (f32[2,216,256]{2,1,0:T(8,128)S(1)}, f32[2,216,256]{2,1,0:T(8,128)S(1)}, f32[8,216]{1,0:T(8,128)S(1)}) custom-call(bf16[8,96,216]{2,1,0:T(8,128)(2,1)S(1)} %all_to_all.27.g_ref, bf16[8,96,256]{2,1,0:T(8,128)(2,1)S(1)} %slice.17.w0_ref, bf16[8,96,256]{2,1,0:T(8,128)(2,1)S(1)} %collective-permute-done.2.w1_ref, ...), custom_call_target="tpu_custom_call" | custom-call | tf_op jit(solution)/shard_map/grads/pallas_call | solution.py:425
  99.7 1.3 collective-permute-start.9
  101.0 1.4 collective-permute-done.9.got_ref
  102.5 3.0 %collective-permute-start.10 = (bf16[216,256]{1,0:T(8,128)(2,1)S(1)}, bf16[216,256]{1,0:T(8,128)(2,1)S(1)}, u32[]{:S(2)}, u32[]{:S(2)}) collective-permute-start(bf16[216,256]{1,0:T(8,128)(2,1)S(1)} %fusion.1), channel_id=1, source_target_pairs={{0,16},{16,0},{1,17},{17,1},{2,18},{18,2},{3,19},{19,3},{4,20},{20... | collective-permute-start | bytes 331784 | tf_op jit(solution)/shard_map/ppermute | solution.py:344
  105.5 2.9 %collective-permute-done.10.their_ref = bf16[216,256]{1,0:T(8,128)(2,1)S(1)} collective-permute-done((bf16[216,256]{1,0:T(8,128)(2,1)S(1)}, bf16[216,256]{1,0:T(8,128)(2,1)S(1)}, u32[]{:S(2)}, u32[]{:S(2)}) %collective-permute-start.10) | collective-permute-done | bytes 110624 | tf_op jit(solution)/shard_map/ppermute | solution.py:344
  108.4 3.8 %backward.1 = (f32[24,256]{1,0:T(8,128)S(1)}, f32[16,256]{1,0:T(8,128)S(1)}) custom-call(s32[1,216]{1,0:T(1,128)S(1)} %bitcast.24, s32[1,216]{1,0:T(1,128)S(1)} %bitcast.27, bf16[8,80,256]{2,1,0:T(8,128)(2,1)S(1)} %slice.16.own_ref.a_ref, bf16[8,80,256]{2,1,0:T(8,128)(2,1)S(1)} %collective-permute-done.1.own_ref.b_ref, ...), custom_call_target="tpu_custom_call" | custom-call | tf_op jit(solution)/shard_map/backward/pallas_call | solution.py:435
  112.1 1.3 collective-permute-start.11
  113.4 0.8 collective-permute-done.11.got_ref
  114.3 12.6 %all_to_all.28.got_ref = f32[8,24,256]{2,1,0:T(8,128)S(1)} all-to-all(f32[8,24,256]{2,1,0:T(8,128)S(1)} %send_z.1), channel_id=1, replica_groups=mesh['ylo'=2,'x'=4,'yhi'=2,'z'=8,'core'=2] {'z'}, dimensions={0} | all-to-all | bytes 393216 | tf_op jit(solution)/shard_map/all_to_all | solution.py:450
  126.9 14.9 %all_to_all.29.got_ref = f32[16,32,256]{2,1,0:T(8,128)S(1)} all-to-all(f32[16,32,256]{2,1,0:T(8,128)S(1)} %send_dom.1), channel_id=1, replica_groups=mesh['ylo'=2,'x'=4,'yhi'=2,'z'=8,'core'=2] {'ylo','x','yhi'}, dimensions={0} | all-to-all | bytes 1048576 | tf_op jit(solution)/shard_map/all_to_all | solution.py:452
  141.9 2.9 %collective-permute-start.12 = (f32[8,256]{1,0:T(8,128)S(1)}, f32[8,256]{1,0:T(8,128)S(1)}, u32[]{:S(2)}, u32[]{:S(2)}) collective-permute-start(f32[8,256]{1,0:T(8,128)S(1)} %get-tuple-element.41.mine_ref), channel_id=1, source_target_pairs={{0,1},{1,0},{2,3},{3,2},{4,5},{5,4},{6,7},{7,6},{8,9},{9,8},{10,11... | collective-permute-start | bytes 24584 | tf_op jit(solution)/shard_map/ppermute | solution.py:344
  144.8 0.8 collective-permute-done.12.got_ref
  145.7 0.6 finish.1
  (37 shorter events, 0.6 us)
Async XLA Ops:
  0.6 40.5 %copy-start.8 = (f32[256]{0:T(256)S(1)}, f32[256]{0:T(256)}, u32[]{:S(2)}) copy-start(f32[256]{0:T(256)} %param.19) | copy-start | bytes 3076
  0.6 40.5 %copy-start.5 = (s32[216]{0:T(256)S(1)}, s32[216]{0:T(256)}, u32[]{:S(2)}) copy-start(s32[216]{0:T(256)} %param.16) | copy-start | bytes 2596
  0.7 40.5 %copy-start.4 = (s32[216]{0:T(256)S(1)}, s32[216]{0:T(256)}, u32[]{:S(2)}) copy-start(s32[216]{0:T(256)} %param.15) | copy-start | bytes 2596
  3.4 48.5 %copy-start.2 = (s32[2,27,256]{2,0,1:T(2,128)S(1)}, s32[2,27,256]{2,0,1:T(2,128)}, u32[]{:S(2)}) copy-start(s32[2,27,256]{2,0,1:T(2,128)} %param.26) | copy-start | bytes 165892
  3.4 48.5 %copy-start.3 = (s32[27,256]{1,0:T(8,128)S(1)}, s32[27,256]{1,0:T(8,128)}, u32[]{:S(2)}) copy-start(s32[27,256]{1,0:T(8,128)} %status_ref.5) | copy-start | bytes 82948
  3.4 48.5 %copy-start.6 = (f32[256]{0:T(256)S(1)}, f32[256]{0:T(256)}, u32[]{:S(2)}) copy-start(f32[256]{0:T(256)} %param.27) | copy-start | bytes 3076
  3.4 48.5 %copy-start.9 = (f32[256]{0:T(256)S(1)}, f32[256]{0:T(256)}, u32[]{:S(2)}) copy-start(f32[256]{0:T(256)} %param.24) | copy-start | bytes 3076
  32.7 16.3 %collective-permute-start.3 = (bf16[8,96,256]{2,1,0:T(8,128)(2,1)S(1)}, bf16[8,96,256]{2,1,0:T(8,128)(2,1)S(1)}, u32[]{:S(2)}, u32[]{:S(2)}) collective-permute-start(bf16[8,96,256]{2,1,0:T(8,128)(2,1)S(1)} %slice.17.w0_ref), channel_id=1, source_target_pairs={{0,96},{32,0},{64,32},{96,64},{1,97},{33,1},{65,33},{97,65},{2,98}... | collective-permute-start | bytes 1179656 | tf_op jit(solution)/shard_map/ppermute | solution.py:344
  35.3 13.7 %collective-permute-start.2 = (bf16[8,96,256]{2,1,0:T(8,128)(2,1)S(1)}, bf16[8,96,256]{2,1,0:T(8,128)(2,1)S(1)}, u32[]{:S(2)}, u32[]{:S(2)}) collective-permute-start(bf16[8,96,256]{2,1,0:T(8,128)(2,1)S(1)} %slice.17.w0_ref), channel_id=1, source_target_pairs={{0,32},{32,64},{64,96},{96,0},{1,33},{33,65},{65,97},{97,1},{2,34}... | collective-permute-start | bytes 1179656 | tf_op jit(solution)/shard_map/ppermute | solution.py:344
  35.3 5.8 %collective-permute-start = (bf16[8,80,256]{2,1,0:T(8,128)(2,1)S(1)}, bf16[8,80,256]{2,1,0:T(8,128)(2,1)S(1)}, u32[]{:S(2)}, u32[]{:S(2)}) collective-permute-start(bf16[8,80,256]{2,1,0:T(8,128)(2,1)S(1)} %slice.16.own_ref.a_ref), channel_id=1, source_target_pairs={{0,1},{1,0},{2,3},{3,2},{4,5},{5,4},{6,7},{7,6},{8,9},{9,8},{10,11... | collective-permute-start | bytes 983048 | tf_op jit(solution)/shard_map/ppermute | solution.py:344
  38.2 10.8 %collective-permute-start.1 = (bf16[8,80,256]{2,1,0:T(8,128)(2,1)S(1)}, bf16[8,80,256]{2,1,0:T(8,128)(2,1)S(1)}, u32[]{:S(2)}, u32[]{:S(2)}) collective-permute-start(bf16[8,80,256]{2,1,0:T(8,128)(2,1)S(1)} %slice.16.own_ref.a_ref), channel_id=1, source_target_pairs={{0,16},{16,0},{1,17},{17,1},{2,18},{18,2},{3,19},{19,3},{4,20},{20... | collective-permute-start | bytes 983048 | tf_op jit(solution)/shard_map/ppermute | solution.py:344
  41.2 2.2 %copy-start = (bf16[8192,256]{1,0:T(8,128)(2,1)S(1)}, bf16[8192,256]{1,0:T(8,128)(2,1)}, u32[]{:S(2)}) copy-start(bf16[8192,256]{1,0:T(8,128)(2,1)} %param.18) | copy-start | bytes 12582916
  43.3 8.6 %copy-start.1 = (bf16[8192,256]{1,0:T(8,128)(2,1)S(1)}, bf16[8192,256]{1,0:T(8,128)(2,1)}, u32[]{:S(2)}) copy-start(bf16[8192,256]{1,0:T(8,128)(2,1)} %param.18) | copy-start | bytes 12582916
  49.0 2.9 %collective-permute-start.4 = (bf16[8,80,256]{2,1,0:T(8,128)(2,1)S(1)}, bf16[8,80,256]{2,1,0:T(8,128)(2,1)S(1)}, u32[]{:S(2)}, u32[]{:S(2)}) collective-permute-start(bf16[8,80,256]{2,1,0:T(8,128)(2,1)S(1)} %collective-permute-done.1.own_ref.b_ref), channel_id=1, source_target_pairs={{0,1},{1,0},{2,3},{3,2},{4,5},{5,4},{6,7},{7,6},{8,9},{9,8},{10,11... | collective-permute-start | bytes 983048 | tf_op jit(solution)/shard_map/ppermute | solution.py:344
  49.9 12.2 %collective-permute-start.8 = (bf16[8,96,256]{2,1,0:T(8,128)(2,1)S(1)}, bf16[8,96,256]{2,1,0:T(8,128)(2,1)S(1)}, u32[]{:S(2)}, u32[]{:S(2)}) collective-permute-start(bf16[8,96,256]{2,1,0:T(8,128)(2,1)S(1)} %slice.17.w0_ref), channel_id=1, source_target_pairs={{0,64},{32,96},{64,0},{96,32},{1,65},{33,97},{65,1},{97,33},{2,66}... | collective-permute-start | bytes 1179656 | tf_op jit(solution)/shard_map/ppermute | solution.py:344
  51.9 29.2 %copy-start.10 = (f32[96]{0:T(128)S(1)}, f32[96]{0:T(128)}, u32[]{:S(2)}) copy-start(f32[96]{0:T(128)} %param.28) | copy-start | bytes 1156
  51.9 29.2 %copy-start.11 = (f32[96]{0:T(128)S(1)}, f32[96]{0:T(128)}, u32[]{:S(2)}) copy-start(f32[96]{0:T(128)} %param.29) | copy-start | bytes 1156
  55.0 5.8 %collective-permute-start.5 = (bf16[216,256]{1,0:T(8,128)(2,1)S(1)}, bf16[216,256]{1,0:T(8,128)(2,1)S(1)}, u32[]{:S(2)}, u32[]{:S(2)}) collective-permute-start(bf16[216,256]{1,0:T(8,128)(2,1)S(1)} %get-tuple-element.30.a_ref), channel_id=1, source_target_pairs={{0,16},{16,0},{1,17},{17,1},{2,18},{18,2},{3,19},{19,3},{4,20},{20... | collective-permute-start | bytes 331784 | tf_op jit(solution)/shard_map/ppermute | solution.py:344
  57.9 4.1 %collective-permute-start.6 = (bf16[216,256]{1,0:T(8,128)(2,1)S(1)}, bf16[216,256]{1,0:T(8,128)(2,1)S(1)}, u32[]{:S(2)}, u32[]{:S(2)}) collective-permute-start(bf16[216,256]{1,0:T(8,128)(2,1)S(1)} %get-tuple-element.30.a_ref), channel_id=1, source_target_pairs={{0,1},{1,0},{2,3},{3,2},{4,5},{5,4},{6,7},{7,6},{8,9},{9,8},{10,11... | collective-permute-start | bytes 331784 | tf_op jit(solution)/shard_map/ppermute | solution.py:344
  60.8 2.2 %collective-permute-start.7 = (bf16[216,256]{1,0:T(8,128)(2,1)S(1)}, bf16[216,256]{1,0:T(8,128)(2,1)S(1)}, u32[]{:S(2)}, u32[]{:S(2)}) collective-permute-start(bf16[216,256]{1,0:T(8,128)(2,1)S(1)} %collective-permute-done.5.b_ref), channel_id=1, source_target_pairs={{0,1},{1,0},{2,3},{3,2},{4,5},{5,4},{6,7},{7,6},{8,9},{9,8},{10,11... | collective-permute-start | bytes 331784 | tf_op jit(solution)/shard_map/ppermute | solution.py:344
  99.7 2.7 %collective-permute-start.9 = (f32[2,216,256]{2,1,0:T(8,128)S(1)}, f32[2,216,256]{2,1,0:T(8,128)S(1)}, u32[]{:S(2)}, u32[]{:S(2)}) collective-permute-start(f32[2,216,256]{2,1,0:T(8,128)S(1)} %get-tuple-element.37), channel_id=1, source_target_pairs={{0,1},{1,0},{2,3},{3,2},{4,5},{5,4},{6,7},{7,6},{8,9},{9,8},{10,11... | collective-permute-start | bytes 1327112 | tf_op jit(solution)/shard_map/ppermute | solution.py:344
  102.5 5.9 %collective-permute-start.10 = (bf16[216,256]{1,0:T(8,128)(2,1)S(1)}, bf16[216,256]{1,0:T(8,128)(2,1)S(1)}, u32[]{:S(2)}, u32[]{:S(2)}) collective-permute-start(bf16[216,256]{1,0:T(8,128)(2,1)S(1)} %fusion.1), channel_id=1, source_target_pairs={{0,16},{16,0},{1,17},{17,1},{2,18},{18,2},{3,19},{19,3},{4,20},{20... | collective-permute-start | bytes 331784 | tf_op jit(solution)/shard_map/ppermute | solution.py:344
  108.4 37.3 %copy-start.7 = (f32[256]{0:T(256)S(1)}, f32[256]{0:T(256)}, u32[]{:S(2)}) copy-start(f32[256]{0:T(256)} %param.22) | copy-start | bytes 3076
  112.1 2.1 %collective-permute-start.11 = (f32[16,256]{1,0:T(8,128)S(1)}, f32[16,256]{1,0:T(8,128)S(1)}, u32[]{:S(2)}, u32[]{:S(2)}) collective-permute-start(f32[16,256]{1,0:T(8,128)S(1)} %get-tuple-element.40), channel_id=1, source_target_pairs={{0,1},{1,0},{2,3},{3,2},{4,5},{5,4},{6,7},{7,6},{8,9},{9,8},{10,11... | collective-permute-start | bytes 49160 | tf_op jit(solution)/shard_map/ppermute | solution.py:344
  141.9 3.8 %collective-permute-start.12 = (f32[8,256]{1,0:T(8,128)S(1)}, f32[8,256]{1,0:T(8,128)S(1)}, u32[]{:S(2)}, u32[]{:S(2)}) collective-permute-start(f32[8,256]{1,0:T(8,128)S(1)} %get-tuple-element.41.mine_ref), channel_id=1, source_target_pairs={{0,1},{1,0},{2,3},{3,2},{4,5},{5,4},{6,7},{7,6},{8,9},{9,8},{10,11... | collective-permute-start | bytes 24584 | tf_op jit(solution)/shard_map/ppermute | solution.py:344

commit v4 on v3

v4 whole, which is shorter than its diff:
```python
import functools

import jax
import jax.numpy as jnp
from jax import lax
from jax.experimental import pallas as pl
from jax.experimental.pallas import tpu as pltpu
from jax.sharding import Mesh
from jax.sharding import PartitionSpec as P

HIDDEN_SIZE = 8192
CLASSES = 10
GROUP = 8
LANES = 256
LIMIT = 16 * 1024 * 1024

grid_step = 0.0625
step_rate = 0.25
epsilon = 1e-06

ROWS_ALL = 72
CLASS_ROWS = ((0, 30, 2), (2, 59, 5), (7, 64, 3))

DOM = ("ylo", "x")
NEU = ("yhi", "z", "core")
F32, BF16 = jnp.float32, jnp.bfloat16


def spread(per_domain):
    count, width = per_domain.shape
    return jnp.broadcast_to(per_domain[:, None, :], (count, GROUP, width)).reshape(
        count * GROUP, width
    )


def contract(left, right, left_dim, right_dim):
    return lax.dot_general(
        left, right, (((left_dim,), (right_dim,)), ((), ())), preferred_element_type=F32
    )


def selector(label, offset):
    second = label + offset
    second = jnp.where(second >= CLASSES, second - CLASSES, second)
    rows = lax.broadcasted_iota(jnp.int32, (ROWS_ALL, label.shape[1]), 0)
    classes = jnp.full_like(rows, -1)
    for first, at, count in CLASS_ROWS:
        classes = jnp.where((rows >= at) & (rows < at + count), rows - at + first, classes)
    picked = jnp.where(classes == label, 1.0, 0.0) - jnp.where(classes == second, 1.0, 0.0)
    return picked.astype(BF16)


def pieces(values):
    high = lax.reduce_precision(values, 8, 7)
    middle = lax.reduce_precision(values - high, 8, 7)
    return high, middle, (values - high) - middle


def clamped(status, low, up):
    active, unsplit = status == 1, status == 2
    up = jnp.where(unsplit, up, jnp.where(active, 1, 0)).astype(F32)
    low = jnp.where(unsplit, low, jnp.where(active, 0, 1)).astype(F32)
    return low, up


def compose(low, up, classes, slopes):
    return jnp.concatenate(
        [up, *pieces(slopes), classes[0:2], low, classes[2:10], jnp.zeros((5, LANES), F32)], axis=0
    ).astype(BF16)


def decode(block, domains):
    wide = block.astype(F32)
    up, low = wide[0:32][:domains], wide[32:64][:domains]
    slope = wide[27:28] + wide[28:29] + wide[29:30]
    ratio = up / (up + low)
    unsplit = (up > 0.0) & (low > 0.0)
    return up, low, ratio, slope, unsplit


def relax_rows(coeffs, status, low, up, slopes):
    ratio = up / (up + low)
    cept = ratio * (low * grid_step)
    unsplit = status == 2
    fixed = jnp.where(status == 1, 1.0, 0.0)
    at_pos = spread(jnp.where(unsplit, jnp.broadcast_to(slopes, ratio.shape), fixed))
    at_neg = spread(jnp.where(unsplit, ratio, fixed))
    off_neg = spread(jnp.where(unsplit, cept, 0.0))
    on_pos = spread(jnp.where(unsplit, 1.0, 0.0))
    positive = coeffs >= 0.0
    factor = jnp.where(positive, at_pos, at_neg)
    offset = jnp.where(positive, 0.0, off_neg)
    chosen = jnp.where(positive, on_pos, 0.0)
    return factor, offset, chosen


def prep_kernel(status_ref, bounds_ref, class_ref, slopes_ref, weight_ref, out_ref, status, bounds, sems):
    x = lax.axis_index("x")
    count, feats = out_ref.shape[0], weight_ref.shape[0]
    firsts = [
        pltpu.make_async_copy(status_ref, status, sems.at[count]),
        pltpu.make_async_copy(bounds_ref, bounds, sems.at[count + 1]),
    ]
    copies = [
        pltpu.make_async_copy(
            weight_ref.at[:, pl.ds(pl.multiple_of(((x // 2 * count + k) * 2 + x % 2) * LANES, LANES), LANES)],
            out_ref.at[k, pl.ds(0, feats)],
            sems.at[k],
        )
        for k in range(count)
    ]
    for copy in firsts + copies:
        copy.start()
    for copy in firsts:
        copy.wait()
    low, up = clamped(status[...], bounds[:, 0], bounds[:, 1])
    info = compose(low, up, class_ref[...].astype(F32), slopes_ref[...])
    for k in range(count):
        out_ref[k, feats : feats + ROWS_ALL] = info
    for copy in copies:
        copy.wait()


def forward_half(label_ref, offset_ref, own_ref, other_ref, weight_ref, total):
    core = lax.axis_index("core")
    domains = label_ref.shape[1] // GROUP
    select = selector(label_ref[...], offset_ref[...])
    acc = total[...]
    for k in range(own_ref.shape[0]):
        for ref, side in ((own_ref, core), (other_ref, 1 - core)):
            block = ref[k]
            _, _, ratio, slope, unsplit = decode(block, domains)
            coeffs = contract(select, block, 0, 0)
            at_pos = jnp.where(unsplit, jnp.broadcast_to(slope, ratio.shape), ratio)
            factor = jnp.where(coeffs >= 0.0, spread(at_pos), spread(ratio))
            sent = (coeffs * factor).astype(BF16)
            acc = acc + jnp.dot(sent, weight_ref[0, k, side], preferred_element_type=F32)
    total[...] = acc


def own_kernel(label_ref, offset_ref, info_ref, bias_ref, const_ref, extra_ref):
    domains = label_ref.shape[1] // GROUP
    block = info_ref[lax.axis_index("z")]
    _, low, ratio, slope, unsplit = decode(block, domains)
    coeffs = contract(selector(label_ref[...], offset_ref[...]), block, 0, 0)
    at_pos = jnp.where(unsplit, jnp.broadcast_to(slope, ratio.shape), ratio)
    positive = coeffs >= 0.0
    sent = (coeffs * jnp.where(positive, spread(at_pos), spread(ratio))).astype(BF16)
    cept = spread(jnp.where(unsplit, ratio * (low * grid_step), 0.0))
    const_ref[...] = row_sums(sent.astype(F32) * bias_ref[...] + jnp.where(positive, 0.0, coeffs * cept))
    kept = jnp.maximum(coeffs, 0.0) * spread(jnp.where(unsplit, 1.0, 0.0))
    extra_ref[...] = jnp.sum(kept, axis=0, keepdims=True) * bias_ref[...]


def near_kernel(label_ref, offset_ref, own_ref, other_ref, weight_ref, total_ref):
    @pl.when(pl.program_id(0) == 0)
    def _():
        total_ref[...] = jnp.zeros_like(total_ref)

    forward_half(label_ref, offset_ref, own_ref, other_ref, weight_ref, total_ref)


def far_kernel(
    label_ref, offset_ref, own_ref, other_ref, weight_ref, so_far_ref, own_const_ref,
    status_ref, bounds_ref, slopes_ref, bias_ref, sent_ref, coeffs_ref, const_ref, total,
):
    @pl.when(pl.program_id(0) == 0)
    def _():
        total[...] = so_far_ref[...]

    forward_half(label_ref, offset_ref, own_ref, other_ref, weight_ref, total)

    @pl.when(pl.program_id(0) == pl.num_programs(0) - 1)
    def _():
        coeffs = total[...]
        factor, offset, _ = relax_rows(
            coeffs, status_ref[...], bounds_ref[:, 0].astype(F32), bounds_ref[:, 1].astype(F32), slopes_ref[...]
        )
        sent = (coeffs * factor).astype(BF16)
        sent_ref[...] = sent
        coeffs_ref[...] = coeffs
        const_ref[...] = own_const_ref[...] + row_sums(sent.astype(F32) * bias_ref[...] + coeffs * offset)


def row_sums(values):
    return lax.dot_general(
        jnp.ones((8, values.shape[1]), F32), values, (((1,), (1,)), ((), ())),
        precision=lax.Precision.HIGHEST, preferred_element_type=F32,
    )


def hold(held, refs, own):
    for place, ref in enumerate(refs):
        held[own ^ ((place % 2) * 2 + place // 2)] = ref[...]


SHIFTS = (0, 1, 3, 2)


def input_kernel(a_ref, b_ref, c_ref, d_ref, w0_ref, w1_ref, w2_ref, w3_ref, out_ref, held):
    own, x = lax.axis_index("yhi") * 2 + lax.axis_index("core"), lax.axis_index("x")
    hold(held, (a_ref, b_ref, c_ref, d_ref), own)
    zs, feats, _ = w0_ref.shape
    acc = None
    for by, ref in zip(SHIFTS, (w0_ref, w1_ref, w2_ref, w3_ref)):
        part = contract(ref[...].reshape(zs * feats, LANES), held[(x + 4 - by) % 4], 1, 1)
        acc = part if acc is None else acc + part
    out_ref[...] = acc.reshape(zs, feats, acc.shape[1]).astype(BF16)


def column(row):
    count = row.shape[1]
    down = lax.broadcasted_iota(jnp.int32, (count, count), 0)
    across = lax.broadcasted_iota(jnp.int32, (count, count), 1)
    return jnp.sum(jnp.where(down == across, row, 0.0), axis=1, keepdims=True)


def box_kernel(parts_ref, center_ref, radius_ref, const_ref, grads_ref, bound_ref):
    coeffs = parts_ref[0].astype(F32)
    for k in range(1, parts_ref.shape[0]):
        coeffs = coeffs + parts_ref[k].astype(F32)
    center, radius = column(center_ref[...]), column(radius_ref[...])
    wide = center - jnp.where(coeffs > 0.0, radius, jnp.where(coeffs < 0.0, -radius, 0.0))
    grads = wide.astype(BF16)
    for k in range(grads_ref.shape[0]):
        grads_ref[k] = grads
    rest = coeffs * (wide - grads.astype(F32))
    bound_ref[...] = jnp.sum(rest, axis=0, keepdims=True) + const_ref[0:1]


def grads_kernel(
    g_ref, w0_ref, w1_ref, w2_ref, w3_ref, a_ref, b_ref, c_ref, d_ref, so_far_ref,
    near_ref, far_ref, back_ref, held,
):
    own, x = lax.axis_index("yhi") * 2 + lax.axis_index("core"), lax.axis_index("x")
    hold(held, (a_ref, b_ref, c_ref, d_ref), own)
    zs, feats, rows = g_ref.shape
    grads = g_ref[...].reshape(zs * feats, rows)
    terms = None
    for by, ref in zip(SHIFTS, (w0_ref, w1_ref, w2_ref, w3_ref)):
        q = (x + 4 - by) % 4
        part = contract(grads, ref[...].reshape(zs * feats, LANES), 0, 0)
        term = part * held[q].astype(F32)
        terms = term if terms is None else terms + term
        place = own ^ q

        @pl.when(place == 0)
        def _():
            near_ref[...] = part

        @pl.when(place == 2)
        def _():
            far_ref[0:rows] = part

        @pl.when(place % 2 == 1)
        def _():
            back_ref[place // 2, 0:rows] = part

    bound = row_sums(terms) + so_far_ref[...]
    for ref in (far_ref, back_ref.at[1]):
        ref[rows : rows + 8] = jnp.zeros((8, LANES), F32)
        ref[rows : rows + 8, 0:rows] = bound
    back_ref[0, rows : rows + 8] = jnp.zeros((8, LANES), F32)


def their_kernel(far_ref, got_ref, out_ref, bound_ref):
    rows = far_ref.shape[0] - 8
    total = far_ref[...] + got_ref[1]
    bound_ref[...] = total[rows : rows + 8]
    tail = jnp.concatenate([*pieces(total[rows : rows + 1]), jnp.zeros((5, LANES), F32)], axis=0)
    out_ref[...] = jnp.concatenate([total[0:rows], tail], axis=0).astype(BF16)


def backward_kernel(
    label_ref, offset_ref, a_ref, b_ref, c_ref, d_ref, weight_ref, extra_ref,
    status_ref, bounds_ref, slopes_ref, bias_ref, coeffs_ref, near_ref, got_ref, their_ref, bound_ref,
    mine_ref, other_ref, back,
):
    step = pl.program_id(0)
    yhi, z, core = (lax.axis_index(n) for n in NEU)
    domains = status_ref.shape[0]
    select = selector(label_ref[...], offset_ref[...])

    @pl.when(step == 0)
    def _():
        coeffs = coeffs_ref[...]
        rows = coeffs.shape[0]
        their = their_ref[...].astype(F32)
        grads = near_ref[...] + got_ref[0, 0:rows] + their[0:rows] + bias_ref[...]
        factor, offset, chosen = relax_rows(
            coeffs, status_ref[...], bounds_ref[:, 0].astype(F32), bounds_ref[:, 1].astype(F32), slopes_ref[...]
        )
        back[...] = (grads * factor + offset).astype(BF16)
        mine_ref[16:24] = jnp.zeros((8, LANES), F32)
        mine_ref[16:17] = jnp.sum(grads * coeffs * chosen, axis=0, keepdims=True)
        mine_ref[17:18] = bound_ref[0:1] + their[rows : rows + 1] + their[rows + 1 : rows + 2] + their[rows + 2 : rows + 3]

    zs = a_ref.shape[0]
    for k in range(zs):
        for place, ref in enumerate((a_ref, b_ref, c_ref, d_ref)):
            y = yhi if place % 2 == 0 else 1 - yhi
            c = core if place // 2 == 0 else 1 - core
            block = ref[k]
            _, _, _, _, unsplit = decode(block, domains)
            coeffs = contract(select, block, 0, 0)
            kept = jnp.maximum(coeffs, 0.0) * spread(jnp.where(unsplit, 1.0, 0.0))
            grads = contract(back[...], weight_ref[y, k, c], 1, 1)
            summed = jnp.sum(grads * kept, axis=0, keepdims=True)
            if place == 0:
                summed = summed + jnp.where(step * zs + k == z, 1.0, 0.0) * extra_ref[...]
            out = mine_ref if place // 2 == 0 else other_ref
            out[pl.ds(y * 8 + step * zs + k, 1)] = summed


def send_z_kernel(mine_ref, got_ref, out_ref):
    deep = mine_ref[0:16] + got_ref[...]
    rest = mine_ref[16:24]
    for k in range(out_ref.shape[0]):
        out_ref[k, 0:16] = deep
        out_ref[k, 16:24] = rest


def send_dom_kernel(got_ref, out_ref, bound_ref):
    total = got_ref[0]
    for k in range(1, got_ref.shape[0]):
        total = total + got_ref[k]
    bound_ref[...] = total[17:18, 0 : bound_ref.shape[1]]
    first = jnp.concatenate([got_ref[k, 16:17] for k in range(got_ref.shape[0])], axis=0)
    for k in range(out_ref.shape[0]):
        out_ref[k, 0:16] = total[0:16]
        out_ref[k, 16:24] = first


def send_core_kernel(got_ref, out_ref, deep_ref, first_ref):
    yhi = lax.axis_index("yhi")
    halves = []
    for y in range(2):
        total = got_ref[y]
        for k in range(1, got_ref.shape[0] // 2):
            total = total + got_ref[2 * k + y]
        halves.append(total)
    deep = halves[0][0:16] + halves[1][0:16]
    deep_ref[...] = deep
    firsts = [half[16:24] for half in halves]
    first_ref[...] = jnp.where(yhi == 0, firsts[0], firsts[1])
    power = jnp.sum(firsts[0] * firsts[0] + firsts[1] * firsts[1], keepdims=True)
    out_ref[0:4] = jnp.broadcast_to(power, (4, LANES))
    out_ref[4:8] = jnp.broadcast_to(jnp.sum(deep * deep, keepdims=True), (4, LANES))


def finish_kernel(mine_ref, got_ref, deep_ref, first_ref, deep_slopes_ref, first_slopes_ref, first_out, deep_out):
    yhi, z = lax.axis_index("yhi"), lax.axis_index("z")
    total = mine_ref[...] + got_ref[...]

    def advance(slopes, gradient, squares):
        root_mean = jnp.sqrt(squares / HIDDEN_SIZE + epsilon)
        return jnp.clip(slopes + step_rate * gradient / root_mean, 0.0, 1.0)

    first_out[...] = advance(first_slopes_ref[...], first_ref[pl.ds(z, 1)], total[0:1])
    deep_out[...] = advance(deep_slopes_ref[...], deep_ref[pl.ds(yhi * 8 + z, 1)], total[4:5])


def whole(shape):
    return pl.BlockSpec(shape, lambda s: (0,) * len(shape))


def shape(dims, kind=F32):
    return jax.ShapeDtypeStruct(dims, kind)


def shifted(value, axis, size, by):
    return lax.ppermute(value, axis, [(i, (i + by) % size) for i in range(size)])


def on_device(
    spec_label, spec_offset, class_rows, deep_weight, deep_bias, deep_status, deep_bounds,
    deep_slopes, first_weight, first_bias, first_status, first_bounds, first_slopes,
    box_center, box_radius,
):
    rows = spec_label.shape[0]
    domains = deep_status.shape[0]
    feats = box_center.shape[0]
    call = functools.partial(
        pl.pallas_call, compiler_params=pltpu.CompilerParams(vmem_limit_bytes=LIMIT)
    )
    vmem, hbm = pl.BlockSpec(), pl.BlockSpec(memory_space=pltpu.HBM)

    message = pl.pallas_call(
        prep_kernel,
        compiler_params=pltpu.CompilerParams(vmem_limit_bytes=58 * 1024 * 1024),
        in_specs=[hbm, hbm, vmem, vmem, hbm],
        out_shape=shape((8, feats + ROWS_ALL, LANES), BF16),
        scratch_shapes=[
            pltpu.VMEM((domains, LANES), jnp.int32),
            pltpu.VMEM((domains, 2, LANES), jnp.int32),
            pltpu.SemaphoreType.DMA((10,)),
        ],
        name="prep",
    )(deep_status, deep_bounds.transpose(1, 0, 2), class_rows, deep_slopes[None], first_weight.T)
    message = lax.all_to_all(message, "z", 0, 0, tiled=True)
    info_a = message[:, feats:]
    info_b = shifted(info_a, "yhi", 2, 1)
    info_c = shifted(info_a, "core", 2, 1)
    info_c, w_own = lax.optimization_barrier((info_c, message[:, :feats]))
    w_all = [w_own, shifted(w_own, "x", 4, 1), shifted(w_own, "x", 4, 3)]

    label, offset = spec_label[None], spec_offset[None]
    weight = deep_weight.reshape(2, 8, 2, LANES, LANES)
    depth = 2
    info_spec = pl.BlockSpec((depth, ROWS_ALL, LANES), lambda s: (s, 0, 0))
    label_specs = [whole((1, rows))] * 2
    layer_specs = [whole((domains, LANES)), whole((domains, 2, LANES)), whole((1, LANES)), whole((1, LANES))]
    layer = (first_status, first_bounds.transpose(1, 0, 2), first_slopes[None], first_bias[None])
    half_spec = lambda other: pl.BlockSpec(
        (1, depth, 2, LANES, LANES), lambda s: (lax.axis_index("yhi") ^ other, s, 0, 0, 0)
    )
    square = whole((rows, LANES))

    total = call(
        near_kernel,
        grid=(8 // depth,),
        in_specs=label_specs + [info_spec] * 2 + [half_spec(0)],
        out_specs=square,
        out_shape=shape((rows, LANES)),
        name="forward_near",
    )(label, offset, info_a, info_c, weight)
    own_const, extra = call(
        own_kernel, out_shape=[shape((8, rows)), shape((1, LANES))], name="own"
    )(label, offset, info_a, deep_bias[None])
    total, own_const, info_b = lax.optimization_barrier((total, own_const, info_b))
    info_d = shifted(info_b, "core", 2, 1)
    info_d, w_all[2] = lax.optimization_barrier((info_d, w_all[2]))
    w_all.append(shifted(w_all[2], "x", 4, 3))
    sent, coeffs, const = call(
        far_kernel,
        grid=(8 // depth,),
        in_specs=label_specs + [info_spec] * 2 + [half_spec(1), square, whole((8, rows))] + layer_specs,
        out_specs=[square, square, whole((8, rows))],
        out_shape=[shape((rows, LANES), BF16), shape((rows, LANES)), shape((8, rows))],
        scratch_shapes=[pltpu.VMEM((rows, LANES), F32)],
        name="forward_far",
    )(label, offset, info_b, info_d, weight, total, own_const, *layer)

    sent_b = shifted(sent, "yhi", 2, 1)
    sent_c = shifted(sent, "core", 2, 1)
    sent_d = shifted(sent_b, "core", 2, 1)
    sents = (sent, sent_b, sent_c, sent_d)
    held = [pltpu.VMEM((4, rows, LANES), BF16)]
    parts = call(
        input_kernel, out_shape=shape((8, feats, rows), BF16), scratch_shapes=held, name="inputs"
    )(*sents, *w_all)
    parts = lax.all_to_all(parts, "z", 0, 0, tiled=True)
    grads, bound = call(
        box_kernel, out_shape=[shape((8, feats, rows), BF16), shape((1, rows))], name="box"
    )(parts, box_center[None], box_radius[None], const)
    grads = lax.all_to_all(grads, "z", 0, 0, tiled=True)
    near, far, back = call(
        grads_kernel,
        out_shape=[shape((rows, LANES)), shape((rows + 8, LANES)), shape((2, rows + 8, LANES))],
        scratch_shapes=held,
        name="grads",
    )(grads, *w_all, *sents, bound)
    got = shifted(back, "core", 2, 1)
    their, bound = call(
        their_kernel, out_shape=[shape((rows + 8, LANES), BF16), shape((8, LANES))], name="their"
    )(far, got)
    their = shifted(their, "yhi", 2, 1)

    mine, other = call(
        backward_kernel,
        grid=(8 // depth,),
        in_specs=label_specs
        + [info_spec] * 4
        + [pl.BlockSpec((2, depth, 2, LANES, LANES), lambda s: (0, s, 0, 0, 0)), whole((1, LANES))]
        + layer_specs
        + [square, square, pl.BlockSpec((1, rows + 8, LANES), lambda s: (0, 0, 0)), whole((rows + 8, LANES)), whole((8, LANES))],
        out_specs=[whole((24, LANES)), whole((16, LANES))],
        out_shape=[shape((24, LANES)), shape((16, LANES))],
        scratch_shapes=[pltpu.VMEM((rows, LANES), BF16)],
        name="backward",
    )(label, offset, info_a, info_b, info_c, info_d, weight, extra, *layer, coeffs, near, got, their, bound)

    to_z = call(send_z_kernel, out_shape=shape((8, 24, LANES)), name="send_z")(mine, shifted(other, "core", 2, 1))
    got = lax.all_to_all(to_z, "z", 0, 0, tiled=True)
    to_dom, bound = call(
        send_dom_kernel, out_shape=[shape((16, 24, LANES)), shape((1, rows))], name="send_dom"
    )(got)
    got = lax.all_to_all(to_dom, DOM + ("yhi",), 0, 0, tiled=True)
    to_core, deep, first = call(
        send_core_kernel,
        out_shape=[shape((8, LANES)), shape((16, LANES)), shape((8, LANES))],
        name="send_core",
    )(got)
    first_next, deep_next = call(
        finish_kernel, out_shape=[shape((1, LANES)), shape((1, LANES))], name="finish"
    )(to_core, shifted(to_core, "core", 2, 1), deep, first, deep_slopes[None], first_slopes[None])
    return bound[0], first_next[0], deep_next[0]


def solution(mesh):
    fine = Mesh(mesh.devices.reshape(2, 4, 2, 8, 2), DOM + NEU)
    in_specs = (
        P(DOM), P(DOM), P(None, NEU), P(None, NEU), P(NEU), P(DOM, NEU), P(None, DOM, NEU), P(NEU),
        P(None, NEU), P(NEU), P(DOM, NEU), P(None, DOM, NEU), P(NEU), P(NEU), P(NEU),
    )
    out_specs = (P(DOM), P(NEU), P(NEU))
    return jax.shard_map(on_device, mesh=fine, in_specs=in_specs, out_specs=out_specs, check_vma=False)
```

time: 147 us -> 144 us (0.980)
  blocking collectives: 91 us -> 86.5 us
  waiting for transfers between devices: 11.3 us -> 14.1 us
  local copies, waits for them, and re-layouts: 2.29 us -> 0.1 us
    all_to_all x1, blocking collectives: 14.9 us -> 11.1 us  [on_device(): got = lax.all_to_all(to_dom, DOM + ('yhi',), 0, 0, tiled=True)]
    ppermute x13, waiting for transfers between devices: 11.3 us -> 14.1 us  [shifted(): lax.ppermute(value, axis, [(i, (i + by) % size) for i in range(size)])]
    unnamed x24 -> x22, local copies, waits for them, and re-layouts: 2.24 us -> 0.06 us
    pallas_call x3 -> x5, Pallas kernels: 2.37 us -> 3.48 us  [the longest x1 1.75 us: on_device(): call(grads_kernel, out_shape=[shape((rows, LANES)), shape((rows + 8, LANE...]
where the time goes in v4:
time: 144 us
  blocking collectives  86.5 us (60%)
  starting transfers between devices  25.4 us (18%)
  Pallas kernels  16.8 us (12%)
  waiting for transfers between devices  14.1 us (10%)
    all_to_all x1, blocking collectives, on_device(): message = lax.all_to_all(message, 'z', 0, 0, tiled=True)  28.6 us
    ppermute x13, starting transfers between devices, shifted(): lax.ppermute(value, axis, [(i, (i + by) % size) for i in range(size)])  25.4 us
    all_to_all x1, blocking collectives, on_device(): parts = lax.all_to_all(parts, 'z', 0, 0, tiled=True)  17.5 us
    all_to_all x1, blocking collectives, on_device(): grads = lax.all_to_all(grads, 'z', 0, 0, tiled=True)  16.7 us
    ppermute x13, waiting for transfers between devices, shifted(): lax.ppermute(value, axis, [(i, (i + by) % size) for i in range(size)])  14.1 us
    all_to_all x1, blocking collectives, on_device(): got = lax.all_to_all(to_z, 'z', 0, 0, tiled=True)  12.6 us
    all_to_all x1, blocking collectives, on_device(): got = lax.all_to_all(to_dom, DOM + ('yhi',), 0, 0, tiled=True)  11.1 us
    pallas_call x1, Pallas kernels, on_device(): call(backward_kernel, grid=(8 // depth,), in_specs=label_specs + [info_sp...  3.62 us
  transfers between devices with their start and end apart: 13, of which 8 were waited for; matrix products, arithmetic and copies ran while one was open for 0% of the time, Pallas kernels for 4%

profile of v4, /device:TPU:1, one launch (start us, length us, event | category | flops | bytes accessed | tf_op | source)
XLA Modules:
  0.0 143.8 jit_solution(2693900658990832729)
XLA Ops:
  0.7 3.2 %prep.1 = bf16[8,168,256]{2,1,0:T(8,128)(2,1)} custom-call(s32[27,256]{1,0:T(8,128)} %status_ref.3, s32[27,2,256]{2,1,0:T(2,128)} %bitcast.39, bf16[10,256]{1,0:T(8,128)(2,1)} %class_ref.1, f32[1,256]{1,0:T(1,128)} %bitcast.31, bf16[96,8192]{1,0:T(8,128)(2,1)} %bitcast.38), custom_call_target="tpu_custom_call" | custom-call | tf_op jit(solution)/shard_map/prep/pallas_call | solution.py:388
  4.0 28.6 %all_to_all.25 = bf16[8,168,256]{2,1,0:T(8,128)(2,1)S(1)} all-to-all(bf16[8,168,256]{2,1,0:T(8,128)(2,1)} %prep.1), channel_id=1, replica_groups=mesh['ylo'=2,'x'=4,'yhi'=2,'z'=8,'core'=2] {'z'}, dimensions={0} | all-to-all | bytes 1376256 | tf_op jit(solution)/shard_map/all_to_all | solution.py:400
  32.6 2.6 %collective-permute-start = (bf16[8,72,256]{2,1,0:T(8,128)(2,1)S(1)}, bf16[8,72,256]{2,1,0:T(8,128)(2,1)S(1)}, u32[]{:S(2)}, u32[]{:S(2)}) collective-permute-start(bf16[8,72,256]{2,1,0:T(8,128)(2,1)S(1)} %slice.8.own_ref.info_ref.a_ref), channel_id=1, source_target_pairs={{0,1},{1,0},{2,3},{3,2},{4,5},{5,4},{6,7},{7,6},{8,9},{9,8},{10,11... | collective-permute-start | bytes 884744 | tf_op jit(solution)/shard_map/ppermute | solution.py:372
  35.2 2.9 %collective-permute-start.1 = (bf16[8,72,256]{2,1,0:T(8,128)(2,1)S(1)}, bf16[8,72,256]{2,1,0:T(8,128)(2,1)S(1)}, u32[]{:S(2)}, u32[]{:S(2)}) collective-permute-start(bf16[8,72,256]{2,1,0:T(8,128)(2,1)S(1)} %slice.8.own_ref.info_ref.a_ref), channel_id=1, source_target_pairs={{0,16},{16,0},{1,17},{17,1},{2,18},{18,2},{3,19},{19,3},{4,20},{20... | collective-permute-start | bytes 884744 | tf_op jit(solution)/shard_map/ppermute | solution.py:372
  38.2 2.6 %collective-permute-start.3 = (bf16[8,96,256]{2,1,0:T(8,128)(2,1)S(1)}, bf16[8,96,256]{2,1,0:T(8,128)(2,1)S(1)}, u32[]{:S(2)}, u32[]{:S(2)}) collective-permute-start(bf16[8,96,256]{2,1,0:T(8,128)(2,1)S(1)} %slice.9.w0_ref), channel_id=1, source_target_pairs={{0,96},{32,0},{64,32},{96,64},{1,97},{33,1},{65,33},{97,65},{2,98}... | collective-permute-start | bytes 1179656 | tf_op jit(solution)/shard_map/ppermute | solution.py:372
  41.3 2.6 %forward_near.1.so_far_ref = f32[216,256]{1,0:T(8,128)S(1)} custom-call(s32[1,216]{1,0:T(1,128)S(1)} %bitcast.21, s32[1,216]{1,0:T(1,128)S(1)} %bitcast.25, bf16[8,72,256]{2,1,0:T(8,128)(2,1)S(1)} %slice.8.own_ref.info_ref.a_ref, bf16[8,72,256]{2,1,0:T(8,128)(2,1)S(1)} %collective-permute-done.other_ref.c_ref, bf16[2,8,2,256,256]{4,3,2,1,0:T(8,128)(2,1)S(1)} %bitcast.15), custom_call_target="tpu_custom_call" | custom-call | tf_op jit(solution)/shard_map/forward_near/pallas_call | solution.py:419
  43.9 1.4 collective-permute-done.1.own_ref.b_ref
  45.3 0.9 collective-permute-start.2
  46.1 1.2 collective-permute-start.7
  47.4 1.5 %collective-permute-done.3.w2_ref = bf16[8,96,256]{2,1,0:T(8,128)(2,1)S(1)} collective-permute-done((bf16[8,96,256]{2,1,0:T(8,128)(2,1)S(1)}, bf16[8,96,256]{2,1,0:T(8,128)(2,1)S(1)}, u32[]{:S(2)}, u32[]{:S(2)}) %collective-permute-start.3) | collective-permute-done | bytes 393248 | tf_op jit(solution)/shard_map/ppermute | solution.py:372
  48.9 3.4 %collective-permute-start.8 = (bf16[8,96,256]{2,1,0:T(8,128)(2,1)S(1)}, bf16[8,96,256]{2,1,0:T(8,128)(2,1)S(1)}, u32[]{:S(2)}, u32[]{:S(2)}) collective-permute-start(bf16[8,96,256]{2,1,0:T(8,128)(2,1)S(1)} %collective-permute-done.3.w2_ref), channel_id=1, source_target_pairs={{0,96},{32,0},{64,32},{96,64},{1,97},{33,1},{65,33},{97,65},{2,98}... | collective-permute-start | bytes 1179656 | tf_op jit(solution)/shard_map/ppermute | solution.py:372
  52.3 3.0 %forward_far.1 = (bf16[216,256]{1,0:T(8,128)(2,1)S(1)}, f32[216,256]{1,0:T(8,128)S(1)}, f32[8,216]{1,0:T(8,128)S(1)}) custom-call(s32[1,216]{1,0:T(1,128)S(1)} %bitcast.22, s32[1,216]{1,0:T(1,128)S(1)} %bitcast.26, bf16[8,72,256]{2,1,0:T(8,128)(2,1)S(1)} %collective-permute-done.1.own_ref.b_ref, ...), custom_call_target="tpu_custom_call" | custom-call | tf_op jit(solution)/shard_map/forward_far/pallas_call | solution.py:434
  55.3 1.1 collective-permute-start.4
  56.4 1.8 %collective-permute-start.5 = (bf16[216,256]{1,0:T(8,128)(2,1)S(1)}, bf16[216,256]{1,0:T(8,128)(2,1)S(1)}, u32[]{:S(2)}, u32[]{:S(2)}) collective-permute-start(bf16[216,256]{1,0:T(8,128)(2,1)S(1)} %get-tuple-element.40.a_ref), channel_id=1, source_target_pairs={{0,1},{1,0},{2,3},{3,2},{4,5},{5,4},{6,7},{7,6},{8,9},{9,8},{10,11... | collective-permute-start | bytes 331784 | tf_op jit(solution)/shard_map/ppermute | solution.py:372
  58.1 2.3 %collective-permute-done.4.b_ref = bf16[216,256]{1,0:T(8,128)(2,1)S(1)} collective-permute-done((bf16[216,256]{1,0:T(8,128)(2,1)S(1)}, bf16[216,256]{1,0:T(8,128)(2,1)S(1)}, u32[]{:S(2)}, u32[]{:S(2)}) %collective-permute-start.4) | collective-permute-done | bytes 110624 | tf_op jit(solution)/shard_map/ppermute | solution.py:372
  60.4 2.6 %collective-permute-start.6 = (bf16[216,256]{1,0:T(8,128)(2,1)S(1)}, bf16[216,256]{1,0:T(8,128)(2,1)S(1)}, u32[]{:S(2)}, u32[]{:S(2)}) collective-permute-start(bf16[216,256]{1,0:T(8,128)(2,1)S(1)} %collective-permute-done.4.b_ref), channel_id=1, source_target_pairs={{0,1},{1,0},{2,3},{3,2},{4,5},{5,4},{6,7},{7,6},{8,9},{9,8},{10,11... | collective-permute-start | bytes 331784 | tf_op jit(solution)/shard_map/ppermute | solution.py:372
  63.0 1.0 collective-permute-done.6.d_ref
  64.0 0.6 inputs.1
  64.6 17.5 %all_to_all.26.parts_ref = bf16[8,96,216]{2,1,0:T(8,128)(2,1)S(1)} all-to-all(bf16[8,96,216]{2,1,0:T(8,128)(2,1)S(1)} %inputs.1), channel_id=1, replica_groups=mesh['ylo'=2,'x'=4,'yhi'=2,'z'=8,'core'=2] {'z'}, dimensions={0} | all-to-all | bytes 663552 | tf_op jit(solution)/shard_map/all_to_all | solution.py:452
  82.3 16.7 %all_to_all.27.g_ref = bf16[8,96,216]{2,1,0:T(8,128)(2,1)S(1)} all-to-all(bf16[8,96,216]{2,1,0:T(8,128)(2,1)S(1)} %get-tuple-element.43), channel_id=1, replica_groups=mesh['ylo'=2,'x'=4,'yhi'=2,'z'=8,'core'=2] {'z'}, dimensions={0} | all-to-all | bytes 663552 | tf_op jit(solution)/shard_map/all_to_all | solution.py:456
  99.0 1.7 %grads.1 = (f32[216,256]{1,0:T(8,128)S(1)}, f32[224,256]{1,0:T(8,128)S(1)}, f32[2,224,256]{2,1,0:T(8,128)S(1)}) custom-call(bf16[8,96,216]{2,1,0:T(8,128)(2,1)S(1)} %all_to_all.27.g_ref, bf16[8,96,256]{2,1,0:T(8,128)(2,1)S(1)} %slice.9.w0_ref, bf16[8,96,256]{2,1,0:T(8,128)(2,1)S(1)} %collective-permute-done.7.w1_ref, ...), custom_call_target="tpu_custom_call" | custom-call | tf_op jit(solution)/shard_map/grads/pallas_call | solution.py:457
  100.8 1.3 collective-permute-start.9
  102.1 1.4 %collective-permute-done.9.got_ref = f32[2,224,256]{2,1,0:T(8,128)S(1)} collective-permute-done((f32[2,224,256]{2,1,0:T(8,128)S(1)}, f32[2,224,256]{2,1,0:T(8,128)S(1)}, u32[]{:S(2)}, u32[]{:S(2)}) %collective-permute-start.9) | collective-permute-done | bytes 458784 | tf_op jit(solution)/shard_map/ppermute | solution.py:372
  103.6 1.2 collective-permute-start.10
  104.8 4.8 %collective-permute-done.10.their_ref = bf16[224,256]{1,0:T(8,128)(2,1)S(1)} collective-permute-done((bf16[224,256]{1,0:T(8,128)(2,1)S(1)}, bf16[224,256]{1,0:T(8,128)(2,1)S(1)}, u32[]{:S(2)}, u32[]{:S(2)}) %collective-permute-start.10) | collective-permute-done | bytes 114720 | tf_op jit(solution)/shard_map/ppermute | solution.py:372
  109.6 3.6 %backward.1 = (f32[24,256]{1,0:T(8,128)S(1)}, f32[16,256]{1,0:T(8,128)S(1)}) custom-call(s32[1,216]{1,0:T(1,128)S(1)} %bitcast.23, s32[1,216]{1,0:T(1,128)S(1)} %bitcast.27, bf16[8,72,256]{2,1,0:T(8,128)(2,1)S(1)} %slice.8.own_ref.info_ref.a_ref, bf16[8,72,256]{2,1,0:T(8,128)(2,1)S(1)} %collective-permute-done.1.own_ref.b_ref, ...), custom_call_target="tpu_custom_call" | custom-call | tf_op jit(solution)/shard_map/backward/pallas_call | solution.py:469
  113.2 1.3 collective-permute-start.11
  114.5 0.8 collective-permute-done.11.got_ref
  115.3 12.6 %all_to_all.28.got_ref = f32[8,24,256]{2,1,0:T(8,128)S(1)} all-to-all(f32[8,24,256]{2,1,0:T(8,128)S(1)} %send_z.1), channel_id=1, replica_groups=mesh['ylo'=2,'x'=4,'yhi'=2,'z'=8,'core'=2] {'z'}, dimensions={0} | all-to-all | bytes 393216 | tf_op jit(solution)/shard_map/all_to_all | solution.py:484
  128.5 11.1 %all_to_all.29.got_ref = f32[16,24,256]{2,1,0:T(8,128)S(1)} all-to-all(f32[16,24,256]{2,1,0:T(8,128)S(1)} %get-tuple-element.53), channel_id=1, replica_groups=mesh['ylo'=2,'x'=4,'yhi'=2,'z'=8,'core'=2] {'ylo','x','yhi'}, dimensions={0} | all-to-all | bytes 786432 | tf_op jit(solution)/shard_map/all_to_all | solution.py:488
  139.7 2.6 %collective-permute-start.12 = (f32[8,256]{1,0:T(8,128)S(1)}, f32[8,256]{1,0:T(8,128)S(1)}, u32[]{:S(2)}, u32[]{:S(2)}) collective-permute-start(f32[8,256]{1,0:T(8,128)S(1)} %get-tuple-element.54.mine_ref), channel_id=1, source_target_pairs={{0,1},{1,0},{2,3},{3,2},{4,5},{5,4},{6,7},{7,6},{8,9},{9,8},{10,11... | collective-permute-start | bytes 24584 | tf_op jit(solution)/shard_map/ppermute | solution.py:372
  142.3 0.8 collective-permute-done.12.got_ref
  (36 shorter events, 2.1 us)
Async XLA Ops:
  0.6 40.1 %copy-start.8 = (f32[256]{0:T(256)S(1)}, f32[256]{0:T(256)}, u32[]{:S(2)}) copy-start(f32[256]{0:T(256)} %param.19) | copy-start | bytes 3076
  0.6 40.1 %copy-start.4 = (s32[216]{0:T(256)S(1)}, s32[216]{0:T(256)}, u32[]{:S(2)}) copy-start(s32[216]{0:T(256)} %param.16) | copy-start | bytes 2596
  0.7 40.1 %copy-start.3 = (s32[216]{0:T(256)S(1)}, s32[216]{0:T(256)}, u32[]{:S(2)}) copy-start(s32[216]{0:T(256)} %param.15) | copy-start | bytes 2596
  0.7 40.6 %copy-start = (bf16[8192,256]{1,0:T(8,128)(2,1)S(1)}, bf16[8192,256]{1,0:T(8,128)(2,1)}, u32[]{:S(2)}) copy-start(bf16[8192,256]{1,0:T(8,128)(2,1)} %param.18) | copy-start | bytes 12582916
  3.9 48.4 %copy-start.1 = (s32[2,27,256]{2,0,1:T(2,128)S(1)}, s32[2,27,256]{2,0,1:T(2,128)}, u32[]{:S(2)}) copy-start(s32[2,27,256]{2,0,1:T(2,128)} %param.26) | copy-start | bytes 165892
  3.9 48.3 %copy-start.2 = (s32[27,256]{1,0:T(8,128)S(1)}, s32[27,256]{1,0:T(8,128)}, u32[]{:S(2)}) copy-start(s32[27,256]{1,0:T(8,128)} %status_ref.5) | copy-start | bytes 82948
  3.9 48.3 %copy-start.5 = (f32[256]{0:T(256)S(1)}, f32[256]{0:T(256)}, u32[]{:S(2)}) copy-start(f32[256]{0:T(256)} %param.27) | copy-start | bytes 3076
  4.0 48.3 %copy-start.7 = (f32[256]{0:T(256)S(1)}, f32[256]{0:T(256)}, u32[]{:S(2)}) copy-start(f32[256]{0:T(256)} %param.24) | copy-start | bytes 3076
  32.6 5.5 %collective-permute-start = (bf16[8,72,256]{2,1,0:T(8,128)(2,1)S(1)}, bf16[8,72,256]{2,1,0:T(8,128)(2,1)S(1)}, u32[]{:S(2)}, u32[]{:S(2)}) collective-permute-start(bf16[8,72,256]{2,1,0:T(8,128)(2,1)S(1)} %slice.8.own_ref.info_ref.a_ref), channel_id=1, source_target_pairs={{0,1},{1,0},{2,3},{3,2},{4,5},{5,4},{6,7},{7,6},{8,9},{9,8},{10,11... | collective-permute-start | bytes 884744 | tf_op jit(solution)/shard_map/ppermute | solution.py:372
  35.2 10.1 %collective-permute-start.1 = (bf16[8,72,256]{2,1,0:T(8,128)(2,1)S(1)}, bf16[8,72,256]{2,1,0:T(8,128)(2,1)S(1)}, u32[]{:S(2)}, u32[]{:S(2)}) collective-permute-start(bf16[8,72,256]{2,1,0:T(8,128)(2,1)S(1)} %slice.8.own_ref.info_ref.a_ref), channel_id=1, source_target_pairs={{0,16},{16,0},{1,17},{17,1},{2,18},{18,2},{3,19},{19,3},{4,20},{20... | collective-permute-start | bytes 884744 | tf_op jit(solution)/shard_map/ppermute | solution.py:372
  38.2 10.7 %collective-permute-start.3 = (bf16[8,96,256]{2,1,0:T(8,128)(2,1)S(1)}, bf16[8,96,256]{2,1,0:T(8,128)(2,1)S(1)}, u32[]{:S(2)}, u32[]{:S(2)}) collective-permute-start(bf16[8,96,256]{2,1,0:T(8,128)(2,1)S(1)} %slice.9.w0_ref), channel_id=1, source_target_pairs={{0,96},{32,0},{64,32},{96,64},{1,97},{33,1},{65,33},{97,65},{2,98}... | collective-permute-start | bytes 1179656 | tf_op jit(solution)/shard_map/ppermute | solution.py:372
  43.9 38.3 %copy-start.9 = (f32[96]{0:T(128)S(1)}, f32[96]{0:T(128)}, u32[]{:S(2)}) copy-start(f32[96]{0:T(128)} %param.28) | copy-start | bytes 1156
  43.9 38.3 %copy-start.10 = (f32[96]{0:T(128)S(1)}, f32[96]{0:T(128)}, u32[]{:S(2)}) copy-start(f32[96]{0:T(128)} %param.29) | copy-start | bytes 1156
  45.3 2.1 %collective-permute-start.2 = (bf16[8,72,256]{2,1,0:T(8,128)(2,1)S(1)}, bf16[8,72,256]{2,1,0:T(8,128)(2,1)S(1)}, u32[]{:S(2)}, u32[]{:S(2)}) collective-permute-start(bf16[8,72,256]{2,1,0:T(8,128)(2,1)S(1)} %collective-permute-done.1.own_ref.b_ref), channel_id=1, source_target_pairs={{0,1},{1,0},{2,3},{3,2},{4,5},{5,4},{6,7},{7,6},{8,9},{9,8},{10,11... | collective-permute-start | bytes 884744 | tf_op jit(solution)/shard_map/ppermute | solution.py:372
  46.1 16.9 %collective-permute-start.7 = (bf16[8,96,256]{2,1,0:T(8,128)(2,1)S(1)}, bf16[8,96,256]{2,1,0:T(8,128)(2,1)S(1)}, u32[]{:S(2)}, u32[]{:S(2)}) collective-permute-start(bf16[8,96,256]{2,1,0:T(8,128)(2,1)S(1)} %slice.9.w0_ref), channel_id=1, source_target_pairs={{0,32},{32,64},{64,96},{96,0},{1,33},{33,65},{65,97},{97,1},{2,34}... | collective-permute-start | bytes 1179656 | tf_op jit(solution)/shard_map/ppermute | solution.py:372
  48.9 15.1 %collective-permute-start.8 = (bf16[8,96,256]{2,1,0:T(8,128)(2,1)S(1)}, bf16[8,96,256]{2,1,0:T(8,128)(2,1)S(1)}, u32[]{:S(2)}, u32[]{:S(2)}) collective-permute-start(bf16[8,96,256]{2,1,0:T(8,128)(2,1)S(1)} %collective-permute-done.3.w2_ref), channel_id=1, source_target_pairs={{0,96},{32,0},{64,32},{96,64},{1,97},{33,1},{65,33},{97,65},{2,98}... | collective-permute-start | bytes 1179656 | tf_op jit(solution)/shard_map/ppermute | solution.py:372
  55.3 5.1 %collective-permute-start.4 = (bf16[216,256]{1,0:T(8,128)(2,1)S(1)}, bf16[216,256]{1,0:T(8,128)(2,1)S(1)}, u32[]{:S(2)}, u32[]{:S(2)}) collective-permute-start(bf16[216,256]{1,0:T(8,128)(2,1)S(1)} %get-tuple-element.40.a_ref), channel_id=1, source_target_pairs={{0,16},{16,0},{1,17},{17,1},{2,18},{18,2},{3,19},{19,3},{4,20},{20... | collective-permute-start | bytes 331784 | tf_op jit(solution)/shard_map/ppermute | solution.py:372
  56.4 6.7 %collective-permute-start.5 = (bf16[216,256]{1,0:T(8,128)(2,1)S(1)}, bf16[216,256]{1,0:T(8,128)(2,1)S(1)}, u32[]{:S(2)}, u32[]{:S(2)}) collective-permute-start(bf16[216,256]{1,0:T(8,128)(2,1)S(1)} %get-tuple-element.40.a_ref), channel_id=1, source_target_pairs={{0,1},{1,0},{2,3},{3,2},{4,5},{5,4},{6,7},{7,6},{8,9},{9,8},{10,11... | collective-permute-start | bytes 331784 | tf_op jit(solution)/shard_map/ppermute | solution.py:372
  60.4 3.6 %collective-permute-start.6 = (bf16[216,256]{1,0:T(8,128)(2,1)S(1)}, bf16[216,256]{1,0:T(8,128)(2,1)S(1)}, u32[]{:S(2)}, u32[]{:S(2)}) collective-permute-start(bf16[216,256]{1,0:T(8,128)(2,1)S(1)} %collective-permute-done.4.b_ref), channel_id=1, source_target_pairs={{0,1},{1,0},{2,3},{3,2},{4,5},{5,4},{6,7},{7,6},{8,9},{9,8},{10,11... | collective-permute-start | bytes 331784 | tf_op jit(solution)/shard_map/ppermute | solution.py:372
  100.8 2.8 %collective-permute-start.9 = (f32[2,224,256]{2,1,0:T(8,128)S(1)}, f32[2,224,256]{2,1,0:T(8,128)S(1)}, u32[]{:S(2)}, u32[]{:S(2)}) collective-permute-start(f32[2,224,256]{2,1,0:T(8,128)S(1)} %get-tuple-element.46), channel_id=1, source_target_pairs={{0,1},{1,0},{2,3},{3,2},{4,5},{5,4},{6,7},{7,6},{8,9},{9,8},{10,11... | collective-permute-start | bytes 1376264 | tf_op jit(solution)/shard_map/ppermute | solution.py:372
  103.6 5.9 %collective-permute-start.10 = (bf16[224,256]{1,0:T(8,128)(2,1)S(1)}, bf16[224,256]{1,0:T(8,128)(2,1)S(1)}, u32[]{:S(2)}, u32[]{:S(2)}) collective-permute-start(bf16[224,256]{1,0:T(8,128)(2,1)S(1)} %get-tuple-element.48), channel_id=1, source_target_pairs={{0,16},{16,0},{1,17},{17,1},{2,18},{18,2},{3,19},{19,3},{4,20},{20... | collective-permute-start | bytes 344072 | tf_op jit(solution)/shard_map/ppermute | solution.py:372
  109.6 33.6 %copy-start.6 = (f32[256]{0:T(256)S(1)}, f32[256]{0:T(256)}, u32[]{:S(2)}) copy-start(f32[256]{0:T(256)} %param.22) | copy-start | bytes 3076
  113.2 2.1 %collective-permute-start.11 = (f32[16,256]{1,0:T(8,128)S(1)}, f32[16,256]{1,0:T(8,128)S(1)}, u32[]{:S(2)}, u32[]{:S(2)}) collective-permute-start(f32[16,256]{1,0:T(8,128)S(1)} %get-tuple-element.51), channel_id=1, source_target_pairs={{0,1},{1,0},{2,3},{3,2},{4,5},{5,4},{6,7},{7,6},{8,9},{9,8},{10,11... | collective-permute-start | bytes 49160 | tf_op jit(solution)/shard_map/ppermute | solution.py:372
  139.7 3.4 %collective-permute-start.12 = (f32[8,256]{1,0:T(8,128)S(1)}, f32[8,256]{1,0:T(8,128)S(1)}, u32[]{:S(2)}, u32[]{:S(2)}) collective-permute-start(f32[8,256]{1,0:T(8,128)S(1)} %get-tuple-element.54.mine_ref), channel_id=1, source_target_pairs={{0,1},{1,0},{2,3},{3,2},{4,5},{5,4},{6,7},{7,6},{8,9},{9,8},{10,11... | collective-permute-start | bytes 24584 | tf_op jit(solution)/shard_map/ppermute | solution.py:372

commit v5 on v4

--- a/solution.py
+++ b/solution.py
@@ -197,13 +197,18 @@
 SHIFTS = (0, 1, 3, 2)
 
 
-def input_kernel(a_ref, b_ref, c_ref, d_ref, w0_ref, w1_ref, w2_ref, w3_ref, out_ref, held):
+def weights(w0_ref, w1_ref, w2_ref, low_ref, high_ref):
+    last = jnp.concatenate([low_ref[...], high_ref[...]], axis=0)
+    return [block.reshape(-1, LANES) for block in (w0_ref[...], w1_ref[...], w2_ref[...], last)]
+
+
+def input_kernel(a_ref, b_ref, c_ref, d_ref, w0_ref, w1_ref, w2_ref, w3_ref, w4_ref, out_ref, held):
     own, x = lax.axis_index("yhi") * 2 + lax.axis_index("core"), lax.axis_index("x")
     hold(held, (a_ref, b_ref, c_ref, d_ref), own)
     zs, feats, _ = w0_ref.shape
     acc = None
-    for by, ref in zip(SHIFTS, (w0_ref, w1_ref, w2_ref, w3_ref)):
-        part = contract(ref[...].reshape(zs * feats, LANES), held[(x + 4 - by) % 4], 1, 1)
+    for by, weight in zip(SHIFTS, weights(w0_ref, w1_ref, w2_ref, w3_ref, w4_ref)):
+        part = contract(weight, held[(x + 4 - by) % 4], 1, 1)
         acc = part if acc is None else acc + part
     out_ref[...] = acc.reshape(zs, feats, acc.shape[1]).astype(BF16)
 
@@ -229,7 +234,7 @@
 
 
 def grads_kernel(
-    g_ref, w0_ref, w1_ref, w2_ref, w3_ref, a_ref, b_ref, c_ref, d_ref, so_far_ref,
+    g_ref, w0_ref, w1_ref, w2_ref, w3_ref, w4_ref, a_ref, b_ref, c_ref, d_ref, so_far_ref,
     near_ref, far_ref, back_ref, held,
 ):
     own, x = lax.axis_index("yhi") * 2 + lax.axis_index("core"), lax.axis_index("x")
@@ -237,9 +242,9 @@
     zs, feats, rows = g_ref.shape
     grads = g_ref[...].reshape(zs * feats, rows)
     terms = None
-    for by, ref in zip(SHIFTS, (w0_ref, w1_ref, w2_ref, w3_ref)):
+    for by, weight in zip(SHIFTS, weights(w0_ref, w1_ref, w2_ref, w3_ref, w4_ref)):
         q = (x + 4 - by) % 4
-        part = contract(grads, ref[...].reshape(zs * feats, LANES), 0, 0)
+        part = contract(grads, weight, 0, 0)
         term = part * held[q].astype(F32)
         terms = term if terms is None else terms + term
         place = own ^ q
@@ -429,8 +434,6 @@
     )(label, offset, info_a, deep_bias[None])
     total, own_const, info_b = lax.optimization_barrier((total, own_const, info_b))
     info_d = shifted(info_b, "core", 2, 1)
-    info_d, w_all[2] = lax.optimization_barrier((info_d, w_all[2]))
-    w_all.append(shifted(w_all[2], "x", 4, 3))
     sent, coeffs, const = call(
         far_kernel,
         grid=(8 // depth,),
@@ -441,6 +444,8 @@
         name="forward_far",
     )(label, offset, info_b, info_d, weight, total, own_const, *layer)
 
+    sent, w_all[1], w_all[2] = lax.optimization_barrier((sent, w_all[1], w_all[2]))
+    w_all += [shifted(w_all[1][:4], "x", 4, 1), shifted(w_all[2][4:], "x", 4, 3)]
     sent_b = shifted(sent, "yhi", 2, 1)
     sent_c = shifted(sent, "core", 2, 1)
     sent_d = shifted(sent_b, "core", 2, 1)

time: 144 us -> 143 us (level)
  blocking collectives: 86.5 us -> 83.5 us
  waiting for transfers between devices: 14.1 us -> 16.2 us
    all_to_all x1, blocking collectives: 17.5 us -> 14.6 us  [on_device(): parts = lax.all_to_all(parts, 'z', 0, 0, tiled=True)]
    ppermute x13 -> x14, waiting for transfers between devices: 14.1 us -> 16.2 us  [shifted(): lax.ppermute(value, axis, [(i, (i + by) % size) for i in range(size)])]
    all_to_all x1, blocking collectives: 16.7 us -> 14.9 us  [on_device(): grads = lax.all_to_all(grads, 'z', 0, 0, tiled=True)]
    all_to_all x1, blocking collectives: 11.1 us -> 12.7 us  [on_device(): got = lax.all_to_all(to_dom, DOM + ('yhi',), 0, 0, tiled=True)]
    ppermute x13 -> x14, starting transfers between devices: 25.4 us -> 24.9 us  [shifted(): lax.ppermute(value, axis, [(i, (i + by) % size) for i in range(size)])]
  transfers between devices with their start and end apart: 13 -> 14, of which waited for: 8 -> 9; matrix products, arithmetic and copies ran while one was open for 0% -> 0% of each run, Pallas kernels for 4% -> 4%
where the time goes in v5:
time: 143 us; the launch traced here: 142 us
  blocking collectives  83.5 us (58%)
  starting transfers between devices  24.9 us (17%)
  Pallas kernels  16.9 us (12%)
  waiting for transfers between devices  16.2 us (11%)
    all_to_all x1, blocking collectives, on_device(): message = lax.all_to_all(message, 'z', 0, 0, tiled=True)  28.6 us
    ppermute x14, starting transfers between devices, shifted(): lax.ppermute(value, axis, [(i, (i + by) % size) for i in range(size)])  24.9 us
    ppermute x14, waiting for transfers between devices, shifted(): lax.ppermute(value, axis, [(i, (i + by) % size) for i in range(size)])  16.2 us
    all_to_all x1, blocking collectives, on_device(): grads = lax.all_to_all(grads, 'z', 0, 0, tiled=True)  14.9 us
    all_to_all x1, blocking collectives, on_device(): parts = lax.all_to_all(parts, 'z', 0, 0, tiled=True)  14.6 us
    all_to_all x1, blocking collectives, on_device(): got = lax.all_to_all(to_dom, DOM + ('yhi',), 0, 0, tiled=True)  12.7 us
    all_to_all x1, blocking collectives, on_device(): got = lax.all_to_all(to_z, 'z', 0, 0, tiled=True)  12.6 us
    pallas_call x1, Pallas kernels, on_device(): call(backward_kernel, grid=(8 // depth,), in_specs=label_specs + [info_sp...  3.62 us
  transfers between devices with their start and end apart: 14, of which 9 were waited for; matrix products, arithmetic and copies ran while one was open for 0% of the time, Pallas kernels for 4%

profile of v5, /device:TPU:1, one launch (start us, length us, event | category | flops | bytes accessed | tf_op | source)
XLA Modules:
  0.0 142.5 jit_solution(9243992315183995000)
XLA Ops:
  0.7 3.3 %prep.1 = bf16[8,168,256]{2,1,0:T(8,128)(2,1)} custom-call(s32[27,256]{1,0:T(8,128)} %status_ref.3, s32[27,2,256]{2,1,0:T(2,128)} %bitcast.39, bf16[10,256]{1,0:T(8,128)(2,1)} %class_ref.1, f32[1,256]{1,0:T(1,128)} %bitcast.31, bf16[96,8192]{1,0:T(8,128)(2,1)} %bitcast.38), custom_call_target="tpu_custom_call" | custom-call | tf_op jit(solution)/shard_map/prep/pallas_call | solution.py:393
  4.0 28.6 %all_to_all.25 = bf16[8,168,256]{2,1,0:T(8,128)(2,1)S(1)} all-to-all(bf16[8,168,256]{2,1,0:T(8,128)(2,1)} %prep.1), channel_id=1, replica_groups=mesh['ylo'=2,'x'=4,'yhi'=2,'z'=8,'core'=2] {'z'}, dimensions={0} | all-to-all | bytes 1376256 | tf_op jit(solution)/shard_map/all_to_all | solution.py:405
  32.6 2.6 %collective-permute-start = (bf16[8,72,256]{2,1,0:T(8,128)(2,1)S(1)}, bf16[8,72,256]{2,1,0:T(8,128)(2,1)S(1)}, u32[]{:S(2)}, u32[]{:S(2)}) collective-permute-start(bf16[8,72,256]{2,1,0:T(8,128)(2,1)S(1)} %slice.16.own_ref.info_ref.a_ref), channel_id=1, source_target_pairs={{0,1},{1,0},{2,3},{3,2},{4,5},{5,4},{6,7},{7,6},{8,9},{9,8},{10,11... | collective-permute-start | bytes 884744 | tf_op jit(solution)/shard_map/ppermute | solution.py:377
  35.2 2.9 %collective-permute-start.1 = (bf16[8,72,256]{2,1,0:T(8,128)(2,1)S(1)}, bf16[8,72,256]{2,1,0:T(8,128)(2,1)S(1)}, u32[]{:S(2)}, u32[]{:S(2)}) collective-permute-start(bf16[8,72,256]{2,1,0:T(8,128)(2,1)S(1)} %slice.16.own_ref.info_ref.a_ref), channel_id=1, source_target_pairs={{0,16},{16,0},{1,17},{17,1},{2,18},{18,2},{3,19},{19,3},{4,20},{20... | collective-permute-start | bytes 884744 | tf_op jit(solution)/shard_map/ppermute | solution.py:377
  38.2 2.6 %collective-permute-start.4 = (bf16[8,96,256]{2,1,0:T(8,128)(2,1)S(1)}, bf16[8,96,256]{2,1,0:T(8,128)(2,1)S(1)}, u32[]{:S(2)}, u32[]{:S(2)}) collective-permute-start(bf16[8,96,256]{2,1,0:T(8,128)(2,1)S(1)} %slice.17.w0_ref), channel_id=1, source_target_pairs={{0,96},{32,0},{64,32},{96,64},{1,97},{33,1},{65,33},{97,65},{2,98}... | collective-permute-start | bytes 1179656 | tf_op jit(solution)/shard_map/ppermute | solution.py:377
  41.3 2.6 %forward_near.1.so_far_ref = f32[216,256]{1,0:T(8,128)S(1)} custom-call(s32[1,216]{1,0:T(1,128)S(1)} %bitcast.21, s32[1,216]{1,0:T(1,128)S(1)} %bitcast.25, bf16[8,72,256]{2,1,0:T(8,128)(2,1)S(1)} %slice.16.own_ref.info_ref.a_ref, bf16[8,72,256]{2,1,0:T(8,128)(2,1)S(1)} %collective-permute-done.other_ref.c_ref, bf16[2,8,2,256,256]{4,3,2,1,0:T(8,128)(2,1)S(1)} %bitcast.15), custom_call_target="tpu_custom_call" | custom-call | tf_op jit(solution)/shard_map/forward_near/pallas_call | solution.py:424
  43.9 1.4 collective-permute-done.1.own_ref.b_ref
  45.3 0.9 collective-permute-start.2
  46.2 1.2 collective-permute-done.2.other_ref.d_ref
  47.4 3.0 %forward_far.1 = (bf16[216,256]{1,0:T(8,128)(2,1)S(1)}, f32[216,256]{1,0:T(8,128)S(1)}, f32[8,216]{1,0:T(8,128)S(1)}) custom-call(s32[1,216]{1,0:T(1,128)S(1)} %bitcast.22, s32[1,216]{1,0:T(1,128)S(1)} %bitcast.26, bf16[8,72,256]{2,1,0:T(8,128)(2,1)S(1)} %collective-permute-done.1.own_ref.b_ref, ...), custom_call_target="tpu_custom_call" | custom-call | tf_op jit(solution)/shard_map/forward_far/pallas_call | solution.py:437
  50.4 1.6 %collective-permute-done.3.w1_ref = bf16[8,96,256]{2,1,0:T(8,128)(2,1)S(1)} collective-permute-done((bf16[8,96,256]{2,1,0:T(8,128)(2,1)S(1)}, bf16[8,96,256]{2,1,0:T(8,128)(2,1)S(1)}, u32[]{:S(2)}, u32[]{:S(2)}) %collective-permute-start.3) | collective-permute-done | bytes 393248 | tf_op jit(solution)/shard_map/ppermute | solution.py:377
  52.0 1.4 %collective-permute-start.5 = (bf16[216,256]{1,0:T(8,128)(2,1)S(1)}, bf16[216,256]{1,0:T(8,128)(2,1)S(1)}, u32[]{:S(2)}, u32[]{:S(2)}) collective-permute-start(bf16[216,256]{1,0:T(8,128)(2,1)S(1)} %get-tuple-element.41.a_ref), channel_id=1, source_target_pairs={{0,16},{16,0},{1,17},{17,1},{2,18},{18,2},{3,19},{19,3},{4,20},{20... | collective-permute-start | bytes 331784 | tf_op jit(solution)/shard_map/ppermute | solution.py:377
  53.5 2.6 %collective-permute-start.9 = (bf16[4,96,256]{2,1,0:T(8,128)(2,1)S(1)}, bf16[4,96,256]{2,1,0:T(8,128)(2,1)S(1)}, u32[]{:S(2)}, u32[]{:S(2)}) collective-permute-start(bf16[4,96,256]{2,1,0:T(8,128)(2,1)S(1)} %slice.15), channel_id=1, source_target_pairs={{0,96},{32,0},{64,32},{96,64},{1,97},{33,1},{65,33},{97,65},{2,98}... | collective-permute-start | bytes 589832 | tf_op jit(solution)/shard_map/ppermute | solution.py:377
  56.0 1.0 collective-permute-start.6
  57.1 2.7 %collective-permute-start.7 = (bf16[216,256]{1,0:T(8,128)(2,1)S(1)}, bf16[216,256]{1,0:T(8,128)(2,1)S(1)}, u32[]{:S(2)}, u32[]{:S(2)}) collective-permute-start(bf16[216,256]{1,0:T(8,128)(2,1)S(1)} %collective-permute-done.5.b_ref), channel_id=1, source_target_pairs={{0,1},{1,0},{2,3},{3,2},{4,5},{5,4},{6,7},{7,6},{8,9},{9,8},{10,11... | collective-permute-start | bytes 331784 | tf_op jit(solution)/shard_map/ppermute | solution.py:377
  59.7 2.9 %collective-permute-done.8.w3_ref = bf16[4,96,256]{2,1,0:T(8,128)(2,1)S(1)} collective-permute-done((bf16[4,96,256]{2,1,0:T(8,128)(2,1)S(1)}, bf16[4,96,256]{2,1,0:T(8,128)(2,1)S(1)}, u32[]{:S(2)}, u32[]{:S(2)}) %collective-permute-start.8) | collective-permute-done | bytes 196640 | tf_op jit(solution)/shard_map/ppermute | solution.py:377
  62.7 0.6 inputs.1
  63.3 14.6 %all_to_all.26.parts_ref = bf16[8,96,216]{2,1,0:T(8,128)(2,1)S(1)} all-to-all(bf16[8,96,216]{2,1,0:T(8,128)(2,1)S(1)} %inputs.1), channel_id=1, replica_groups=mesh['ylo'=2,'x'=4,'yhi'=2,'z'=8,'core'=2] {'z'}, dimensions={0} | all-to-all | bytes 663552 | tf_op jit(solution)/shard_map/all_to_all | solution.py:457
  78.1 14.9 %all_to_all.27.g_ref = bf16[8,96,216]{2,1,0:T(8,128)(2,1)S(1)} all-to-all(bf16[8,96,216]{2,1,0:T(8,128)(2,1)S(1)} %get-tuple-element.45), channel_id=1, replica_groups=mesh['ylo'=2,'x'=4,'yhi'=2,'z'=8,'core'=2] {'z'}, dimensions={0} | all-to-all | bytes 663552 | tf_op jit(solution)/shard_map/all_to_all | solution.py:461
  93.0 1.8 %grads.1 = (f32[216,256]{1,0:T(8,128)S(1)}, f32[224,256]{1,0:T(8,128)S(1)}, f32[2,224,256]{2,1,0:T(8,128)S(1)}) custom-call(bf16[8,96,216]{2,1,0:T(8,128)(2,1)S(1)} %all_to_all.27.g_ref, bf16[8,96,256]{2,1,0:T(8,128)(2,1)S(1)} %slice.17.w0_ref, bf16[8,96,256]{2,1,0:T(8,128)(2,1)S(1)} %collective-permute-done.3.w1_ref, ...), custom_call_target="tpu_custom_call" | custom-call | tf_op jit(solution)/shard_map/grads/pallas_call | solution.py:462
  94.8 4.1 %collective-permute-start.10 = (f32[2,224,256]{2,1,0:T(8,128)S(1)}, f32[2,224,256]{2,1,0:T(8,128)S(1)}, u32[]{:S(2)}, u32[]{:S(2)}) collective-permute-start(f32[2,224,256]{2,1,0:T(8,128)S(1)} %get-tuple-element.48), channel_id=1, source_target_pairs={{0,1},{1,0},{2,3},{3,2},{4,5},{5,4},{6,7},{7,6},{8,9},{9,8},{10,11... | collective-permute-start | bytes 1376264 | tf_op jit(solution)/shard_map/ppermute | solution.py:377
  99.0 1.4 %collective-permute-done.10.got_ref = f32[2,224,256]{2,1,0:T(8,128)S(1)} collective-permute-done((f32[2,224,256]{2,1,0:T(8,128)S(1)}, f32[2,224,256]{2,1,0:T(8,128)S(1)}, u32[]{:S(2)}, u32[]{:S(2)}) %collective-permute-start.10) | collective-permute-done | bytes 458784 | tf_op jit(solution)/shard_map/ppermute | solution.py:377
  100.7 5.9 %collective-permute-done.11.their_ref = bf16[224,256]{1,0:T(8,128)(2,1)S(1)} collective-permute-done((bf16[224,256]{1,0:T(8,128)(2,1)S(1)}, bf16[224,256]{1,0:T(8,128)(2,1)S(1)}, u32[]{:S(2)}, u32[]{:S(2)}) %collective-permute-start.11) | collective-permute-done | bytes 114720 | tf_op jit(solution)/shard_map/ppermute | solution.py:377
  106.6 3.6 %backward.1 = (f32[24,256]{1,0:T(8,128)S(1)}, f32[16,256]{1,0:T(8,128)S(1)}) custom-call(s32[1,216]{1,0:T(1,128)S(1)} %bitcast.23, s32[1,216]{1,0:T(1,128)S(1)} %bitcast.27, bf16[8,72,256]{2,1,0:T(8,128)(2,1)S(1)} %slice.16.own_ref.info_ref.a_ref, bf16[8,72,256]{2,1,0:T(8,128)(2,1)S(1)} %collective-permute-done.1.own_ref.b_ref, ...), custom_call_target="tpu_custom_call" | custom-call | tf_op jit(solution)/shard_map/backward/pallas_call | solution.py:474
  110.2 1.3 collective-permute-start.12
  111.5 0.8 collective-permute-done.12.got_ref
  112.4 12.6 %all_to_all.28.got_ref = f32[8,24,256]{2,1,0:T(8,128)S(1)} all-to-all(f32[8,24,256]{2,1,0:T(8,128)S(1)} %send_z.1), channel_id=1, replica_groups=mesh['ylo'=2,'x'=4,'yhi'=2,'z'=8,'core'=2] {'z'}, dimensions={0} | all-to-all | bytes 393216 | tf_op jit(solution)/shard_map/all_to_all | solution.py:489
  124.9 0.6 send_dom.1
  125.5 12.7 %all_to_all.29.got_ref = f32[16,24,256]{2,1,0:T(8,128)S(1)} all-to-all(f32[16,24,256]{2,1,0:T(8,128)S(1)} %get-tuple-element.55), channel_id=1, replica_groups=mesh['ylo'=2,'x'=4,'yhi'=2,'z'=8,'core'=2] {'ylo','x','yhi'}, dimensions={0} | all-to-all | bytes 786432 | tf_op jit(solution)/shard_map/all_to_all | solution.py:493
  138.4 2.7 %collective-permute-start.13 = (f32[8,256]{1,0:T(8,128)S(1)}, f32[8,256]{1,0:T(8,128)S(1)}, u32[]{:S(2)}, u32[]{:S(2)}) collective-permute-start(f32[8,256]{1,0:T(8,128)S(1)} %get-tuple-element.56.mine_ref), channel_id=1, source_target_pairs={{0,1},{1,0},{2,3},{3,2},{4,5},{5,4},{6,7},{7,6},{8,9},{9,8},{10,11... | collective-permute-start | bytes 24584 | tf_op jit(solution)/shard_map/ppermute | solution.py:377
  141.0 0.8 collective-permute-done.13.got_ref
  141.9 0.6 finish.1
  (40 shorter events, 1.4 us)
Async XLA Ops:
  0.6 40.1 %copy-start.8 = (f32[256]{0:T(256)S(1)}, f32[256]{0:T(256)}, u32[]{:S(2)}) copy-start(f32[256]{0:T(256)} %param.19) | copy-start | bytes 3076
  0.6 40.1 %copy-start.4 = (s32[216]{0:T(256)S(1)}, s32[216]{0:T(256)}, u32[]{:S(2)}) copy-start(s32[216]{0:T(256)} %param.16) | copy-start | bytes 2596
  0.7 40.1 %copy-start.3 = (s32[216]{0:T(256)S(1)}, s32[216]{0:T(256)}, u32[]{:S(2)}) copy-start(s32[216]{0:T(256)} %param.15) | copy-start | bytes 2596
  0.7 40.6 %copy-start = (bf16[8192,256]{1,0:T(8,128)(2,1)S(1)}, bf16[8192,256]{1,0:T(8,128)(2,1)}, u32[]{:S(2)}) copy-start(bf16[8192,256]{1,0:T(8,128)(2,1)} %param.18) | copy-start | bytes 12582916
  3.9 43.4 %copy-start.1 = (s32[2,27,256]{2,0,1:T(2,128)S(1)}, s32[2,27,256]{2,0,1:T(2,128)}, u32[]{:S(2)}) copy-start(s32[2,27,256]{2,0,1:T(2,128)} %param.26) | copy-start | bytes 165892
  3.9 43.4 %copy-start.2 = (s32[27,256]{1,0:T(8,128)S(1)}, s32[27,256]{1,0:T(8,128)}, u32[]{:S(2)}) copy-start(s32[27,256]{1,0:T(8,128)} %status_ref.5) | copy-start | bytes 82948
  4.0 43.4 %copy-start.5 = (f32[256]{0:T(256)S(1)}, f32[256]{0:T(256)}, u32[]{:S(2)}) copy-start(f32[256]{0:T(256)} %param.27) | copy-start | bytes 3076
  4.0 43.4 %copy-start.7 = (f32[256]{0:T(256)S(1)}, f32[256]{0:T(256)}, u32[]{:S(2)}) copy-start(f32[256]{0:T(256)} %param.24) | copy-start | bytes 3076
  32.6 5.5 %collective-permute-start = (bf16[8,72,256]{2,1,0:T(8,128)(2,1)S(1)}, bf16[8,72,256]{2,1,0:T(8,128)(2,1)S(1)}, u32[]{:S(2)}, u32[]{:S(2)}) collective-permute-start(bf16[8,72,256]{2,1,0:T(8,128)(2,1)S(1)} %slice.16.own_ref.info_ref.a_ref), channel_id=1, source_target_pairs={{0,1},{1,0},{2,3},{3,2},{4,5},{5,4},{6,7},{7,6},{8,9},{9,8},{10,11... | collective-permute-start | bytes 884744 | tf_op jit(solution)/shard_map/ppermute | solution.py:377
  35.2 10.1 %collective-permute-start.1 = (bf16[8,72,256]{2,1,0:T(8,128)(2,1)S(1)}, bf16[8,72,256]{2,1,0:T(8,128)(2,1)S(1)}, u32[]{:S(2)}, u32[]{:S(2)}) collective-permute-start(bf16[8,72,256]{2,1,0:T(8,128)(2,1)S(1)} %slice.16.own_ref.info_ref.a_ref), channel_id=1, source_target_pairs={{0,16},{16,0},{1,17},{17,1},{2,18},{18,2},{3,19},{19,3},{4,20},{20... | collective-permute-start | bytes 884744 | tf_op jit(solution)/shard_map/ppermute | solution.py:377
  38.2 12.2 %collective-permute-start.4 = (bf16[8,96,256]{2,1,0:T(8,128)(2,1)S(1)}, bf16[8,96,256]{2,1,0:T(8,128)(2,1)S(1)}, u32[]{:S(2)}, u32[]{:S(2)}) collective-permute-start(bf16[8,96,256]{2,1,0:T(8,128)(2,1)S(1)} %slice.17.w0_ref), channel_id=1, source_target_pairs={{0,96},{32,0},{64,32},{96,64},{1,97},{33,1},{65,33},{97,65},{2,98}... | collective-permute-start | bytes 1179656 | tf_op jit(solution)/shard_map/ppermute | solution.py:377
  40.7 11.2 %collective-permute-start.3 = (bf16[8,96,256]{2,1,0:T(8,128)(2,1)S(1)}, bf16[8,96,256]{2,1,0:T(8,128)(2,1)S(1)}, u32[]{:S(2)}, u32[]{:S(2)}) collective-permute-start(bf16[8,96,256]{2,1,0:T(8,128)(2,1)S(1)} %slice.17.w0_ref), channel_id=1, source_target_pairs={{0,32},{32,64},{64,96},{96,0},{1,33},{33,65},{65,97},{97,1},{2,34}... | collective-permute-start | bytes 1179656 | tf_op jit(solution)/shard_map/ppermute | solution.py:377
  45.3 2.1 %collective-permute-start.2 = (bf16[8,72,256]{2,1,0:T(8,128)(2,1)S(1)}, bf16[8,72,256]{2,1,0:T(8,128)(2,1)S(1)}, u32[]{:S(2)}, u32[]{:S(2)}) collective-permute-start(bf16[8,72,256]{2,1,0:T(8,128)(2,1)S(1)} %collective-permute-done.1.own_ref.b_ref), channel_id=1, source_target_pairs={{0,1},{1,0},{2,3},{3,2},{4,5},{5,4},{6,7},{7,6},{8,9},{9,8},{10,11... | collective-permute-start | bytes 884744 | tf_op jit(solution)/shard_map/ppermute | solution.py:377
  47.4 30.6 %copy-start.9 = (f32[96]{0:T(128)S(1)}, f32[96]{0:T(128)}, u32[]{:S(2)}) copy-start(f32[96]{0:T(128)} %param.28) | copy-start | bytes 1156
  47.4 30.6 %copy-start.10 = (f32[96]{0:T(128)S(1)}, f32[96]{0:T(128)}, u32[]{:S(2)}) copy-start(f32[96]{0:T(128)} %param.29) | copy-start | bytes 1156
  52.0 5.1 %collective-permute-start.5 = (bf16[216,256]{1,0:T(8,128)(2,1)S(1)}, bf16[216,256]{1,0:T(8,128)(2,1)S(1)}, u32[]{:S(2)}, u32[]{:S(2)}) collective-permute-start(bf16[216,256]{1,0:T(8,128)(2,1)S(1)} %get-tuple-element.41.a_ref), channel_id=1, source_target_pairs={{0,16},{16,0},{1,17},{17,1},{2,18},{18,2},{3,19},{19,3},{4,20},{20... | collective-permute-start | bytes 331784 | tf_op jit(solution)/shard_map/ppermute | solution.py:377
  53.5 6.3 %collective-permute-start.9 = (bf16[4,96,256]{2,1,0:T(8,128)(2,1)S(1)}, bf16[4,96,256]{2,1,0:T(8,128)(2,1)S(1)}, u32[]{:S(2)}, u32[]{:S(2)}) collective-permute-start(bf16[4,96,256]{2,1,0:T(8,128)(2,1)S(1)} %slice.15), channel_id=1, source_target_pairs={{0,96},{32,0},{64,32},{96,64},{1,97},{33,1},{65,33},{97,65},{2,98}... | collective-permute-start | bytes 589832 | tf_op jit(solution)/shard_map/ppermute | solution.py:377
  56.0 6.7 %collective-permute-start.8 = (bf16[4,96,256]{2,1,0:T(8,128)(2,1)S(1)}, bf16[4,96,256]{2,1,0:T(8,128)(2,1)S(1)}, u32[]{:S(2)}, u32[]{:S(2)}) collective-permute-start(bf16[4,96,256]{2,1,0:T(8,128)(2,1)S(1)} %slice.14), channel_id=1, source_target_pairs={{0,32},{32,64},{64,96},{96,0},{1,33},{33,65},{65,97},{97,1},{2,34}... | collective-permute-start | bytes 589832 | tf_op jit(solution)/shard_map/ppermute | solution.py:377
  56.0 3.7 %collective-permute-start.6 = (bf16[216,256]{1,0:T(8,128)(2,1)S(1)}, bf16[216,256]{1,0:T(8,128)(2,1)S(1)}, u32[]{:S(2)}, u32[]{:S(2)}) collective-permute-start(bf16[216,256]{1,0:T(8,128)(2,1)S(1)} %get-tuple-element.41.a_ref), channel_id=1, source_target_pairs={{0,1},{1,0},{2,3},{3,2},{4,5},{5,4},{6,7},{7,6},{8,9},{9,8},{10,11... | collective-permute-start | bytes 331784 | tf_op jit(solution)/shard_map/ppermute | solution.py:377
  57.1 5.6 %collective-permute-start.7 = (bf16[216,256]{1,0:T(8,128)(2,1)S(1)}, bf16[216,256]{1,0:T(8,128)(2,1)S(1)}, u32[]{:S(2)}, u32[]{:S(2)}) collective-permute-start(bf16[216,256]{1,0:T(8,128)(2,1)S(1)} %collective-permute-done.5.b_ref), channel_id=1, source_target_pairs={{0,1},{1,0},{2,3},{3,2},{4,5},{5,4},{6,7},{7,6},{8,9},{9,8},{10,11... | collective-permute-start | bytes 331784 | tf_op jit(solution)/shard_map/ppermute | solution.py:377
  94.8 5.6 %collective-permute-start.10 = (f32[2,224,256]{2,1,0:T(8,128)S(1)}, f32[2,224,256]{2,1,0:T(8,128)S(1)}, u32[]{:S(2)}, u32[]{:S(2)}) collective-permute-start(f32[2,224,256]{2,1,0:T(8,128)S(1)} %get-tuple-element.48), channel_id=1, source_target_pairs={{0,1},{1,0},{2,3},{3,2},{4,5},{5,4},{6,7},{7,6},{8,9},{9,8},{10,11... | collective-permute-start | bytes 1376264 | tf_op jit(solution)/shard_map/ppermute | solution.py:377
  100.5 6.1 %collective-permute-start.11 = (bf16[224,256]{1,0:T(8,128)(2,1)S(1)}, bf16[224,256]{1,0:T(8,128)(2,1)S(1)}, u32[]{:S(2)}, u32[]{:S(2)}) collective-permute-start(bf16[224,256]{1,0:T(8,128)(2,1)S(1)} %get-tuple-element.50), channel_id=1, source_target_pairs={{0,16},{16,0},{1,17},{17,1},{2,18},{18,2},{3,19},{19,3},{4,20},{20... | collective-permute-start | bytes 344072 | tf_op jit(solution)/shard_map/ppermute | solution.py:377
  106.6 35.3 %copy-start.6 = (f32[256]{0:T(256)S(1)}, f32[256]{0:T(256)}, u32[]{:S(2)}) copy-start(f32[256]{0:T(256)} %param.22) | copy-start | bytes 3076
  110.2 2.1 %collective-permute-start.12 = (f32[16,256]{1,0:T(8,128)S(1)}, f32[16,256]{1,0:T(8,128)S(1)}, u32[]{:S(2)}, u32[]{:S(2)}) collective-permute-start(f32[16,256]{1,0:T(8,128)S(1)} %get-tuple-element.53), channel_id=1, source_target_pairs={{0,1},{1,0},{2,3},{3,2},{4,5},{5,4},{6,7},{7,6},{8,9},{9,8},{10,11... | collective-permute-start | bytes 49160 | tf_op jit(solution)/shard_map/ppermute | solution.py:377
  138.4 3.5 %collective-permute-start.13 = (f32[8,256]{1,0:T(8,128)S(1)}, f32[8,256]{1,0:T(8,128)S(1)}, u32[]{:S(2)}, u32[]{:S(2)}) collective-permute-start(f32[8,256]{1,0:T(8,128)S(1)} %get-tuple-element.56.mine_ref), channel_id=1, source_target_pairs={{0,1},{1,0},{2,3},{3,2},{4,5},{5,4},{6,7},{7,6},{8,9},{9,8},{10,11... | collective-permute-start | bytes 24584 | tf_op jit(solution)/shard_map/ppermute | solution.py:377

commit v6 on v5

--- a/solution.py
+++ b/solution.py
@@ -121,21 +121,27 @@
         copy.wait()
 
 
-def forward_half(label_ref, offset_ref, own_ref, other_ref, weight_ref, total):
+def forward_half(label_ref, offset_ref, own_ref, other_ref, weight_ref, flip, total):
     core = lax.axis_index("core")
     domains = label_ref.shape[1] // GROUP
     select = selector(label_ref[...], offset_ref[...])
-    acc = total[...]
-    for k in range(own_ref.shape[0]):
-        for ref, side in ((own_ref, core), (other_ref, 1 - core)):
-            block = ref[k]
-            _, _, ratio, slope, unsplit = decode(block, domains)
-            coeffs = contract(select, block, 0, 0)
-            at_pos = jnp.where(unsplit, jnp.broadcast_to(slope, ratio.shape), ratio)
-            factor = jnp.where(coeffs >= 0.0, spread(at_pos), spread(ratio))
-            sent = (coeffs * factor).astype(BF16)
-            acc = acc + jnp.dot(sent, weight_ref[0, k, side], preferred_element_type=F32)
-    total[...] = acc
+    half = lax.axis_index("yhi") ^ flip
+
+    def step(pair, carry):
+        acc = total[...]
+        for k in (2 * pair, 2 * pair + 1):
+            for ref, side in ((own_ref, core), (other_ref, 1 - core)):
+                block = ref[k]
+                _, _, ratio, slope, unsplit = decode(block, domains)
+                coeffs = contract(select, block, 0, 0)
+                at_pos = jnp.where(unsplit, jnp.broadcast_to(slope, ratio.shape), ratio)
+                factor = jnp.where(coeffs >= 0.0, spread(at_pos), spread(ratio))
+                sent = (coeffs * factor).astype(BF16)
+                acc = acc + jnp.dot(sent, weight_ref[half, k, side], preferred_element_type=F32)
+        total[...] = acc
+        return carry
+
+    lax.fori_loop(0, own_ref.shape[0] // 2, step, 0, unroll=True)
 
 
 def own_kernel(label_ref, offset_ref, info_ref, bias_ref, const_ref, extra_ref):
@@ -153,33 +159,23 @@
 
 
 def near_kernel(label_ref, offset_ref, own_ref, other_ref, weight_ref, total_ref):
-    @pl.when(pl.program_id(0) == 0)
-    def _():
-        total_ref[...] = jnp.zeros_like(total_ref)
-
-    forward_half(label_ref, offset_ref, own_ref, other_ref, weight_ref, total_ref)
+    total_ref[...] = jnp.zeros_like(total_ref)
+    forward_half(label_ref, offset_ref, own_ref, other_ref, weight_ref, 0, total_ref)
 
 
 def far_kernel(
     label_ref, offset_ref, own_ref, other_ref, weight_ref, so_far_ref, own_const_ref,
-    status_ref, bounds_ref, slopes_ref, bias_ref, sent_ref, coeffs_ref, const_ref, total,
+    status_ref, bounds_ref, slopes_ref, bias_ref, sent_ref, coeffs_ref, const_ref,
 ):
-    @pl.when(pl.program_id(0) == 0)
-    def _():
-        total[...] = so_far_ref[...]
-
-    forward_half(label_ref, offset_ref, own_ref, other_ref, weight_ref, total)
-
-    @pl.when(pl.program_id(0) == pl.num_programs(0) - 1)
-    def _():
-        coeffs = total[...]
-        factor, offset, _ = relax_rows(
-            coeffs, status_ref[...], bounds_ref[:, 0].astype(F32), bounds_ref[:, 1].astype(F32), slopes_ref[...]
-        )
-        sent = (coeffs * factor).astype(BF16)
-        sent_ref[...] = sent
-        coeffs_ref[...] = coeffs
-        const_ref[...] = own_const_ref[...] + row_sums(sent.astype(F32) * bias_ref[...] + coeffs * offset)
+    coeffs_ref[...] = so_far_ref[...]
+    forward_half(label_ref, offset_ref, own_ref, other_ref, weight_ref, 1, coeffs_ref)
+    coeffs = coeffs_ref[...]
+    factor, offset, _ = relax_rows(
+        coeffs, status_ref[...], bounds_ref[:, 0].astype(F32), bounds_ref[:, 1].astype(F32), slopes_ref[...]
+    )
+    sent = (coeffs * factor).astype(BF16)
+    sent_ref[...] = sent
+    const_ref[...] = own_const_ref[...] + row_sums(sent.astype(F32) * bias_ref[...] + coeffs * offset)
 
 
 def row_sums(values):
@@ -281,40 +277,40 @@
     status_ref, bounds_ref, slopes_ref, bias_ref, coeffs_ref, near_ref, got_ref, their_ref, bound_ref,
     mine_ref, other_ref, back,
 ):
-    step = pl.program_id(0)
     yhi, z, core = (lax.axis_index(n) for n in NEU)
     domains = status_ref.shape[0]
     select = selector(label_ref[...], offset_ref[...])
 
-    @pl.when(step == 0)
-    def _():
-        coeffs = coeffs_ref[...]
-        rows = coeffs.shape[0]
-        their = their_ref[...].astype(F32)
-        grads = near_ref[...] + got_ref[0, 0:rows] + their[0:rows] + bias_ref[...]
-        factor, offset, chosen = relax_rows(
-            coeffs, status_ref[...], bounds_ref[:, 0].astype(F32), bounds_ref[:, 1].astype(F32), slopes_ref[...]
-        )
-        back[...] = (grads * factor + offset).astype(BF16)
-        mine_ref[16:24] = jnp.zeros((8, LANES), F32)
-        mine_ref[16:17] = jnp.sum(grads * coeffs * chosen, axis=0, keepdims=True)
-        mine_ref[17:18] = bound_ref[0:1] + their[rows : rows + 1] + their[rows + 1 : rows + 2] + their[rows + 2 : rows + 3]
-
-    zs = a_ref.shape[0]
-    for k in range(zs):
-        for place, ref in enumerate((a_ref, b_ref, c_ref, d_ref)):
-            y = yhi if place % 2 == 0 else 1 - yhi
-            c = core if place // 2 == 0 else 1 - core
-            block = ref[k]
-            _, _, _, _, unsplit = decode(block, domains)
-            coeffs = contract(select, block, 0, 0)
-            kept = jnp.maximum(coeffs, 0.0) * spread(jnp.where(unsplit, 1.0, 0.0))
-            grads = contract(back[...], weight_ref[y, k, c], 1, 1)
-            summed = jnp.sum(grads * kept, axis=0, keepdims=True)
-            if place == 0:
-                summed = summed + jnp.where(step * zs + k == z, 1.0, 0.0) * extra_ref[...]
-            out = mine_ref if place // 2 == 0 else other_ref
-            out[pl.ds(y * 8 + step * zs + k, 1)] = summed
+    coeffs = coeffs_ref[...]
+    rows = coeffs.shape[0]
+    their = their_ref[...].astype(F32)
+    grads = near_ref[...] + got_ref[0, 0:rows] + their[0:rows] + bias_ref[...]
+    factor, offset, chosen = relax_rows(
+        coeffs, status_ref[...], bounds_ref[:, 0].astype(F32), bounds_ref[:, 1].astype(F32), slopes_ref[...]
+    )
+    back[...] = (grads * factor + offset).astype(BF16)
+    mine_ref[16:24] = jnp.zeros((8, LANES), F32)
+    mine_ref[16:17] = jnp.sum(grads * coeffs * chosen, axis=0, keepdims=True)
+    mine_ref[17:18] = bound_ref[0:1] + their[rows : rows + 1] + their[rows + 1 : rows + 2] + their[rows + 2 : rows + 3]
+
+    def step(pair, carry):
+        for k in (2 * pair, 2 * pair + 1):
+            for place, ref in enumerate((a_ref, b_ref, c_ref, d_ref)):
+                y = yhi if place % 2 == 0 else 1 - yhi
+                c = core if place // 2 == 0 else 1 - core
+                block = ref[k]
+                _, _, _, _, unsplit = decode(block, domains)
+                coeffs = contract(select, block, 0, 0)
+                kept = jnp.maximum(coeffs, 0.0) * spread(jnp.where(unsplit, 1.0, 0.0))
+                grads = contract(back[...], weight_ref[y, k, c], 1, 1)
+                summed = jnp.sum(grads * kept, axis=0, keepdims=True)
+                if place == 0:
+                    summed = summed + jnp.where(k == z, 1.0, 0.0) * extra_ref[...]
+                out = mine_ref if place // 2 == 0 else other_ref
+                out[pl.ds(y * 8 + k, 1)] = summed
+        return carry
+
+    lax.fori_loop(0, a_ref.shape[0] // 2, step, 0, unroll=True)
 
 
 def send_z_kernel(mine_ref, got_ref, out_ref):
@@ -363,10 +359,6 @@
 
     first_out[...] = advance(first_slopes_ref[...], first_ref[pl.ds(z, 1)], total[0:1])
     deep_out[...] = advance(deep_slopes_ref[...], deep_ref[pl.ds(yhi * 8 + z, 1)], total[4:5])
-
-
-def whole(shape):
-    return pl.BlockSpec(shape, lambda s: (0,) * len(shape))
 
 
 def shape(dims, kind=F32):
@@ -411,21 +403,9 @@
 
     label, offset = spec_label[None], spec_offset[None]
     weight = deep_weight.reshape(2, 8, 2, LANES, LANES)
-    depth = 2
-    info_spec = pl.BlockSpec((depth, ROWS_ALL, LANES), lambda s: (s, 0, 0))
-    label_specs = [whole((1, rows))] * 2
-    layer_specs = [whole((domains, LANES)), whole((domains, 2, LANES)), whole((1, LANES)), whole((1, LANES))]
     layer = (first_status, first_bounds.transpose(1, 0, 2), first_slopes[None], first_bias[None])
-    half_spec = lambda other: pl.BlockSpec(
-        (1, depth, 2, LANES, LANES), lambda s: (lax.axis_index("yhi") ^ other, s, 0, 0, 0)
-    )
-    square = whole((rows, LANES))
-
     total = call(
         near_kernel,
-        grid=(8 // depth,),
-        in_specs=label_specs + [info_spec] * 2 + [half_spec(0)],
-        out_specs=square,
         out_shape=shape((rows, LANES)),
         name="forward_near",
     )(label, offset, info_a, info_c, weight)
@@ -436,11 +416,7 @@
     info_d = shifted(info_b, "core", 2, 1)
     sent, coeffs, const = call(
         far_kernel,
-        grid=(8 // depth,),
-        in_specs=label_specs + [info_spec] * 2 + [half_spec(1), square, whole((8, rows))] + layer_specs,
-        out_specs=[square, square, whole((8, rows))],
         out_shape=[shape((rows, LANES), BF16), shape((rows, LANES)), shape((8, rows))],
-        scratch_shapes=[pltpu.VMEM((rows, LANES), F32)],
         name="forward_far",
     )(label, offset, info_b, info_d, weight, total, own_const, *layer)
 
@@ -473,13 +449,6 @@
 
     mine, other = call(
         backward_kernel,
-        grid=(8 // depth,),
-        in_specs=label_specs
-        + [info_spec] * 4
-        + [pl.BlockSpec((2, depth, 2, LANES, LANES), lambda s: (0, s, 0, 0, 0)), whole((1, LANES))]
-        + layer_specs
-        + [square, square, pl.BlockSpec((1, rows + 8, LANES), lambda s: (0, 0, 0)), whole((rows + 8, LANES)), whole((8, LANES))],
-        out_specs=[whole((24, LANES)), whole((16, LANES))],
         out_shape=[shape((24, LANES)), shape((16, LANES))],
         scratch_shapes=[pltpu.VMEM((rows, LANES), BF16)],
         name="backward",

time: 143 us -> 139 us (0.972)
  Pallas kernels: 16.9 us -> 14 us
  blocking collectives: 83.5 us -> 81.7 us
    pallas_call x3, Pallas kernels: 9.18 us -> 6.1 us  [the longest x1 2.58 us: on_device(): call(backward_kernel, out_shape=[shape((24, LANES)), shape((16, LANES))],...]
    all_to_all x1, blocking collectives: 12.7 us -> 11 us  [on_device(): got = lax.all_to_all(to_dom, DOM + ('yhi',), 0, 0, tiled=True)]
  transfers between devices with their start and end apart: 14 -> 14, of which waited for: 9 -> 9; matrix products, arithmetic and copies ran while one was open for 0% -> 0% of each run, Pallas kernels for 4% -> 3%
where the time goes in v6:
time: 139 us
  blocking collectives  81.7 us (59%)
  starting transfers between devices  24.8 us (18%)
  waiting for transfers between devices  17.4 us (13%)
  Pallas kernels  14 us (10%)
    all_to_all x1, blocking collectives, on_device(): message = lax.all_to_all(message, 'z', 0, 0, tiled=True)  28.6 us
    ppermute x14, starting transfers between devices, shifted(): lax.ppermute(value, axis, [(i, (i + by) % size) for i in range(size)])  24.8 us
    ppermute x14, waiting for transfers between devices, shifted(): lax.ppermute(value, axis, [(i, (i + by) % size) for i in range(size)])  17.4 us
    all_to_all x1, blocking collectives, on_device(): grads = lax.all_to_all(grads, 'z', 0, 0, tiled=True)  14.9 us
    all_to_all x1, blocking collectives, on_device(): parts = lax.all_to_all(parts, 'z', 0, 0, tiled=True)  14.7 us
    all_to_all x1, blocking collectives, on_device(): got = lax.all_to_all(to_z, 'z', 0, 0, tiled=True)  12.6 us
    all_to_all x1, blocking collectives, on_device(): got = lax.all_to_all(to_dom, DOM + ('yhi',), 0, 0, tiled=True)  11 us
    pallas_call x1, Pallas kernels, on_device(): pl.pallas_call(prep_kernel, compiler_params=pltpu.CompilerParams(vmem_lim...  3.25 us
  transfers between devices with their start and end apart: 14, of which 9 were waited for; matrix products, arithmetic and copies ran while one was open for 0% of the time, Pallas kernels for 3%

profile of v6, /device:TPU:1, one launch (start us, length us, event | category | flops | bytes accessed | tf_op | source)
XLA Modules:
  0.0 138.8 jit_solution(4171430826380880684)
XLA Ops:
  0.7 3.3 %prep.1 = bf16[8,168,256]{2,1,0:T(8,128)(2,1)} custom-call(s32[27,256]{1,0:T(8,128)} %status_ref.3, s32[27,2,256]{2,1,0:T(2,128)} %bitcast.39, bf16[10,256]{1,0:T(8,128)(2,1)} %class_ref.1, f32[1,256]{1,0:T(1,128)} %bitcast.31, bf16[96,8192]{1,0:T(8,128)(2,1)} %bitcast.38), custom_call_target="tpu_custom_call" | custom-call | tf_op jit(solution)/shard_map/prep/pallas_call | solution.py:385
  4.0 28.6 %all_to_all.25 = bf16[8,168,256]{2,1,0:T(8,128)(2,1)S(1)} all-to-all(bf16[8,168,256]{2,1,0:T(8,128)(2,1)} %prep.1), channel_id=1, replica_groups=mesh['ylo'=2,'x'=4,'yhi'=2,'z'=8,'core'=2] {'z'}, dimensions={0} | all-to-all | bytes 1376256 | tf_op jit(solution)/shard_map/all_to_all | solution.py:397
  32.6 2.6 %collective-permute-start = (bf16[8,72,256]{2,1,0:T(8,128)(2,1)S(1)}, bf16[8,72,256]{2,1,0:T(8,128)(2,1)S(1)}, u32[]{:S(2)}, u32[]{:S(2)}) collective-permute-start(bf16[8,72,256]{2,1,0:T(8,128)(2,1)S(1)} %slice.16.own_ref.info_ref.a_ref), channel_id=1, source_target_pairs={{0,1},{1,0},{2,3},{3,2},{4,5},{5,4},{6,7},{7,6},{8,9},{9,8},{10,11... | collective-permute-start | bytes 884744 | tf_op jit(solution)/shard_map/ppermute | solution.py:369
  35.2 2.9 %collective-permute-start.1 = (bf16[8,72,256]{2,1,0:T(8,128)(2,1)S(1)}, bf16[8,72,256]{2,1,0:T(8,128)(2,1)S(1)}, u32[]{:S(2)}, u32[]{:S(2)}) collective-permute-start(bf16[8,72,256]{2,1,0:T(8,128)(2,1)S(1)} %slice.16.own_ref.info_ref.a_ref), channel_id=1, source_target_pairs={{0,16},{16,0},{1,17},{17,1},{2,18},{18,2},{3,19},{19,3},{4,20},{20... | collective-permute-start | bytes 884744 | tf_op jit(solution)/shard_map/ppermute | solution.py:369
  38.2 2.6 %collective-permute-start.4 = (bf16[8,96,256]{2,1,0:T(8,128)(2,1)S(1)}, bf16[8,96,256]{2,1,0:T(8,128)(2,1)S(1)}, u32[]{:S(2)}, u32[]{:S(2)}) collective-permute-start(bf16[8,96,256]{2,1,0:T(8,128)(2,1)S(1)} %slice.17.w0_ref), channel_id=1, source_target_pairs={{0,96},{32,0},{64,32},{96,64},{1,97},{33,1},{65,33},{97,65},{2,98}... | collective-permute-start | bytes 1179656 | tf_op jit(solution)/shard_map/ppermute | solution.py:369
  41.3 1.5 %forward_near.1.so_far_ref = f32[216,256]{1,0:T(8,128)S(1)} custom-call(s32[1,216]{1,0:T(1,128)S(1)} %bitcast.21, s32[1,216]{1,0:T(1,128)S(1)} %bitcast.25, bf16[8,72,256]{2,1,0:T(8,128)(2,1)S(1)} %slice.16.own_ref.info_ref.a_ref, bf16[8,72,256]{2,1,0:T(8,128)(2,1)S(1)} %collective-permute-done.other_ref.c_ref, bf16[2,8,2,256,256]{4,3,2,1,0:T(8,128)(2,1)S(1)} %bitcast.15), custom_call_target="tpu_custom_call" | custom-call | tf_op jit(solution)/shard_map/forward_near/pallas_call | solution.py:407
  42.7 2.5 %collective-permute-done.1.own_ref.b_ref = bf16[8,72,256]{2,1,0:T(8,128)(2,1)S(1)} collective-permute-done((bf16[8,72,256]{2,1,0:T(8,128)(2,1)S(1)}, bf16[8,72,256]{2,1,0:T(8,128)(2,1)S(1)}, u32[]{:S(2)}, u32[]{:S(2)}) %collective-permute-start.1) | collective-permute-done | bytes 294944 | tf_op jit(solution)/shard_map/ppermute | solution.py:369
  45.3 0.9 collective-permute-start.2
  46.2 1.2 collective-permute-done.2.other_ref.d_ref
  47.4 2.1 %forward_far.1 = (bf16[216,256]{1,0:T(8,128)(2,1)S(1)}, f32[216,256]{1,0:T(8,128)S(1)}, f32[8,216]{1,0:T(8,128)S(1)}) custom-call(s32[1,216]{1,0:T(1,128)S(1)} %bitcast.22, s32[1,216]{1,0:T(1,128)S(1)} %bitcast.26, bf16[8,72,256]{2,1,0:T(8,128)(2,1)S(1)} %collective-permute-done.1.own_ref.b_ref, ...), custom_call_target="tpu_custom_call" | custom-call | tf_op jit(solution)/shard_map/forward_far/pallas_call | solution.py:417
  49.5 2.5 %collective-permute-done.3.w1_ref = bf16[8,96,256]{2,1,0:T(8,128)(2,1)S(1)} collective-permute-done((bf16[8,96,256]{2,1,0:T(8,128)(2,1)S(1)}, bf16[8,96,256]{2,1,0:T(8,128)(2,1)S(1)}, u32[]{:S(2)}, u32[]{:S(2)}) %collective-permute-start.3) | collective-permute-done | bytes 393248 | tf_op jit(solution)/shard_map/ppermute | solution.py:369
  52.0 1.1 collective-permute-start.5
  53.1 2.0 %collective-permute-start.9 = (bf16[4,96,256]{2,1,0:T(8,128)(2,1)S(1)}, bf16[4,96,256]{2,1,0:T(8,128)(2,1)S(1)}, u32[]{:S(2)}, u32[]{:S(2)}) collective-permute-start(bf16[4,96,256]{2,1,0:T(8,128)(2,1)S(1)} %slice.15), channel_id=1, source_target_pairs={{0,96},{32,0},{64,32},{96,64},{1,97},{33,1},{65,33},{97,65},{2,98}... | collective-permute-start | bytes 589832 | tf_op jit(solution)/shard_map/ppermute | solution.py:369
  55.1 1.9 %collective-permute-start.6 = (bf16[216,256]{1,0:T(8,128)(2,1)S(1)}, bf16[216,256]{1,0:T(8,128)(2,1)S(1)}, u32[]{:S(2)}, u32[]{:S(2)}) collective-permute-start(bf16[216,256]{1,0:T(8,128)(2,1)S(1)} %get-tuple-element.41.a_ref), channel_id=1, source_target_pairs={{0,1},{1,0},{2,3},{3,2},{4,5},{5,4},{6,7},{7,6},{8,9},{9,8},{10,11... | collective-permute-start | bytes 331784 | tf_op jit(solution)/shard_map/ppermute | solution.py:369
  57.1 2.7 %collective-permute-start.7 = (bf16[216,256]{1,0:T(8,128)(2,1)S(1)}, bf16[216,256]{1,0:T(8,128)(2,1)S(1)}, u32[]{:S(2)}, u32[]{:S(2)}) collective-permute-start(bf16[216,256]{1,0:T(8,128)(2,1)S(1)} %collective-permute-done.5.b_ref), channel_id=1, source_target_pairs={{0,1},{1,0},{2,3},{3,2},{4,5},{5,4},{6,7},{7,6},{8,9},{9,8},{10,11... | collective-permute-start | bytes 331784 | tf_op jit(solution)/shard_map/ppermute | solution.py:369
  59.7 2.0 %collective-permute-done.8.w3_ref = bf16[4,96,256]{2,1,0:T(8,128)(2,1)S(1)} collective-permute-done((bf16[4,96,256]{2,1,0:T(8,128)(2,1)S(1)}, bf16[4,96,256]{2,1,0:T(8,128)(2,1)S(1)}, u32[]{:S(2)}, u32[]{:S(2)}) %collective-permute-start.8) | collective-permute-done | bytes 196640 | tf_op jit(solution)/shard_map/ppermute | solution.py:369
  61.8 0.6 inputs.1
  62.4 14.7 %all_to_all.26.parts_ref = bf16[8,96,216]{2,1,0:T(8,128)(2,1)S(1)} all-to-all(bf16[8,96,216]{2,1,0:T(8,128)(2,1)S(1)} %inputs.1), channel_id=1, replica_groups=mesh['ylo'=2,'x'=4,'yhi'=2,'z'=8,'core'=2] {'z'}, dimensions={0} | all-to-all | bytes 663552 | tf_op jit(solution)/shard_map/all_to_all | solution.py:433
  77.2 14.9 %all_to_all.27.g_ref = bf16[8,96,216]{2,1,0:T(8,128)(2,1)S(1)} all-to-all(bf16[8,96,216]{2,1,0:T(8,128)(2,1)S(1)} %get-tuple-element.45), channel_id=1, replica_groups=mesh['ylo'=2,'x'=4,'yhi'=2,'z'=8,'core'=2] {'z'}, dimensions={0} | all-to-all | bytes 663552 | tf_op jit(solution)/shard_map/all_to_all | solution.py:437
  92.1 2.0 %grads.1 = (f32[216,256]{1,0:T(8,128)S(1)}, f32[224,256]{1,0:T(8,128)S(1)}, f32[2,224,256]{2,1,0:T(8,128)S(1)}) custom-call(bf16[8,96,216]{2,1,0:T(8,128)(2,1)S(1)} %all_to_all.27.g_ref, bf16[8,96,256]{2,1,0:T(8,128)(2,1)S(1)} %slice.17.w0_ref, bf16[8,96,256]{2,1,0:T(8,128)(2,1)S(1)} %collective-permute-done.3.w1_ref, ...), custom_call_target="tpu_custom_call" | custom-call | tf_op jit(solution)/shard_map/grads/pallas_call | solution.py:438
  94.1 4.1 %collective-permute-start.10 = (f32[2,224,256]{2,1,0:T(8,128)S(1)}, f32[2,224,256]{2,1,0:T(8,128)S(1)}, u32[]{:S(2)}, u32[]{:S(2)}) collective-permute-start(f32[2,224,256]{2,1,0:T(8,128)S(1)} %get-tuple-element.48), channel_id=1, source_target_pairs={{0,1},{1,0},{2,3},{3,2},{4,5},{5,4},{6,7},{7,6},{8,9},{9,8},{10,11... | collective-permute-start | bytes 1376264 | tf_op jit(solution)/shard_map/ppermute | solution.py:369
  98.2 1.4 %collective-permute-done.10.got_ref = f32[2,224,256]{2,1,0:T(8,128)S(1)} collective-permute-done((f32[2,224,256]{2,1,0:T(8,128)S(1)}, f32[2,224,256]{2,1,0:T(8,128)S(1)}, u32[]{:S(2)}, u32[]{:S(2)}) %collective-permute-start.10) | collective-permute-done | bytes 458784 | tf_op jit(solution)/shard_map/ppermute | solution.py:369
  99.8 5.9 %collective-permute-done.11.their_ref = bf16[224,256]{1,0:T(8,128)(2,1)S(1)} collective-permute-done((bf16[224,256]{1,0:T(8,128)(2,1)S(1)}, bf16[224,256]{1,0:T(8,128)(2,1)S(1)}, u32[]{:S(2)}, u32[]{:S(2)}) %collective-permute-start.11) | collective-permute-done | bytes 114720 | tf_op jit(solution)/shard_map/ppermute | solution.py:369
  105.7 2.6 %backward.1 = (f32[24,256]{1,0:T(8,128)S(1)}, f32[16,256]{1,0:T(8,128)S(1)}) custom-call(s32[1,216]{1,0:T(1,128)S(1)} %bitcast.23, s32[1,216]{1,0:T(1,128)S(1)} %bitcast.27, bf16[8,72,256]{2,1,0:T(8,128)(2,1)S(1)} %slice.16.own_ref.info_ref.a_ref, bf16[8,72,256]{2,1,0:T(8,128)(2,1)S(1)} %collective-permute-done.1.own_ref.b_ref, ...), custom_call_target="tpu_custom_call" | custom-call | tf_op jit(solution)/shard_map/backward/pallas_call | solution.py:450
  108.3 1.3 collective-permute-start.12
  109.6 0.8 collective-permute-done.12.got_ref
  110.4 12.6 %all_to_all.28.got_ref = f32[8,24,256]{2,1,0:T(8,128)S(1)} all-to-all(f32[8,24,256]{2,1,0:T(8,128)S(1)} %send_z.1), channel_id=1, replica_groups=mesh['ylo'=2,'x'=4,'yhi'=2,'z'=8,'core'=2] {'z'}, dimensions={0} | all-to-all | bytes 393216 | tf_op jit(solution)/shard_map/all_to_all | solution.py:458
  123.0 0.6 send_dom.1
  123.6 11.0 %all_to_all.29.got_ref = f32[16,24,256]{2,1,0:T(8,128)S(1)} all-to-all(f32[16,24,256]{2,1,0:T(8,128)S(1)} %get-tuple-element.55), channel_id=1, replica_groups=mesh['ylo'=2,'x'=4,'yhi'=2,'z'=8,'core'=2] {'ylo','x','yhi'}, dimensions={0} | all-to-all | bytes 786432 | tf_op jit(solution)/shard_map/all_to_all | solution.py:462
  134.7 2.7 %collective-permute-start.13 = (f32[8,256]{1,0:T(8,128)S(1)}, f32[8,256]{1,0:T(8,128)S(1)}, u32[]{:S(2)}, u32[]{:S(2)}) collective-permute-start(f32[8,256]{1,0:T(8,128)S(1)} %get-tuple-element.56.mine_ref), channel_id=1, source_target_pairs={{0,1},{1,0},{2,3},{3,2},{4,5},{5,4},{6,7},{7,6},{8,9},{9,8},{10,11... | collective-permute-start | bytes 24584 | tf_op jit(solution)/shard_map/ppermute | solution.py:369
  137.4 0.8 collective-permute-done.13.got_ref
  138.2 0.6 finish.1
  (40 shorter events, 1.2 us)
Async XLA Ops:
  0.6 40.1 %copy-start.8 = (f32[256]{0:T(256)S(1)}, f32[256]{0:T(256)}, u32[]{:S(2)}) copy-start(f32[256]{0:T(256)} %param.19) | copy-start | bytes 3076
  0.6 40.1 %copy-start.4 = (s32[216]{0:T(256)S(1)}, s32[216]{0:T(256)}, u32[]{:S(2)}) copy-start(s32[216]{0:T(256)} %param.16) | copy-start | bytes 2596
  0.7 40.1 %copy-start.3 = (s32[216]{0:T(256)S(1)}, s32[216]{0:T(256)}, u32[]{:S(2)}) copy-start(s32[216]{0:T(256)} %param.15) | copy-start | bytes 2596
  0.7 40.6 %copy-start = (bf16[8192,256]{1,0:T(8,128)(2,1)S(1)}, bf16[8192,256]{1,0:T(8,128)(2,1)}, u32[]{:S(2)}) copy-start(bf16[8192,256]{1,0:T(8,128)(2,1)} %param.18) | copy-start | bytes 12582916
  3.9 43.4 %copy-start.1 = (s32[2,27,256]{2,0,1:T(2,128)S(1)}, s32[2,27,256]{2,0,1:T(2,128)}, u32[]{:S(2)}) copy-start(s32[2,27,256]{2,0,1:T(2,128)} %param.26) | copy-start | bytes 165892
  3.9 43.4 %copy-start.2 = (s32[27,256]{1,0:T(8,128)S(1)}, s32[27,256]{1,0:T(8,128)}, u32[]{:S(2)}) copy-start(s32[27,256]{1,0:T(8,128)} %status_ref.5) | copy-start | bytes 82948
  4.0 43.4 %copy-start.5 = (f32[256]{0:T(256)S(1)}, f32[256]{0:T(256)}, u32[]{:S(2)}) copy-start(f32[256]{0:T(256)} %param.27) | copy-start | bytes 3076
  4.0 43.4 %copy-start.7 = (f32[256]{0:T(256)S(1)}, f32[256]{0:T(256)}, u32[]{:S(2)}) copy-start(f32[256]{0:T(256)} %param.24) | copy-start | bytes 3076
  32.6 5.5 %collective-permute-start = (bf16[8,72,256]{2,1,0:T(8,128)(2,1)S(1)}, bf16[8,72,256]{2,1,0:T(8,128)(2,1)S(1)}, u32[]{:S(2)}, u32[]{:S(2)}) collective-permute-start(bf16[8,72,256]{2,1,0:T(8,128)(2,1)S(1)} %slice.16.own_ref.info_ref.a_ref), channel_id=1, source_target_pairs={{0,1},{1,0},{2,3},{3,2},{4,5},{5,4},{6,7},{7,6},{8,9},{9,8},{10,11... | collective-permute-start | bytes 884744 | tf_op jit(solution)/shard_map/ppermute | solution.py:369
  35.2 10.1 %collective-permute-start.1 = (bf16[8,72,256]{2,1,0:T(8,128)(2,1)S(1)}, bf16[8,72,256]{2,1,0:T(8,128)(2,1)S(1)}, u32[]{:S(2)}, u32[]{:S(2)}) collective-permute-start(bf16[8,72,256]{2,1,0:T(8,128)(2,1)S(1)} %slice.16.own_ref.info_ref.a_ref), channel_id=1, source_target_pairs={{0,16},{16,0},{1,17},{17,1},{2,18},{18,2},{3,19},{19,3},{4,20},{20... | collective-permute-start | bytes 884744 | tf_op jit(solution)/shard_map/ppermute | solution.py:369
  38.2 11.3 %collective-permute-start.4 = (bf16[8,96,256]{2,1,0:T(8,128)(2,1)S(1)}, bf16[8,96,256]{2,1,0:T(8,128)(2,1)S(1)}, u32[]{:S(2)}, u32[]{:S(2)}) collective-permute-start(bf16[8,96,256]{2,1,0:T(8,128)(2,1)S(1)} %slice.17.w0_ref), channel_id=1, source_target_pairs={{0,96},{32,0},{64,32},{96,64},{1,97},{33,1},{65,33},{97,65},{2,98}... | collective-permute-start | bytes 1179656 | tf_op jit(solution)/shard_map/ppermute | solution.py:369
  40.7 11.2 %collective-permute-start.3 = (bf16[8,96,256]{2,1,0:T(8,128)(2,1)S(1)}, bf16[8,96,256]{2,1,0:T(8,128)(2,1)S(1)}, u32[]{:S(2)}, u32[]{:S(2)}) collective-permute-start(bf16[8,96,256]{2,1,0:T(8,128)(2,1)S(1)} %slice.17.w0_ref), channel_id=1, source_target_pairs={{0,32},{32,64},{64,96},{96,0},{1,33},{33,65},{65,97},{97,1},{2,34}... | collective-permute-start | bytes 1179656 | tf_op jit(solution)/shard_map/ppermute | solution.py:369
  45.3 2.1 %collective-permute-start.2 = (bf16[8,72,256]{2,1,0:T(8,128)(2,1)S(1)}, bf16[8,72,256]{2,1,0:T(8,128)(2,1)S(1)}, u32[]{:S(2)}, u32[]{:S(2)}) collective-permute-start(bf16[8,72,256]{2,1,0:T(8,128)(2,1)S(1)} %collective-permute-done.1.own_ref.b_ref), channel_id=1, source_target_pairs={{0,1},{1,0},{2,3},{3,2},{4,5},{5,4},{6,7},{7,6},{8,9},{9,8},{10,11... | collective-permute-start | bytes 884744 | tf_op jit(solution)/shard_map/ppermute | solution.py:369
  47.4 29.7 %copy-start.9 = (f32[96]{0:T(128)S(1)}, f32[96]{0:T(128)}, u32[]{:S(2)}) copy-start(f32[96]{0:T(128)} %param.28) | copy-start | bytes 1156
  47.4 29.7 %copy-start.10 = (f32[96]{0:T(128)S(1)}, f32[96]{0:T(128)}, u32[]{:S(2)}) copy-start(f32[96]{0:T(128)} %param.29) | copy-start | bytes 1156
  52.0 5.1 %collective-permute-start.5 = (bf16[216,256]{1,0:T(8,128)(2,1)S(1)}, bf16[216,256]{1,0:T(8,128)(2,1)S(1)}, u32[]{:S(2)}, u32[]{:S(2)}) collective-permute-start(bf16[216,256]{1,0:T(8,128)(2,1)S(1)} %get-tuple-element.41.a_ref), channel_id=1, source_target_pairs={{0,16},{16,0},{1,17},{17,1},{2,18},{18,2},{3,19},{19,3},{4,20},{20... | collective-permute-start | bytes 331784 | tf_op jit(solution)/shard_map/ppermute | solution.py:369
  53.1 6.7 %collective-permute-start.9 = (bf16[4,96,256]{2,1,0:T(8,128)(2,1)S(1)}, bf16[4,96,256]{2,1,0:T(8,128)(2,1)S(1)}, u32[]{:S(2)}, u32[]{:S(2)}) collective-permute-start(bf16[4,96,256]{2,1,0:T(8,128)(2,1)S(1)} %slice.15), channel_id=1, source_target_pairs={{0,96},{32,0},{64,32},{96,64},{1,97},{33,1},{65,33},{97,65},{2,98}... | collective-permute-start | bytes 589832 | tf_op jit(solution)/shard_map/ppermute | solution.py:369
  55.1 6.7 %collective-permute-start.8 = (bf16[4,96,256]{2,1,0:T(8,128)(2,1)S(1)}, bf16[4,96,256]{2,1,0:T(8,128)(2,1)S(1)}, u32[]{:S(2)}, u32[]{:S(2)}) collective-permute-start(bf16[4,96,256]{2,1,0:T(8,128)(2,1)S(1)} %slice.14), channel_id=1, source_target_pairs={{0,32},{32,64},{64,96},{96,0},{1,33},{33,65},{65,97},{97,1},{2,34}... | collective-permute-start | bytes 589832 | tf_op jit(solution)/shard_map/ppermute | solution.py:369
  55.1 4.6 %collective-permute-start.6 = (bf16[216,256]{1,0:T(8,128)(2,1)S(1)}, bf16[216,256]{1,0:T(8,128)(2,1)S(1)}, u32[]{:S(2)}, u32[]{:S(2)}) collective-permute-start(bf16[216,256]{1,0:T(8,128)(2,1)S(1)} %get-tuple-element.41.a_ref), channel_id=1, source_target_pairs={{0,1},{1,0},{2,3},{3,2},{4,5},{5,4},{6,7},{7,6},{8,9},{9,8},{10,11... | collective-permute-start | bytes 331784 | tf_op jit(solution)/shard_map/ppermute | solution.py:369
  57.1 4.7 %collective-permute-start.7 = (bf16[216,256]{1,0:T(8,128)(2,1)S(1)}, bf16[216,256]{1,0:T(8,128)(2,1)S(1)}, u32[]{:S(2)}, u32[]{:S(2)}) collective-permute-start(bf16[216,256]{1,0:T(8,128)(2,1)S(1)} %collective-permute-done.5.b_ref), channel_id=1, source_target_pairs={{0,1},{1,0},{2,3},{3,2},{4,5},{5,4},{6,7},{7,6},{8,9},{9,8},{10,11... | collective-permute-start | bytes 331784 | tf_op jit(solution)/shard_map/ppermute | solution.py:369
  94.1 5.6 %collective-permute-start.10 = (f32[2,224,256]{2,1,0:T(8,128)S(1)}, f32[2,224,256]{2,1,0:T(8,128)S(1)}, u32[]{:S(2)}, u32[]{:S(2)}) collective-permute-start(f32[2,224,256]{2,1,0:T(8,128)S(1)} %get-tuple-element.48), channel_id=1, source_target_pairs={{0,1},{1,0},{2,3},{3,2},{4,5},{5,4},{6,7},{7,6},{8,9},{9,8},{10,11... | collective-permute-start | bytes 1376264 | tf_op jit(solution)/shard_map/ppermute | solution.py:369
  99.7 5.9 %collective-permute-start.11 = (bf16[224,256]{1,0:T(8,128)(2,1)S(1)}, bf16[224,256]{1,0:T(8,128)(2,1)S(1)}, u32[]{:S(2)}, u32[]{:S(2)}) collective-permute-start(bf16[224,256]{1,0:T(8,128)(2,1)S(1)} %get-tuple-element.50), channel_id=1, source_target_pairs={{0,16},{16,0},{1,17},{17,1},{2,18},{18,2},{3,19},{19,3},{4,20},{20... | collective-permute-start | bytes 344072 | tf_op jit(solution)/shard_map/ppermute | solution.py:369
  105.7 32.6 %copy-start.6 = (f32[256]{0:T(256)S(1)}, f32[256]{0:T(256)}, u32[]{:S(2)}) copy-start(f32[256]{0:T(256)} %param.22) | copy-start | bytes 3076
  108.3 2.1 %collective-permute-start.12 = (f32[16,256]{1,0:T(8,128)S(1)}, f32[16,256]{1,0:T(8,128)S(1)}, u32[]{:S(2)}, u32[]{:S(2)}) collective-permute-start(f32[16,256]{1,0:T(8,128)S(1)} %get-tuple-element.53), channel_id=1, source_target_pairs={{0,1},{1,0},{2,3},{3,2},{4,5},{5,4},{6,7},{7,6},{8,9},{9,8},{10,11... | collective-permute-start | bytes 49160 | tf_op jit(solution)/shard_map/ppermute | solution.py:369
  134.7 3.5 %collective-permute-start.13 = (f32[8,256]{1,0:T(8,128)S(1)}, f32[8,256]{1,0:T(8,128)S(1)}, u32[]{:S(2)}, u32[]{:S(2)}) collective-permute-start(f32[8,256]{1,0:T(8,128)S(1)} %get-tuple-element.56.mine_ref), channel_id=1, source_target_pairs={{0,1},{1,0},{2,3},{3,2},{4,5},{5,4},{6,7},{7,6},{8,9},{9,8},{10,11... | collective-permute-start | bytes 24584 | tf_op jit(solution)/shard_map/ppermute | solution.py:369
